TPU v7x, 32 devices: a whole 2x2x4 slice. The times are simulated.
32 devices in a mesh: corpus: 8 (over z, x), rep: 4 (over y, core).
Axes of the slice: x: 2, y: 2, z: 4, core: 2. Of those that a mesh axis runs over, the one named last changes fastest.
Arguments:
- queries: bfloat16 [4096, 768], P(('corpus', 'rep')), may hold values from -18 to 18
- teacher: float32 [4096, 64], P(('corpus', 'rep')), may hold values from -15 to 305
- slab: bfloat16 [8192, 768], P('corpus'), may hold values from -12 to 12
- candidates: int32 [4096, 64], P(('corpus', 'rep')), may hold values from 0 to 8191, as said below
- hot_ids: int32 [256], replicated, may hold values from 0 to 8191, as said below
- location: int32 [8192], replicated, may hold values from 0 to 8191, as said below
Outputs:
- loss: float32 [4096], P(('corpus', 'rep'))
- query_grad: float32 [4096, 768], P(('corpus', 'rep'))
- slab_grad: float32 [8192, 768], P(('corpus', 'rep'))
Inputs may be any that keep to these rules, and one draw needn't show every extreme that they name: `candidates`: every query names 64 passage ids, exactly 8 of them absent from hot_ids; ids may repeat. With the owner of id p being location[p] // 1024, the ids absent from hot_ids among one device's 128 queries (aligned blocks of 128 rows) fall at most 192 times on any owner; in each block some owner gets exactly 192, the same owner for all blocks whose block number has the same remainder modulo the number of rep devices. `hot_ids`: 256 distinct ids; entries 32 * c to 32 * c + 31 are owned by corpus index c. `location`: A permutation of the passage ids onto slab rows.
All inputs are finite; a program needn't handle non-finite values.
Results may differ from a plain program's by a relative error of at most 0.0026.
Values may be sent and summed in bfloat16 or wider, within the bound.
A program may use at most 128 MiB of HBM per device.

v0:
```python
import math

import jax
import jax.numpy as jnp
from jax import lax
from jax.sharding import PartitionSpec as P

COLD = 8
LANES = 128


def lookup(table, ids):
    rows = table.shape[0] // LANES
    grid = table.reshape(rows, LANES)
    halves = jnp.concatenate([grid // 256, grid % 256], axis=1).astype(jnp.bfloat16)
    pick_row = (ids[:, None] // LANES == jnp.arange(rows, dtype=jnp.int32)[None, :]).astype(
        jnp.bfloat16
    )
    got = jnp.dot(pick_row, halves, preferred_element_type=jnp.float32)
    value = got[:, :LANES] * 256.0 + got[:, LANES:]
    lane = ids[:, None] % LANES == jnp.arange(LANES, dtype=jnp.int32)[None, :]
    return jnp.sum(jnp.where(lane, value, 0.0), axis=1).astype(jnp.int32)


def prepare(teacher, candidates, hot_ids, location):
    q_rows, cand_count = candidates.shape
    teach_top = jnp.max(teacher, axis=1, keepdims=True)
    shifted = teacher - teach_top
    log_target = shifted - jnp.log(jnp.sum(jnp.exp(shifted), axis=1, keepdims=True))
    target = jnp.exp(log_target)
    entropy = jnp.sum(target * log_target, axis=1)
    match = candidates[:, :, None] == hot_ids[None, None, :]
    count = jnp.sum(match.astype(jnp.float32), axis=1)
    target_sum = jnp.sum(jnp.where(match, target[:, :, None], 0.0), axis=1)
    cold = jnp.logical_not(jnp.any(match, axis=2))
    iota = jnp.arange(cand_count, dtype=jnp.int32)
    upto = (iota[:, None] <= iota[None, :]).astype(jnp.bfloat16)
    rank = jnp.dot(cold.astype(jnp.bfloat16), upto, preferred_element_type=jnp.float32)
    slot = jnp.where(cold, rank.astype(jnp.int32) - 1, -1)
    pick = slot[:, None, :] == jnp.arange(COLD, dtype=jnp.int32)[None, :, None]
    cold_ids = jnp.sum(jnp.where(pick, candidates[:, None, :], 0), axis=2)
    cold_target = jnp.sum(jnp.where(pick, target[:, None, :], 0.0), axis=2)
    cold_rows = lookup(location, cold_ids.reshape(-1)).reshape(q_rows, COLD)
    return entropy, count, target_sum, cold_rows, cold_target


def shards(queries, teacher, slab, candidates, hot_ids, location):
    groups = lax.axis_size("corpus")
    reps = lax.axis_size("rep")
    me = lax.axis_index("corpus")
    q_rows, feat_dim = queries.shape
    per_owner = slab.shape[0]
    hot_each = hot_ids.shape[0] // groups
    scale = 2.0 / math.sqrt(feat_dim)
    f32 = jnp.float32

    all_queries = lax.all_gather(queries, "corpus", axis=0, tiled=True)
    entropy, count, target_sum, cold_rows, cold_target = prepare(
        teacher, candidates, hot_ids, location
    )
    parts = [
        count.reshape(q_rows, groups, hot_each).transpose(1, 0, 2),
        target_sum.reshape(q_rows, groups, hot_each).transpose(1, 0, 2),
        jnp.broadcast_to(cold_rows.astype(f32)[None], (groups, q_rows, COLD)),
        jnp.broadcast_to(cold_target[None], (groups, q_rows, COLD)),
    ]
    message = lax.all_to_all(
        jnp.concatenate(parts, axis=2), "corpus", split_axis=0, concat_axis=0, tiled=True
    ).reshape(groups * q_rows, -1)
    count = message[:, :hot_each]
    target_sum = message[:, hot_each : 2 * hot_each]
    cold_rows = message[:, 2 * hot_each : 2 * hot_each + COLD].astype(jnp.int32)
    cold_target = message[:, 2 * hot_each + COLD :]

    own_ids = lax.dynamic_slice_in_dim(hot_ids, me * hot_each, hot_each)
    own_hot = lookup(location, own_ids) - me * per_owner
    row_iota = jnp.arange(per_owner, dtype=jnp.int32)
    place = (own_hot[:, None] == row_iota[None, :]).astype(jnp.bfloat16)
    hot_emb = jnp.dot(place, slab, preferred_element_type=f32).astype(jnp.bfloat16)

    across = (((1,), (1,)), ((), ()))
    hot_scores = scale * lax.dot_general(all_queries, hot_emb, across, preferred_element_type=f32)
    scores = scale * lax.dot_general(all_queries, slab, across, preferred_element_type=f32)
    local = cold_rows - me * per_owner
    mine = (local >= 0) & (local < per_owner)
    cold_scores = jnp.stack(
        [
            jnp.sum(jnp.where(local[:, c, None] == row_iota[None, :], scores, 0.0), axis=1)
            for c in range(COLD)
        ],
        axis=1,
    )
    top = jnp.maximum(
        jnp.max(hot_scores, axis=1), jnp.max(jnp.where(mine, cold_scores, -jnp.inf), axis=1)
    )
    total = jnp.sum((1.0 + count) * jnp.exp(hot_scores - top[:, None]), axis=1) + jnp.sum(
        jnp.where(mine, jnp.exp(cold_scores - top[:, None]), 0.0), axis=1
    )
    dots = jnp.sum(target_sum * hot_scores, axis=1) + jnp.sum(
        jnp.where(mine, cold_target * cold_scores, 0.0), axis=1
    )
    stats = lax.all_gather(jnp.stack([top, total, dots]), "corpus", axis=0)
    tops = stats[:, 0]
    row_top = jnp.max(tops, axis=0)
    log_total = row_top + jnp.log(jnp.sum(stats[:, 1] * jnp.exp(tops - row_top[None]), axis=0))
    loss_all = log_total - jnp.sum(stats[:, 2], axis=0)
    loss_rows = entropy + lax.dynamic_slice_in_dim(loss_all, me * q_rows, q_rows)

    hot_weight = (
        (1.0 + count) * jnp.exp(hot_scores - log_total[:, None]) - target_sum
    ).astype(jnp.bfloat16)
    cold_weight = jnp.where(mine, jnp.exp(cold_scores - log_total[:, None]) - cold_target, 0.0)
    cold_weight = cold_weight.astype(jnp.bfloat16).astype(f32)
    weight = jnp.dot(hot_weight, place, preferred_element_type=f32)
    for c in range(COLD):
        weight = weight + jnp.where(
            local[:, c, None] == row_iota[None, :], cold_weight[:, c, None], 0.0
        )
    weight = weight.astype(jnp.bfloat16)

    slab_part = scale * lax.dot_general(
        weight, all_queries, (((0,), (0,)), ((), ())), preferred_element_type=f32
    )
    slab_parts = lax.all_to_all(
        slab_part.astype(jnp.bfloat16).reshape(reps, per_owner // reps, feat_dim),
        "rep", split_axis=0, concat_axis=0, tiled=True,
    )
    query_part = scale * jnp.dot(weight, slab, preferred_element_type=f32)
    query_parts = lax.all_to_all(
        query_part.astype(jnp.bfloat16).reshape(groups, q_rows, feat_dim),
        "corpus", split_axis=0, concat_axis=0, tiled=True,
    )
    slab_grad = jnp.sum(slab_parts.astype(f32), axis=0)
    query_grad = jnp.sum(query_parts.astype(f32), axis=0)
    return (loss_rows, query_grad, slab_grad)


def solution(mesh):
    return jax.shard_map(
        shards,
        mesh=mesh,
        in_specs=(
            P(("corpus", "rep"), None),
            P(("corpus", "rep"), None),
            P("corpus", None),
            P(("corpus", "rep"), None),
            P(),
            P(),
        ),
        out_specs=(P(("corpus", "rep")), P(("corpus", "rep"), None), P(("corpus", "rep"), None)),
        check_vma=False,
    )
```

profile of v0, /device:TPU:0, one launch (start us, length us, event | category | flops | bytes accessed | tf_op | source)
XLA Modules:
  0.0 184.1 jit_solution(5106646927420530306)
XLA Ops:
  7.2 0.0 copy-start
  7.2 0.0 all-gather.4.cloned.1.call-start
  7.2 0.7 all-gather.4.cloned.1.call-update
  7.9 0.8 reduce_max.36
  8.7 0.8 exponential_reduce_fusion
  9.5 1.3 subtract_exponential_fusion
  10.8 0.8 copy.34
  11.6 4.4 %compare_reduce_fusion = pred[128,64]{1,0:T(8,128)(4,1)S(1)} fusion(s32[256]{0:T(256)} %param.10, s32[128,64]{1,0:T(8,128)S(1)} %copy.34), kind=kLoop, calls=%fused_computation | loop fusion | flops 4186112 | bytes 41984 | tf_op jit(solution)/shard_map/reduce_or | solution.py:35
  16.0 0.1 copy.38
  16.1 0.2 fusion.3
  16.3 0.8 select_reduce_fusion.9
  17.1 0.1 copy.36
  17.2 0.1 copy.39
  17.3 0.1 broadcast_in_dim_reshape.4
  17.4 3.6 %fusion = (f32[128,256]{1,0:T(8,128)S(1)}, f32[128,256]{1,0:T(8,128)S(1)}) fusion(s32[256]{0:T(256)} %param.10, s32[128,64]{1,0:T(8,128)S(1)} %copy.34, f32[128,64]{1,0:T(8,128)S(1)} %copy.36), kind=kLoop, calls=%fused_computation.3 | loop fusion | flops 10420224 | bytes 328704 | tf_op jit(solution)/shard_map/reduce_sum | solution.py:33
  21.1 0.1 copy.35
  21.2 0.0 copy-start.2
  21.2 0.1 copy.37
  21.3 0.8 fusion.23
  22.1 0.5 fusion.6
  22.6 0.1 fusion.5
  22.7 0.1 convert_element_type.75
  22.8 0.1 select_reduce_fusion.8
  22.9 0.7 pad_maximum_fusion
  23.6 7.3 %all-to-all-start = ((f32[8,128,80]{1,2,0:T(8,128)}), f32[8,128,80]{1,2,0:T(8,128)S(1)}, u32[]{:S(2)}, u32[]{:S(2)}) async-start(f32[8,128,80]{1,2,0:T(8,128)} %pad_maximum_fusion), calls=%async_computation | async-start | bytes 655360 | tf_op jit(solution)/shard_map/all_to_all | solution.py:67
  30.9 0.0 copy-done.2
  30.9 0.1 and_select_fusion.1
  31.0 0.1 and_select_fusion
  31.1 0.2 fusion.32
  31.3 0.2 fusion.36
  31.4 0.5 convert_subtract_fusion
  32.0 9.3 %all-to-all-done = f32[8,128,80]{1,2,0:T(8,128)S(1)} async-done(((f32[8,128,80]{1,2,0:T(8,128)}), f32[8,128,80]{1,2,0:T(8,128)S(1)}, u32[]{:S(2)}, u32[]{:S(2)}) %all-to-all-start) | async-done | bytes 327712 | tf_op jit(solution)/shard_map/all_to_all | solution.py:67
  41.4 15.9 %all-gather.4.cloned.1.call-done = bf16[1024,768]{1,0:T(8,128)(2,1)} async-done(((bf16[128,768]{1,0:T(8,128)(2,1)}), bf16[1024,768]{1,0:T(8,128)(2,1)}) %all-gather.4.cloned.1.call-update) | async-done | bytes 1572880 | tf_op jit(solution)/shard_map/all_gather | solution.py:57
  57.2 0.0 copy-done
  57.2 0.0 copy-start.1
  57.2 8.7 %select_reduce_fusion = (f32[1024]{0:T(1024)S(1)}, f32[1024]{0:T(1024)S(1)}, f32[1024]{0:T(1024)S(1)}, f32[1024]{0:T(1024)S(1)}, f32[1024]{0:T(1024)}, /*index=5*/f32[1024]{0:T(1024)}, f32[1024]{0:T(1024)}, f32[1024]{0:T(1024)}) fusion(s32[1024]{0:T(1024)S(1)} %bitcast.130, s32[1024]{0:T(1024)S(1)} %bitcast.128, s32[1024]{0:T(1024)S(1)} %bitcast.126, ...), kind=kOutput, calls=%fused_computation.6 | convolution fusion | flops 1636818944 | bytes 3211264 | tf_op jit(solution)/shard_map/dot_general | solution.py:83
  65.9 0.8 stack.41
  66.7 0.0 copy-done.1
  66.7 2.1 %fusion.47 = (f32[1024]{0:T(1024)S(1)}, f32[32,1024]{1,0:T(8,128)}) fusion(bf16[1024,768]{1,0:T(8,128)(2,1)S(1)} %copy-done.1, bf16[1024,768]{1,0:T(8,128)(2,1)S(1)} %copy-done, s32[32]{0:T(128)} %convert_subtract_fusion), kind=kOutput, calls=%fused_computation.127 | convolution fusion | flops 100785152 | bytes 3281024 | tf_op jit(solution)/shard_map/dot_general | solution.py:82
  68.9 1.0 fusion.10
  69.9 30.6 %all-gather.1 = f32[8,3,1024]{2,1,0:T(4,128)S(1)} all-gather(f32[1,3,1024]{2,1,0:T(4,128)S(1)} %maximum_bitcast_fusion), channel_id=2, replica_groups=mesh['corpus'=8,'rep'=4] {'corpus'}, dimensions={0}, use_global_device_ids=true | all-gather | bytes 110592 | tf_op jit(solution)/shard_map/all_gather | solution.py:102
  100.5 0.1 fusion.44
  100.7 6.1 %add_convert_fusion = bf16[1024,1024]{0,1:T(8,128)(2,1)S(1)} fusion(f32[1024]{0:T(1024)S(1)} %bitcast.133, f32[1024]{0:T(1024)S(1)} %bitcast.134, f32[1024]{0:T(1024)S(1)} %bitcast.135, f32[1024]{0:T(1024)S(1)} %bitcast.136, f32[1024]{0:T(1024)S(1)} %bitcast.137, f32[1024]{0:T(1024)S(1)} %bitcast.138, f32[1024]{0:T(1024)S(1)} %bitcast.139, ...), kind=kOutput, calls=%fused_computation.5 | convolution fusion | flops 93519872 | bytes 2560128 | tf_op jit(solution)/shard_map/dot_general | solution.py:114
  106.8 0.0 copy-start.4
  106.8 3.0 %multiply_convert_fusion = bf16[1024,768]{1,0:T(8,128)(2,1)} fusion(bf16[1024,1024]{0,1:T(8,128)(2,1)S(1)} %add_convert_fusion, bf16[1024,768]{1,0:T(8,128)(2,1)S(1)} %copy-done.1), kind=kOutput, calls=%fused_computation.23 | convolution fusion | flops 1612185600 | bytes 5242880 | tf_op jit(solution)/shard_map/dot_general | solution.py:121
  109.8 0.0 copy-done.4
  109.8 3.7 %all-to-all-start.2 = ((bf16[4,256,768]{2,1,0:T(8,128)(2,1)}), bf16[4,256,768]{2,1,0:T(8,128)(2,1)S(1)}, u32[]{:S(2)}, u32[]{:S(2)}) async-start(bf16[4,256,768]{2,1,0:T(8,128)(2,1)} %bitcast.110), calls=%async_computation.2 | async-start | bytes 3145728 | tf_op jit(solution)/shard_map/all_to_all | solution.py:124
  113.6 4.6 %multiply_convert_fusion.1 = bf16[1024,768]{1,0:T(8,128)(2,1)} fusion(bf16[1024,1024]{0,1:T(8,128)(2,1)} %copy-done.4, bf16[1024,768]{1,0:T(8,128)(2,1)S(1)} %copy-done), kind=kOutput, calls=%fused_computation.25 | convolution fusion | flops 1612185600 | bytes 5242880 | tf_op jit(solution)/shard_map/dot_general | solution.py:128
  118.2 0.0 copy-start.3
  118.2 15.3 %all-to-all-done.2 = bf16[4,256,768]{2,1,0:T(8,128)(2,1)S(1)} async-done(((bf16[4,256,768]{2,1,0:T(8,128)(2,1)}), bf16[4,256,768]{2,1,0:T(8,128)(2,1)S(1)}, u32[]{:S(2)}, u32[]{:S(2)}) %all-to-all-start.2) | async-done | bytes 1572896 | tf_op jit(solution)/shard_map/all_to_all | solution.py:124
  133.4 4.3 %all-to-all-start.1 = ((bf16[8,128,768]{2,1,0:T(8,128)(2,1)}), bf16[8,128,768]{2,1,0:T(8,128)(2,1)}, u32[]{:S(2)}, u32[]{:S(2)}) async-start(bf16[8,128,768]{2,1,0:T(8,128)(2,1)} %bitcast.109), calls=%async_computation.1 | async-start | bytes 3145728 | tf_op jit(solution)/shard_map/all_to_all | solution.py:129
  137.7 0.0 copy-done.3
  137.8 0.6 dynamic-slice_add_fusion
  138.3 1.1 convert_reduce_fusion
  139.4 35.4 %all-to-all-done.1 = bf16[8,128,768]{2,1,0:T(8,128)(2,1)} async-done(((bf16[8,128,768]{2,1,0:T(8,128)(2,1)}), bf16[8,128,768]{2,1,0:T(8,128)(2,1)}, u32[]{:S(2)}, u32[]{:S(2)}) %all-to-all-start.1) | async-done | bytes 1572896 | tf_op jit(solution)/shard_map/all_to_all | solution.py:129
  174.8 2.4 %convert_reduce_fusion.1 = f32[128,768]{1,0:T(8,128)} fusion(bf16[8,128,768]{2,1,0:T(8,128)(2,1)} %all-to-all-done.1), kind=kLoop, calls=%fused_computation.24 | loop fusion | flops 1474560 | bytes 1966080 | tf_op jit(solution)/shard_map/reduce_sum | solution.py:134
  (19 shorter events, 0.3 us)
Async XLA Ops:
  7.2 50.1 %copy-start = (bf16[1024,768]{1,0:T(8,128)(2,1)S(1)}, bf16[1024,768]{1,0:T(8,128)(2,1)}, u32[]{:S(2)}) copy-start(bf16[1024,768]{1,0:T(8,128)(2,1)} %param.8) | copy-start | bytes 4718596
  7.2 50.0 %all-gather.4.cloned.1.call-start = ((), (), s32[]{:S(2)}) async-start(), calls=%async_computation.3 | async-start | bytes 1769472 | tf_op jit(solution)/shard_map/all_gather | solution.py:57
  21.2 9.7 %copy-start.2 = (s32[256]{0:T(256)S(1)}, s32[256]{0:T(256)}, u32[]{:S(2)}) copy-start(s32[256]{0:T(256)} %param.10) | copy-start | bytes 3076
  23.6 17.6 %all-to-all-start = ((f32[8,128,80]{1,2,0:T(8,128)}), f32[8,128,80]{1,2,0:T(8,128)S(1)}, u32[]{:S(2)}, u32[]{:S(2)}) async-start(f32[8,128,80]{1,2,0:T(8,128)} %pad_maximum_fusion), calls=%async_computation | async-start | bytes 655360 | tf_op jit(solution)/shard_map/all_to_all | solution.py:67
  57.2 9.5 %copy-start.1 = (bf16[1024,768]{1,0:T(8,128)(2,1)S(1)}, bf16[1024,768]{1,0:T(8,128)(2,1)}, u32[]{:S(2)}) copy-start(bf16[1024,768]{1,0:T(8,128)(2,1)} %all-gather.4.cloned.1.call-done) | copy-start | bytes 4718596
  106.8 3.0 %copy-start.4 = (bf16[1024,1024]{0,1:T(8,128)(2,1)}, bf16[1024,1024]{0,1:T(8,128)(2,1)S(1)}, u32[]{:S(2)}) copy-start(bf16[1024,1024]{0,1:T(8,128)(2,1)S(1)} %add_convert_fusion) | copy-start | bytes 6291460
  109.8 23.6 %all-to-all-start.2 = ((bf16[4,256,768]{2,1,0:T(8,128)(2,1)}), bf16[4,256,768]{2,1,0:T(8,128)(2,1)S(1)}, u32[]{:S(2)}, u32[]{:S(2)}) async-start(bf16[4,256,768]{2,1,0:T(8,128)(2,1)} %bitcast.110), calls=%async_computation.2 | async-start | bytes 3145728 | tf_op jit(solution)/shard_map/all_to_all | solution.py:124
  118.2 19.6 %copy-start.3 = (f32[128]{0:T(128)S(1)}, f32[128]{0:T(128)}, u32[]{:S(2)}) copy-start(f32[128]{0:T(128)} %get-tuple-element.30) | copy-start | bytes 1540
  133.4 41.4 %all-to-all-start.1 = ((bf16[8,128,768]{2,1,0:T(8,128)(2,1)}), bf16[8,128,768]{2,1,0:T(8,128)(2,1)}, u32[]{:S(2)}, u32[]{:S(2)}) async-start(bf16[8,128,768]{2,1,0:T(8,128)(2,1)} %bitcast.109), calls=%async_computation.1 | async-start | bytes 3145728 | tf_op jit(solution)/shard_map/all_to_all | solution.py:129
Sparse Core Ops, SparseCore 0:
  10.2 46.9 all-gather.3
where the time goes:
time: 185 us; the launch traced here: 184 us
  waiting for transfers between devices  76.5 us (41%)
  blocking collectives  30.6 us (17%)
  matrix products  25.4 us (14%)
  other arithmetic  19.6 us (11%)
  starting transfers between devices  15.3 us (8%)
  between operations  14.3 us (8%)
  local copies, waits for them, and re-layouts  2.41 us (1%)
    all_to_all x1, waiting for transfers between devices, shards(): lax.all_to_all(query_part.astype(jnp.bfloat16).reshape(groups, q_rows, fe...  35.4 us
    all_gather x1, blocking collectives, shards(): stats = lax.all_gather(jnp.stack([top, total, dots]), 'corpus', axis=0)  30.6 us
    all_gather x1, waiting for transfers between devices, shards(): all_queries = lax.all_gather(queries, 'corpus', axis=0, tiled=True)  15.9 us
    all_to_all x1, waiting for transfers between devices, shards(): lax.all_to_all(slab_part.astype(jnp.bfloat16).reshape(reps, per_owner //...  15.3 us
    all_to_all x1, waiting for transfers between devices, shards(): lax.all_to_all(jnp.concatenate(parts, axis=2), 'corpus', split_axis=0, co...  9.28 us
    dot_general x1, matrix products, shards(): lax.dot_general(all_queries, slab, across, preferred_element_type=f32)  8.69 us
    all_to_all x1, starting transfers between devices, shards(): lax.all_to_all(jnp.concatenate(parts, axis=2), 'corpus', split_axis=0, co...  7.25 us
    dot_general x1, matrix products, shards(): weight = jnp.dot(hot_weight, place, preferred_element_type=f32)  6.11 us
  transfers between devices with their start and end apart: 4, of which 4 were waited for; matrix products, arithmetic and copies ran while one was open for 13% of the time, Pallas kernels for 0%

commit v1 on v0

--- a/solution.py
+++ b/solution.py
@@ -99,7 +99,11 @@
     dots = jnp.sum(target_sum * hot_scores, axis=1) + jnp.sum(
         jnp.where(mine, cold_target * cold_scores, 0.0), axis=1
     )
-    stats = lax.all_gather(jnp.stack([top, total, dots]), "corpus", axis=0)
+    stats = jnp.stack([top, total, dots])
+    stats = lax.all_to_all(
+        jnp.broadcast_to(stats[None], (groups, *stats.shape)),
+        "corpus", split_axis=0, concat_axis=0, tiled=True,
+    )
     tops = stats[:, 0]
     row_top = jnp.max(tops, axis=0)
     log_total = row_top + jnp.log(jnp.sum(stats[:, 1] * jnp.exp(tops - row_top[None]), axis=0))
@@ -118,19 +122,21 @@
         )
     weight = weight.astype(jnp.bfloat16)
 
-    slab_part = scale * lax.dot_general(
-        weight, all_queries, (((0,), (0,)), ((), ())), preferred_element_type=f32
-    )
-    slab_parts = lax.all_to_all(
-        slab_part.astype(jnp.bfloat16).reshape(reps, per_owner // reps, feat_dim),
-        "rep", split_axis=0, concat_axis=0, tiled=True,
-    )
     query_part = scale * jnp.dot(weight, slab, preferred_element_type=f32)
     query_parts = lax.all_to_all(
         query_part.astype(jnp.bfloat16).reshape(groups, q_rows, feat_dim),
         "corpus", split_axis=0, concat_axis=0, tiled=True,
     )
-    slab_grad = jnp.sum(slab_parts.astype(f32), axis=0)
+    slab_part = scale * lax.dot_general(
+        weight, all_queries, (((0,), (0,)), ((), ())), preferred_element_type=f32
+    )
+    slab_part = slab_part.astype(jnp.bfloat16).reshape(reps, per_owner // reps, feat_dim)
+    rep = lax.axis_index("rep")
+    slab_grad = lax.dynamic_index_in_dim(slab_part, rep, 0, keepdims=False).astype(f32)
+    for step in range(1, reps):
+        outgoing = lax.dynamic_index_in_dim(slab_part, (rep + step) % reps, 0, keepdims=False)
+        arrived = lax.ppermute(outgoing, "rep", [(r, (r + step) % reps) for r in range(reps)])
+        slab_grad = slab_grad + arrived.astype(f32)
     query_grad = jnp.sum(query_parts.astype(f32), axis=0)
     return (loss_rows, query_grad, slab_grad)
 

time: 185 us -> 138 us (0.75)
  waiting for transfers between devices: 76.5 us -> 49.6 us
  blocking collectives: 30.6 us -> 10.6 us
  local copies, waits for them, and re-layouts: 2.41 us -> 4.52 us
    all_gather x1 -> x0, blocking collectives: 30.6 us -> none  [shards(): stats = lax.all_gather(jnp.stack([top, total, dots]), 'corpus', axis=0)]
    all_to_all x1, waiting for transfers between devices: 35.4 us -> 7.45 us  [shards(): lax.all_to_all(query_part.astype(jnp.bfloat16).reshape(groups, q_rows, fe...]
    ppermute x0 -> x3, waiting for transfers between devices: none -> 16.4 us  [shards(): lax.ppermute(outgoing, 'rep', [(r, (r + step) % reps) for r in range(reps)])]
    all_to_all x1 -> x0, waiting for transfers between devices: 15.3 us -> none  [shards(): lax.all_to_all(slab_part.astype(jnp.bfloat16).reshape(reps, per_owner //...]
    all_to_all x0 -> x1, blocking collectives: none -> 10.6 us  [shards(): lax.all_to_all(jnp.broadcast_to(stats[None], (groups, *stats.shape)), 'co...]
    all_to_all x1 -> x0, starting transfers between devices: 3.74 us -> none  [shards(): lax.all_to_all(slab_part.astype(jnp.bfloat16).reshape(reps, per_owner //...]
    ppermute x0 -> x3, starting transfers between devices: none -> 3.21 us  [shards(): lax.ppermute(outgoing, 'rep', [(r, (r + step) % reps) for r in range(reps)])]
    add x0 -> x1, other arithmetic: none -> 2.41 us  [shards(): slab_grad = slab_grad + arrived.astype(f32)]
  transfers between devices with their start and end apart: 4 -> 6, of which waited for: 4 -> 6; matrix products, arithmetic and copies ran while one was open for 13% -> 18% of each run, Pallas kernels for 0% -> 0%
where the time goes in v1:
time: 138 us; the launch traced here: 137 us
  waiting for transfers between devices  49.6 us (36%)
  matrix products  24.8 us (18%)
  other arithmetic  19.5 us (14%)
  between operations  14.4 us (10%)
  starting transfers between devices  14.1 us (10%)
  blocking collectives  10.6 us (8%)
  local copies, waits for them, and re-layouts  4.52 us (3%)
    ppermute x3, waiting for transfers between devices, shards(): lax.ppermute(outgoing, 'rep', [(r, (r + step) % reps) for r in range(reps)])  16.4 us
    all_gather x1, waiting for transfers between devices, shards(): all_queries = lax.all_gather(queries, 'corpus', axis=0, tiled=True)  15.9 us
    all_to_all x1, blocking collectives, shards(): lax.all_to_all(jnp.broadcast_to(stats[None], (groups, *stats.shape)), 'co...  10.6 us
    all_to_all x1, waiting for transfers between devices, shards(): lax.all_to_all(jnp.concatenate(parts, axis=2), 'corpus', split_axis=0, co...  9.25 us
    dot_general x1, matrix products, shards(): lax.dot_general(all_queries, slab, across, preferred_element_type=f32)  8.68 us
    all_to_all x1, waiting for transfers between devices, shards(): lax.all_to_all(query_part.astype(jnp.bfloat16).reshape(groups, q_rows, fe...  7.45 us
    all_to_all x1, starting transfers between devices, shards(): lax.all_to_all(jnp.concatenate(parts, axis=2), 'corpus', split_axis=0, co...  7.25 us
    dot_general x1, matrix products, shards(): weight = jnp.dot(hot_weight, place, preferred_element_type=f32)  6.14 us
  transfers between devices with their start and end apart: 6, of which 6 were waited for; matrix products, arithmetic and copies ran while one was open for 18% of the time, Pallas kernels for 0%

profile of v1, /device:TPU:0, one launch (start us, length us, event | category | flops | bytes accessed | tf_op | source)
XLA Modules:
  0.0 137.4 jit_solution(3545331417960285245)
XLA Ops:
  7.2 0.0 copy-start
  7.2 0.0 all-gather.2.cloned.1.call-start
  7.2 0.7 all-gather.2.cloned.1.call-update
  7.9 0.8 reduce_max.36
  8.7 0.8 exponential_reduce_fusion
  9.5 1.3 subtract_exponential_fusion
  10.8 0.8 copy.34
  11.6 4.4 %compare_reduce_fusion = pred[128,64]{1,0:T(8,128)(4,1)S(1)} fusion(s32[256]{0:T(256)} %param.10, s32[128,64]{1,0:T(8,128)S(1)} %copy.34), kind=kLoop, calls=%fused_computation | loop fusion | flops 4186112 | bytes 41984 | tf_op jit(solution)/shard_map/reduce_or | solution.py:35
  16.0 0.1 copy.38
  16.1 0.2 fusion.3
  16.3 0.8 select_reduce_fusion.9
  17.1 0.1 copy.36
  17.2 0.1 copy.39
  17.3 0.1 broadcast_in_dim_reshape.4
  17.4 3.6 %fusion = (f32[128,256]{1,0:T(8,128)S(1)}, f32[128,256]{1,0:T(8,128)S(1)}) fusion(s32[256]{0:T(256)} %param.10, s32[128,64]{1,0:T(8,128)S(1)} %copy.34, f32[128,64]{1,0:T(8,128)S(1)} %copy.36), kind=kLoop, calls=%fused_computation.3 | loop fusion | flops 10420224 | bytes 328704 | tf_op jit(solution)/shard_map/reduce_sum | solution.py:33
  21.1 0.1 copy.35
  21.2 0.0 copy-start.3
  21.2 0.1 copy.37
  21.3 0.8 fusion.25
  22.1 0.5 fusion.8
  22.5 0.1 fusion.7
  22.7 0.1 convert_element_type.87
  22.8 0.1 select_reduce_fusion.8
  22.9 0.7 pad_maximum_fusion
  23.6 7.3 %all-to-all-start = ((f32[8,128,80]{1,2,0:T(8,128)}), f32[8,128,80]{1,2,0:T(8,128)S(1)}, u32[]{:S(2)}, u32[]{:S(2)}) async-start(f32[8,128,80]{1,2,0:T(8,128)} %pad_maximum_fusion), calls=%async_computation | async-start | bytes 655360 | tf_op jit(solution)/shard_map/all_to_all | solution.py:67
  30.9 0.0 copy-done.3
  30.9 0.1 and_select_fusion.1
  31.0 0.1 and_select_fusion
  31.1 0.2 fusion.34
  31.3 0.2 fusion.38
  31.4 0.6 convert_subtract_fusion
  32.0 9.2 %all-to-all-done = f32[8,128,80]{1,2,0:T(8,128)S(1)} async-done(((f32[8,128,80]{1,2,0:T(8,128)}), f32[8,128,80]{1,2,0:T(8,128)S(1)}, u32[]{:S(2)}, u32[]{:S(2)}) %all-to-all-start) | async-done | bytes 327712 | tf_op jit(solution)/shard_map/all_to_all | solution.py:67
  41.4 0.0 copy-start.4
  41.4 15.9 %all-gather.2.cloned.1.call-done = bf16[1024,768]{1,0:T(8,128)(2,1)} async-done(((bf16[128,768]{1,0:T(8,128)(2,1)}), bf16[1024,768]{1,0:T(8,128)(2,1)}) %all-gather.2.cloned.1.call-update) | async-done | bytes 1572880 | tf_op jit(solution)/shard_map/all_gather | solution.py:57
  57.2 0.0 copy-done
  57.2 8.7 %select_reduce_fusion = (f32[1024]{0:T(1024)S(1)}, f32[1024]{0:T(1024)S(1)}, f32[1024]{0:T(1024)S(1)}, f32[1024]{0:T(1024)S(1)}, f32[1024]{0:T(1024)}, /*index=5*/f32[1024]{0:T(1024)}, f32[1024]{0:T(1024)}, f32[1024]{0:T(1024)}) fusion(s32[1024]{0:T(1024)S(1)} %bitcast.138, s32[1024]{0:T(1024)S(1)} %bitcast.136, s32[1024]{0:T(1024)S(1)} %bitcast.134, ...), kind=kOutput, calls=%fused_computation.6 | convolution fusion | flops 1636818944 | bytes 3211264 | tf_op jit(solution)/shard_map/dot_general | solution.py:83
  65.9 0.0 copy-done.4
  65.9 0.8 stack.41
  66.7 0.0 copy-done.2
  66.7 2.2 %fusion.48 = (f32[1024]{0:T(1024)S(1)}, f32[32,1024]{1,0:T(8,128)}) fusion(bf16[1024,768]{1,0:T(8,128)(2,1)S(1)} %copy-done.2, bf16[1024,768]{1,0:T(8,128)(2,1)S(1)} %copy-done, s32[32]{0:T(128)} %convert_subtract_fusion), kind=kOutput, calls=%fused_computation.131 | convolution fusion | flops 100785152 | bytes 3281024 | tf_op jit(solution)/shard_map/dot_general | solution.py:82
  68.9 1.0 fusion.12
  70.0 10.6 %all_to_all.15 = f32[8,3,1024]{2,1,0:T(4,128)S(1)} all-to-all(f32[8,3,1024]{2,1,0:T(4,128)S(1)} %broadcast_in_dim.208), channel_id=1, replica_groups=mesh['corpus'=8,'rep'=4] {'corpus'}, dimensions={0} | all-to-all | bytes 196608 | tf_op jit(solution)/shard_map/all_to_all | solution.py:103
  80.5 0.1 slice_reduce_fusion
  80.7 6.1 %add_convert_fusion = bf16[1024,1024]{0,1:T(8,128)(2,1)S(1)} fusion(f32[1024]{0:T(1024)S(1)} %bitcast.141, f32[1024]{0:T(1024)S(1)} %bitcast.142, f32[1024]{0:T(1024)S(1)} %bitcast.143, f32[1024]{0:T(1024)S(1)} %bitcast.144, f32[1024]{0:T(1024)S(1)} %bitcast.145, f32[1024]{0:T(1024)S(1)} %bitcast.146, f32[1024]{0:T(1024)S(1)} %bitcast.147, ...), kind=kOutput, calls=%fused_computation.5 | convolution fusion | flops 93519872 | bytes 2560128 | tf_op jit(solution)/shard_map/dot_general | solution.py:118
  86.9 0.0 copy-start.6
  86.9 3.1 %multiply_convert_fusion.1 = bf16[1024,768]{1,0:T(8,128)(2,1)} fusion(bf16[1024,1024]{0,1:T(8,128)(2,1)S(1)} %add_convert_fusion, bf16[1024,768]{1,0:T(8,128)(2,1)S(1)} %copy-done), kind=kOutput, calls=%fused_computation.24 | convolution fusion | flops 1612185600 | bytes 5242880 | tf_op jit(solution)/shard_map/dot_general | solution.py:125
  90.0 0.0 copy-done.6
  90.0 3.6 %all-to-all-start.2 = ((bf16[8,128,768]{2,1,0:T(8,128)(2,1)}), bf16[8,128,768]{2,1,0:T(8,128)(2,1)S(1)}, u32[]{:S(2)}, u32[]{:S(2)}) async-start(bf16[8,128,768]{2,1,0:T(8,128)(2,1)} %bitcast.116), calls=%async_computation.2 | async-start | bytes 3145728 | tf_op jit(solution)/shard_map/all_to_all | solution.py:126
  93.6 3.8 %multiply_convert_fusion = bf16[1024,768]{1,0:T(8,128)(2,1)S(1)} fusion(bf16[1024,1024]{0,1:T(8,128)(2,1)} %copy-done.6, bf16[1024,768]{1,0:T(8,128)(2,1)} %all-gather.2.cloned.1.call-done), kind=kOutput, calls=%fused_computation.22 | convolution fusion | flops 1612185600 | bytes 5242880 | tf_op jit(solution)/shard_map/dot_general | solution.py:130
  97.5 0.0 copy-start.1
  97.5 0.0 copy-start.5
  97.5 1.1 copy-done.1
  98.6 1.0 dynamic-slice_bitcast_fusion.2
  99.6 0.0 collective-permute-start
  99.6 1.7 %collective-permute-start.2 = (bf16[256,768]{1,0:T(8,128)(2,1)}, bf16[256,768]{1,0:T(8,128)(2,1)}, u32[]{:S(2)}, u32[]{:S(2)}) collective-permute-start(bf16[256,768]{1,0:T(8,128)(2,1)} %get-tuple-element.26), channel_id=1, source_target_pairs={{0,3},{1,0},{2,1},{3,2},{4,7},{5,4},{6,5},{7,6},{8,11},{9,8},{10,9... | collective-permute-start | bytes 1179656 | tf_op jit(solution)/shard_map/ppermute | solution.py:138
  101.3 1.5 %collective-permute-start.1 = (bf16[256,768]{1,0:T(8,128)(2,1)S(1)}, bf16[256,768]{1,0:T(8,128)(2,1)}, u32[]{:S(2)}, u32[]{:S(2)}) collective-permute-start(bf16[256,768]{1,0:T(8,128)(2,1)S(1)} %get-tuple-element.27), channel_id=1, source_target_pairs={{0,2},{1,3},{2,0},{3,1},{4,6},{5,7},{6,4},{7,5},{8,10},{9,11},{10,... | collective-permute-start | bytes 1179656 | tf_op jit(solution)/shard_map/ppermute | solution.py:138
  102.8 0.0 copy-done.5
  102.8 0.6 dynamic-slice_add_fusion
  103.4 6.1 %collective-permute-done = bf16[256,768]{1,0:T(8,128)(2,1)} collective-permute-done((bf16[256,768]{1,0:T(8,128)(2,1)}, bf16[256,768]{1,0:T(8,128)(2,1)}, u32[]{:S(2)}, u32[]{:S(2)}) %collective-permute-start) | collective-permute-done | bytes 393248 | tf_op jit(solution)/shard_map/ppermute | solution.py:138
  109.5 1.6 %collective-permute-done.2 = bf16[256,768]{1,0:T(8,128)(2,1)} collective-permute-done((bf16[256,768]{1,0:T(8,128)(2,1)}, bf16[256,768]{1,0:T(8,128)(2,1)}, u32[]{:S(2)}, u32[]{:S(2)}) %collective-permute-start.2) | collective-permute-done | bytes 393248 | tf_op jit(solution)/shard_map/ppermute | solution.py:138
  111.1 8.6 %collective-permute-done.1 = bf16[256,768]{1,0:T(8,128)(2,1)} collective-permute-done((bf16[256,768]{1,0:T(8,128)(2,1)S(1)}, bf16[256,768]{1,0:T(8,128)(2,1)}, u32[]{:S(2)}, u32[]{:S(2)}) %collective-permute-start.1) | collective-permute-done | bytes 393248 | tf_op jit(solution)/shard_map/ppermute | solution.py:138
  119.7 2.4 %fusion.5 = f32[256,768]{1,0:T(8,128)} fusion(bf16[256,768]{1,0:T(8,128)(2,1)} %collective-permute-done.2, bf16[256,768]{1,0:T(8,128)(2,1)} %collective-permute-done.1, bf16[256,768]{1,0:T(8,128)(2,1)} %collective-permute-done, bf16[4,256,768]{2,1,0:T(8,128)(2,1)} %bitcast.118, s32[]{:T(128)S(6)} %select_n.203), kind=kLoop, calls=%fused_computation.32 | loop fusion | flops 1376256 | bytes 2359300 | tf_op jit(solution)/shard_map/add | solution.py:139
  122.1 7.4 %all-to-all-done.2 = bf16[8,128,768]{2,1,0:T(8,128)(2,1)S(1)} async-done(((bf16[8,128,768]{2,1,0:T(8,128)(2,1)}), bf16[8,128,768]{2,1,0:T(8,128)(2,1)S(1)}, u32[]{:S(2)}, u32[]{:S(2)}) %all-to-all-start.2) | async-done | bytes 1572896 | tf_op jit(solution)/shard_map/all_to_all | solution.py:126
  129.6 1.0 convert_reduce_fusion
  (21 shorter events, 0.3 us)
Async XLA Ops:
  7.2 50.1 %copy-start = (bf16[1024,768]{1,0:T(8,128)(2,1)S(1)}, bf16[1024,768]{1,0:T(8,128)(2,1)}, u32[]{:S(2)}) copy-start(bf16[1024,768]{1,0:T(8,128)(2,1)} %param.8) | copy-start | bytes 4718596
  7.2 50.1 %all-gather.2.cloned.1.call-start = ((), (), s32[]{:S(2)}) async-start(), calls=%async_computation.3 | async-start | bytes 1769472 | tf_op jit(solution)/shard_map/all_gather | solution.py:57
  21.2 9.7 %copy-start.3 = (s32[256]{0:T(256)S(1)}, s32[256]{0:T(256)}, u32[]{:S(2)}) copy-start(s32[256]{0:T(256)} %param.10) | copy-start | bytes 3076
  23.6 17.6 %all-to-all-start = ((f32[8,128,80]{1,2,0:T(8,128)}), f32[8,128,80]{1,2,0:T(8,128)S(1)}, u32[]{:S(2)}, u32[]{:S(2)}) async-start(f32[8,128,80]{1,2,0:T(8,128)} %pad_maximum_fusion), calls=%async_computation | async-start | bytes 655360 | tf_op jit(solution)/shard_map/all_to_all | solution.py:67
  41.4 24.6 %copy-start.4 = (s32[1024,1]{0,1:T(1,128)}, s32[1024,1]{0,1:T(1,128)S(1)}, u32[]{:S(2)}) copy-start(s32[1024,1]{0,1:T(1,128)S(1)} %get-tuple-element.47) | copy-start | bytes 12292
  57.2 9.5 %copy-start.2 = (bf16[1024,768]{1,0:T(8,128)(2,1)S(1)}, bf16[1024,768]{1,0:T(8,128)(2,1)}, u32[]{:S(2)}) copy-start(bf16[1024,768]{1,0:T(8,128)(2,1)} %all-gather.2.cloned.1.call-done) | copy-start | bytes 4718596
  86.9 3.1 %copy-start.6 = (bf16[1024,1024]{0,1:T(8,128)(2,1)}, bf16[1024,1024]{0,1:T(8,128)(2,1)S(1)}, u32[]{:S(2)}) copy-start(bf16[1024,1024]{0,1:T(8,128)(2,1)S(1)} %add_convert_fusion) | copy-start | bytes 6291460
  90.0 39.6 %all-to-all-start.2 = ((bf16[8,128,768]{2,1,0:T(8,128)(2,1)}), bf16[8,128,768]{2,1,0:T(8,128)(2,1)S(1)}, u32[]{:S(2)}, u32[]{:S(2)}) async-start(bf16[8,128,768]{2,1,0:T(8,128)(2,1)} %bitcast.116), calls=%async_computation.2 | async-start | bytes 3145728 | tf_op jit(solution)/shard_map/all_to_all | solution.py:126
  97.5 1.2 copy-start.1
  97.5 5.3 %copy-start.5 = (f32[128]{0:T(128)S(1)}, f32[128]{0:T(128)}, u32[]{:S(2)}) copy-start(f32[128]{0:T(128)} %get-tuple-element.31) | copy-start | bytes 1540
  99.6 9.9 %collective-permute-start = (bf16[256,768]{1,0:T(8,128)(2,1)}, bf16[256,768]{1,0:T(8,128)(2,1)}, u32[]{:S(2)}, u32[]{:S(2)}) collective-permute-start(bf16[256,768]{1,0:T(8,128)(2,1)} %get-tuple-element.25), channel_id=1, source_target_pairs={{0,1},{1,2},{2,3},{3,0},{4,5},{5,6},{6,7},{7,4},{8,9},{9,10},{10,1... | collective-permute-start | bytes 1179656 | tf_op jit(solution)/shard_map/ppermute | solution.py:138
  99.6 11.5 %collective-permute-start.2 = (bf16[256,768]{1,0:T(8,128)(2,1)}, bf16[256,768]{1,0:T(8,128)(2,1)}, u32[]{:S(2)}, u32[]{:S(2)}) collective-permute-start(bf16[256,768]{1,0:T(8,128)(2,1)} %get-tuple-element.26), channel_id=1, source_target_pairs={{0,3},{1,0},{2,1},{3,2},{4,7},{5,4},{6,5},{7,6},{8,11},{9,8},{10,9... | collective-permute-start | bytes 1179656 | tf_op jit(solution)/shard_map/ppermute | solution.py:138
  101.3 18.4 %collective-permute-start.1 = (bf16[256,768]{1,0:T(8,128)(2,1)S(1)}, bf16[256,768]{1,0:T(8,128)(2,1)}, u32[]{:S(2)}, u32[]{:S(2)}) collective-permute-start(bf16[256,768]{1,0:T(8,128)(2,1)S(1)} %get-tuple-element.27), channel_id=1, source_target_pairs={{0,2},{1,3},{2,0},{3,1},{4,6},{5,7},{6,4},{7,5},{8,10},{9,11},{10,... | collective-permute-start | bytes 1179656 | tf_op jit(solution)/shard_map/ppermute | solution.py:138
Sparse Core Ops, SparseCore 0:
  10.2 46.9 all-gather.1

commit v2 on v1

--- a/solution.py
+++ b/solution.py
@@ -44,44 +44,35 @@
     return entropy, count, target_sum, cold_rows, cold_target
 
 
-def shards(queries, teacher, slab, candidates, hot_ids, location):
-    groups = lax.axis_size("corpus")
-    reps = lax.axis_size("rep")
-    me = lax.axis_index("corpus")
-    q_rows, feat_dim = queries.shape
+def gather_blocks(block, axis):
+    groups = lax.axis_size(axis)
+    if groups & (groups - 1):
+        return lax.all_gather(block, axis, axis=0)
+    me = lax.axis_index(axis)
+    held = block[None]
+    bit = groups // 2
+    while bit:
+        other = lax.ppermute(held, axis, [(i, i ^ bit) for i in range(groups)])
+        upper = (me // bit) % 2 == 1
+        first = jnp.where(upper, other, held)
+        second = jnp.where(upper, held, other)
+        held = jnp.stack([first, second], axis=1).reshape(-1, *block.shape)
+        bit //= 2
+    return held
+
+
+def score(all_queries, message, slab, hot_emb, base, hot_each, scale):
+    f32 = jnp.float32
     per_owner = slab.shape[0]
-    hot_each = hot_ids.shape[0] // groups
-    scale = 2.0 / math.sqrt(feat_dim)
-    f32 = jnp.float32
-
-    all_queries = lax.all_gather(queries, "corpus", axis=0, tiled=True)
-    entropy, count, target_sum, cold_rows, cold_target = prepare(
-        teacher, candidates, hot_ids, location
-    )
-    parts = [
-        count.reshape(q_rows, groups, hot_each).transpose(1, 0, 2),
-        target_sum.reshape(q_rows, groups, hot_each).transpose(1, 0, 2),
-        jnp.broadcast_to(cold_rows.astype(f32)[None], (groups, q_rows, COLD)),
-        jnp.broadcast_to(cold_target[None], (groups, q_rows, COLD)),
-    ]
-    message = lax.all_to_all(
-        jnp.concatenate(parts, axis=2), "corpus", split_axis=0, concat_axis=0, tiled=True
-    ).reshape(groups * q_rows, -1)
+    row_iota = jnp.arange(per_owner, dtype=jnp.int32)
     count = message[:, :hot_each]
     target_sum = message[:, hot_each : 2 * hot_each]
     cold_rows = message[:, 2 * hot_each : 2 * hot_each + COLD].astype(jnp.int32)
     cold_target = message[:, 2 * hot_each + COLD :]
-
-    own_ids = lax.dynamic_slice_in_dim(hot_ids, me * hot_each, hot_each)
-    own_hot = lookup(location, own_ids) - me * per_owner
-    row_iota = jnp.arange(per_owner, dtype=jnp.int32)
-    place = (own_hot[:, None] == row_iota[None, :]).astype(jnp.bfloat16)
-    hot_emb = jnp.dot(place, slab, preferred_element_type=f32).astype(jnp.bfloat16)
-
     across = (((1,), (1,)), ((), ()))
     hot_scores = scale * lax.dot_general(all_queries, hot_emb, across, preferred_element_type=f32)
     scores = scale * lax.dot_general(all_queries, slab, across, preferred_element_type=f32)
-    local = cold_rows - me * per_owner
+    local = cold_rows - base
     mine = (local >= 0) & (local < per_owner)
     cold_scores = jnp.stack(
         [
@@ -100,16 +91,13 @@
         jnp.where(mine, cold_target * cold_scores, 0.0), axis=1
     )
     stats = jnp.stack([top, total, dots])
-    stats = lax.all_to_all(
-        jnp.broadcast_to(stats[None], (groups, *stats.shape)),
-        "corpus", split_axis=0, concat_axis=0, tiled=True,
-    )
-    tops = stats[:, 0]
-    row_top = jnp.max(tops, axis=0)
-    log_total = row_top + jnp.log(jnp.sum(stats[:, 1] * jnp.exp(tops - row_top[None]), axis=0))
-    loss_all = log_total - jnp.sum(stats[:, 2], axis=0)
-    loss_rows = entropy + lax.dynamic_slice_in_dim(loss_all, me * q_rows, q_rows)
-
+    return stats, (hot_scores, count, target_sum, local, mine, cold_scores, cold_target)
+
+
+def weigh(kept, log_total, place):
+    hot_scores, count, target_sum, local, mine, cold_scores, cold_target = kept
+    f32 = jnp.float32
+    row_iota = jnp.arange(place.shape[1], dtype=jnp.int32)
     hot_weight = (
         (1.0 + count) * jnp.exp(hot_scores - log_total[:, None]) - target_sum
     ).astype(jnp.bfloat16)
@@ -120,15 +108,85 @@
         weight = weight + jnp.where(
             local[:, c, None] == row_iota[None, :], cold_weight[:, c, None], 0.0
         )
-    weight = weight.astype(jnp.bfloat16)
-
-    query_part = scale * jnp.dot(weight, slab, preferred_element_type=f32)
+    return weight.astype(jnp.bfloat16)
+
+
+def shards(queries, teacher, slab, candidates, hot_ids, location):
+    groups = lax.axis_size("corpus")
+    reps = lax.axis_size("rep")
+    me = lax.axis_index("corpus")
+    q_rows, feat_dim = queries.shape
+    per_owner = slab.shape[0]
+    hot_each = hot_ids.shape[0] // groups
+    scale = 2.0 / math.sqrt(feat_dim)
+    f32 = jnp.float32
+
+    half = q_rows // 2
+    all_queries = [gather_blocks(queries[:half], "corpus"), gather_blocks(queries[half:], "corpus")]
+    entropy, count, target_sum, cold_rows, cold_target = prepare(
+        teacher, candidates, hot_ids, location
+    )
+    parts = [
+        count.reshape(q_rows, groups, hot_each).transpose(1, 0, 2),
+        target_sum.reshape(q_rows, groups, hot_each).transpose(1, 0, 2),
+        jnp.broadcast_to(cold_rows.astype(f32)[None], (groups, q_rows, COLD)),
+        jnp.broadcast_to(cold_target[None], (groups, q_rows, COLD)),
+    ]
+    message = lax.all_to_all(
+        jnp.concatenate(parts, axis=2), "corpus", split_axis=0, concat_axis=0, tiled=True
+    )
+
+    own_ids = lax.dynamic_slice_in_dim(hot_ids, me * hot_each, hot_each)
+    own_hot = lookup(location, own_ids) - me * per_owner
+    row_iota = jnp.arange(per_owner, dtype=jnp.int32)
+    place = (own_hot[:, None] == row_iota[None, :]).astype(jnp.bfloat16)
+    hot_emb = jnp.dot(place, slab, preferred_element_type=f32).astype(jnp.bfloat16)
+
+    queries_of = [part.reshape(-1, feat_dim) for part in all_queries]
+    messages = [message[:, :half], message[:, half:]]
+    stats, kept = [], []
+    for part, text in zip(queries_of, messages):
+        one, rest = score(
+            part, text.reshape(part.shape[0], -1), slab, hot_emb, me * per_owner, hot_each, scale
+        )
+        stats.append(one)
+        kept.append(rest)
+    stats = jnp.concatenate(stats, axis=1)
+    stats = lax.all_to_all(
+        jnp.broadcast_to(stats[None], (groups, *stats.shape)),
+        "corpus", split_axis=0, concat_axis=0, tiled=True,
+    )
+    tops = stats[:, 0]
+    row_top = jnp.max(tops, axis=0)
+    log_total = row_top + jnp.log(jnp.sum(stats[:, 1] * jnp.exp(tops - row_top[None]), axis=0))
+    loss_all = log_total - jnp.sum(stats[:, 2], axis=0)
+    split = groups * half
+    loss_own = [
+        lax.dynamic_slice_in_dim(loss_all[:split], me * half, half),
+        lax.dynamic_slice_in_dim(loss_all[split:], me * (q_rows - half), q_rows - half),
+    ]
+    loss_rows = entropy + jnp.concatenate(loss_own)
+
+    weights = [
+        weigh(kept[0], log_total[:split], place),
+        weigh(kept[1], log_total[split:], place),
+    ]
+    query_part = jnp.concatenate(
+        [
+            (scale * jnp.dot(weight, slab, preferred_element_type=f32))
+            .astype(jnp.bfloat16)
+            .reshape(groups, -1, feat_dim)
+            for weight in weights
+        ],
+        axis=1,
+    )
     query_parts = lax.all_to_all(
-        query_part.astype(jnp.bfloat16).reshape(groups, q_rows, feat_dim),
-        "corpus", split_axis=0, concat_axis=0, tiled=True,
-    )
-    slab_part = scale * lax.dot_general(
-        weight, all_queries, (((0,), (0,)), ((), ())), preferred_element_type=f32
+        query_part, "corpus", split_axis=0, concat_axis=0, tiled=True
+    )
+    down = (((0,), (0,)), ((), ()))
+    slab_part = scale * sum(
+        lax.dot_general(weight, part, down, preferred_element_type=f32)
+        for weight, part in zip(weights, queries_of)
     )
     slab_part = slab_part.astype(jnp.bfloat16).reshape(reps, per_owner // reps, feat_dim)
     rep = lax.axis_index("rep")

time: 138 us -> 145 us (1.051)
  between operations: 14.4 us -> 1.74 us
  other arithmetic: 19.5 us -> 27.7 us
  starting transfers between devices: 14.1 us -> 21.4 us
  blocking collectives: 10.6 us -> 12.9 us
  matrix products: 24.8 us -> 26.8 us
  waiting for transfers between devices: 49.6 us -> 47.8 us
    ppermute x0 -> x6, waiting for transfers between devices: none -> 21.5 us  [gather_blocks(): other = lax.ppermute(held, axis, [(i, i ^ bit) for i in range(groups)])]
    all_gather x1 -> x0, waiting for transfers between devices: 15.9 us -> none  [shards(): all_queries = lax.all_gather(queries, 'corpus', axis=0, tiled=True)]
    all_to_all x1, waiting for transfers between devices: 9.25 us -> 0.01 us  [shards(): lax.all_to_all(jnp.concatenate(parts, axis=2), 'corpus', split_axis=0, co...]
    ppermute x0 -> x6, starting transfers between devices: none -> 9.08 us  [gather_blocks(): other = lax.ppermute(held, axis, [(i, i ^ bit) for i in range(groups)])]
    all_to_all x1, blocking collectives: 10.6 us -> 12.9 us  [shards(): lax.all_to_all(jnp.broadcast_to(stats[None], (groups, *stats.shape)), 'co...]
    dot_general x5 -> x11, matrix products: 23.9 us -> 25.9 us  [the longest x2 10.5 us: score(): lax.dot_general(all_queries, slab, across, preferred_element_type=f32)]
    concatenate x0 -> x2, other arithmetic: none -> 1.92 us  [the longest x1 1.25 us: shards(): jnp.concatenate([(scale * jnp.dot(weight, slab, preferred_element_type=f3...]
    reduce_sum x2 -> x4, other arithmetic: 1 us -> 2.85 us  [the longest x2 1.5 us: score(): jnp.sum((1.0 + count) * jnp.exp(hot_scores - top[:, None]), axis=1)]
  transfers between devices with their start and end apart: 6 -> 11, of which waited for: 6 -> 7; matrix products, arithmetic and copies ran while one was open for 18% -> 16% of each run, Pallas kernels for 0% -> 0%
where the time goes in v2:
time: 145 us; the launch traced here: 144 us
  waiting for transfers between devices  47.8 us (33%)
  other arithmetic  27.7 us (19%)
  matrix products  26.8 us (18%)
  starting transfers between devices  21.4 us (15%)
  blocking collectives  12.9 us (9%)
  local copies, waits for them, and re-layouts  5.9 us (4%)
  between operations  1.74 us (1%)
    ppermute x6, waiting for transfers between devices, gather_blocks(): other = lax.ppermute(held, axis, [(i, i ^ bit) for i in range(groups)])  21.5 us
    ppermute x3, waiting for transfers between devices, shards(): lax.ppermute(outgoing, 'rep', [(r, (r + step) % reps) for r in range(reps)])  17.4 us
    all_to_all x1, blocking collectives, shards(): lax.all_to_all(jnp.broadcast_to(stats[None], (groups, *stats.shape)), 'co...  12.9 us
    dot_general x2, matrix products, score(): lax.dot_general(all_queries, slab, across, preferred_element_type=f32)  10.5 us
    ppermute x6, starting transfers between devices, gather_blocks(): other = lax.ppermute(held, axis, [(i, i ^ bit) for i in range(groups)])  9.08 us
    all_to_all x1, waiting for transfers between devices, shards(): lax.all_to_all(query_part, 'corpus', split_axis=0, concat_axis=0, tiled=T...  8.9 us
    dot_general x2, matrix products, weigh(): weight = jnp.dot(hot_weight, place, preferred_element_type=f32)  7.68 us
    all_to_all x1, starting transfers between devices, shards(): lax.all_to_all(jnp.concatenate(parts, axis=2), 'corpus', split_axis=0, co...  6.07 us
  transfers between devices with their start and end apart: 11, of which 7 were waited for; matrix products, arithmetic and copies ran while one was open for 16% of the time, Pallas kernels for 0%

profile of v2, /device:TPU:0, one launch (start us, length us, event | category | flops | bytes accessed | tf_op | source)
XLA Modules:
  0.0 144.3 jit_solution(17950802008398274475)
XLA Ops:
  0.7 1.1 slice_bitcast_fusion.1
  1.7 4.1 %collective-permute-start = (bf16[1,64,768]{2,1,0:T(8,128)(2,1)S(1)}, bf16[1,64,768]{2,1,0:T(8,128)(2,1)S(1)}, u32[]{:S(2)}, u32[]{:S(2)}) collective-permute-start(bf16[1,64,768]{2,1,0:T(8,128)(2,1)S(1)} %get-tuple-element.58), channel_id=1, source_target_pairs={{0,16},{4,20},{8,24},{12,28},{16,0},{20,4},{24,8},{28,12},{1,17},{... | collective-permute-start | bytes 294920 | tf_op jit(solution)/shard_map/ppermute | solution.py:55
  5.9 0.8 reduce_max.54
  6.7 0.8 exponential_reduce_fusion
  7.5 1.3 subtract_exponential_fusion
  8.8 0.8 copy.43
  9.7 4.4 %compare_reduce_fusion = pred[128,64]{1,0:T(8,128)(4,1)S(1)} fusion(s32[256]{0:T(256)} %param.10, s32[128,64]{1,0:T(8,128)S(1)} %copy.43), kind=kLoop, calls=%fused_computation | loop fusion | flops 4186112 | bytes 41984 | tf_op jit(solution)/shard_map/reduce_or | solution.py:35
  14.1 0.2 fusion.3
  14.3 0.8 select_reduce_fusion.17
  15.3 0.8 fusion.14
  16.3 0.5 fusion.8
  17.0 3.0 %fusion = (f32[128,256]{1,0:T(8,128)S(1)}, f32[128,256]{1,0:T(8,128)S(1)}) fusion(s32[256]{0:T(256)S(1)} %copy-done.18, s32[128,64]{1,0:T(8,128)S(1)} %copy.43, f32[128,64]{1,0:T(8,128)S(1)} %copy.45), kind=kLoop, calls=%fused_computation.3 | loop fusion | flops 10420224 | bytes 328704 | tf_op jit(solution)/shard_map/reduce_sum | solution.py:33
  20.2 0.7 pad_maximum_fusion.5
  21.0 6.1 %all-to-all-start = ((f32[8,128,80]{1,2,0:T(8,128)}), f32[8,128,80]{1,2,0:T(8,128)S(1)}, u32[]{:S(2)}, u32[]{:S(2)}) async-start(f32[8,128,80]{1,2,0:T(8,128)} %pad_maximum_fusion.5), calls=%async_computation | async-start | bytes 655360 | tf_op jit(solution)/shard_map/all_to_all | solution.py:135
  27.2 0.2 fusion.26
  27.4 0.2 fusion.31
  27.7 2.1 %collective-permute-start.4 = (bf16[2,64,768]{2,1,0:T(8,128)(2,1)S(1)}, bf16[2,64,768]{2,1,0:T(8,128)(2,1)S(1)}, u32[]{:S(2)}, u32[]{:S(2)}) collective-permute-start(bf16[2,64,768]{2,1,0:T(8,128)(2,1)S(1)} %maximum_bitcast_fusion.1), channel_id=1, source_target_pairs={{0,8},{4,12},{8,0},{12,4},{16,24},{20,28},{24,16},{28,20},{1,9},{5... | collective-permute-start | bytes 589832 | tf_op jit(solution)/shard_map/ppermute | solution.py:55
  29.8 0.4 convolution_convert_fusion
  30.3 9.9 %collective-permute-done.4 = bf16[2,64,768]{2,1,0:T(8,128)(2,1)S(1)} collective-permute-done((bf16[2,64,768]{2,1,0:T(8,128)(2,1)S(1)}, bf16[2,64,768]{2,1,0:T(8,128)(2,1)S(1)}, u32[]{:S(2)}, u32[]{:S(2)}) %collective-permute-start.4) | collective-permute-done | bytes 196640 | tf_op jit(solution)/shard_map/ppermute | solution.py:55
  40.3 1.2 collective-permute-start.5
  41.5 1.0 collective-permute-done.1
  42.6 1.5 %collective-permute-start.2 = (bf16[4,64,768]{2,1,0:T(8,128)(2,1)S(1)}, bf16[4,64,768]{2,1,0:T(8,128)(2,1)}, u32[]{:S(2)}, u32[]{:S(2)}) collective-permute-start(bf16[4,64,768]{2,1,0:T(8,128)(2,1)S(1)} %bitcast.198), channel_id=1, source_target_pairs={{0,4},{4,0},{8,12},{12,8},{16,20},{20,16},{24,28},{28,24},{1,5},{5... | collective-permute-start | bytes 1179656 | tf_op jit(solution)/shard_map/ppermute | solution.py:55
  44.1 0.2 fusion.42
  44.3 0.1 copy.53
  44.4 0.1 reshape.278
  44.5 0.1 copy.50
  44.7 0.1 reshape.275
  44.9 0.6 fusion.45
  45.6 6.4 %collective-permute-done.5 = bf16[4,64,768]{2,1,0:T(8,128)(2,1)} collective-permute-done((bf16[4,64,768]{2,1,0:T(8,128)(2,1)S(1)}, bf16[4,64,768]{2,1,0:T(8,128)(2,1)}, u32[]{:S(2)}, u32[]{:S(2)}) %collective-permute-start.5) | collective-permute-done | bytes 393248 | tf_op jit(solution)/shard_map/ppermute | solution.py:55
  52.0 4.2 %collective-permute-done.2 = bf16[4,64,768]{2,1,0:T(8,128)(2,1)} collective-permute-done((bf16[4,64,768]{2,1,0:T(8,128)(2,1)S(1)}, bf16[4,64,768]{2,1,0:T(8,128)(2,1)}, u32[]{:S(2)}, u32[]{:S(2)}) %collective-permute-start.2) | collective-permute-done | bytes 393248 | tf_op jit(solution)/shard_map/ppermute | solution.py:55
  56.2 1.2 select_bitcast_fusion.1
  57.6 0.4 fusion.49
  58.1 4.9 %select_reduce_fusion = (f32[512]{0:T(512)S(1)}, f32[512]{0:T(512)S(1)}, f32[512]{0:T(512)S(1)}, f32[512]{0:T(512)S(1)}, f32[512]{0:T(512)S(1)}, /*index=5*/f32[512]{0:T(512)S(1)}, f32[512]{0:T(512)S(1)}, f32[512]{0:T(512)S(1)}) fusion(s32[512]{0:T(512)S(1)} %bitcast.239, s32[512]{0:T(512)S(1)} %bitcast.227, s32[512]{0:T(512)S(1)} %bitcast.229, ...), kind=kOutput, calls=%fused_computation.9 | convolution fusion | flops 818409472 | bytes 2392064 | tf_op jit(solution)/shard_map/dot_general | solution.py:74
  63.1 0.6 multiply_reduce_fusion.1
  63.8 0.6 select_reduce_fusion.19
  64.5 1.5 %fusion.50 = (f32[512]{0:T(512)}, f32[512,32]{0,1:T(8,128)}) fusion(bf16[512,768]{1,0:T(8,128)(2,1)S(1)} %bitcast.192, bf16[32,768]{1,0:T(8,128)(2,1)S(1)} %convolution_convert_fusion), kind=kOutput, calls=%fused_computation.186 | convolution fusion | flops 25198080 | bytes 903168 | tf_op jit(solution)/shard_map/dot_general | solution.py:73
  66.2 5.6 %select_reduce_fusion.8 = (f32[512]{0:T(512)}, f32[512]{0:T(512)}, f32[512]{0:T(512)}, f32[512]{0:T(512)}, f32[512]{0:T(512)}, /*index=5*/f32[512]{0:T(512)}, f32[512]{0:T(512)}, f32[512]{0:T(512)}) fusion(s32[512]{0:T(512)S(1)} %bitcast.223, s32[512]{0:T(512)S(1)} %bitcast.211, s32[512]{0:T(512)S(1)} %bitcast.213, s32[512]{0:T(512)S(1)} %bitcast.215, ...), kind=kOutput, calls=%fused_computation.25 | convolution fusion | flops 818409472 | bytes 2392064 | tf_op jit(solution)/shard_map/dot_general | solution.py:74
  71.7 1.3 stack.137
  73.1 0.8 select_reduce_fusion.23
  73.8 0.7 max.34
  74.5 0.9 multiply_reduce_fusion.3
  75.4 0.7 select_reduce_fusion.22
  76.1 0.7 add.239
  76.8 0.7 add.237
  77.5 0.7 maximum_maximum_fusion
  78.2 12.9 %all_to_all.15 = f32[8,3,1024]{2,1,0:T(4,128)S(1)} all-to-all(f32[8,3,1024]{2,1,0:T(4,128)S(1)} %broadcast_in_dim.312), channel_id=1, replica_groups=mesh['corpus'=8,'rep'=4] {'corpus'}, dimensions={0} | all-to-all | bytes 196608 | tf_op jit(solution)/shard_map/all_to_all | solution.py:155
  91.2 0.6 fusion.41
  91.8 0.7 fusion.33
  92.5 4.3 %add_convert_fusion = bf16[512,1024]{1,0:T(8,128)(2,1)S(1)} fusion(f32[512]{0:T(512)S(1)} %bitcast.250, f32[512]{0:T(512)S(1)} %bitcast.251, f32[512]{0:T(512)S(1)} %bitcast.252, f32[512]{0:T(512)S(1)} %bitcast.253, f32[512]{0:T(512)S(1)} %bitcast.254, f32[512]{0:T(512)S(1)} %bitcast.255, f32[512]{0:T(512)S(1)} %bitcast.256, f32[512]{0:T(512)S(1)} %bitcast.249, ...), kind=kOutput, calls=%fused_computation.7 | convolution fusion | flops 46776320 | bytes 1280128 | tf_op jit(solution)/shard_map/dot_general | solution.py:106
  96.9 1.0 multiply_convert_fusion.1
  98.1 3.4 %add_convert_fusion.1 = bf16[512,1024]{1,0:T(8,128)(2,1)S(1)} fusion(f32[512]{0:T(512)S(1)} %bitcast.242, f32[512]{0:T(512)S(1)} %bitcast.243, f32[512]{0:T(512)S(1)} %bitcast.244, f32[512]{0:T(512)S(1)} %bitcast.245, f32[512]{0:T(512)S(1)} %bitcast.246, f32[512]{0:T(512)S(1)} %bitcast.247, f32[512]{0:T(512)S(1)} %bitcast.248, f32[512]{0:T(512)S(1)} %bitcast.241, ...), kind=kOutput, calls=%fused_computation.8 | convolution fusion | flops 46776320 | bytes 1280512 | tf_op jit(solution)/shard_map/dot_general | solution.py:106
  101.5 1.0 multiply_convert_fusion.2
  102.5 1.3 pad_maximum_fusion
  103.7 4.5 %all-to-all-start.2 = ((bf16[8,128,768]{2,1,0:T(8,128)(2,1)}), bf16[8,128,768]{2,1,0:T(8,128)(2,1)}, u32[]{:S(2)}, u32[]{:S(2)}) async-start(bf16[8,128,768]{2,1,0:T(8,128)(2,1)} %pad_maximum_fusion), calls=%async_computation.2 | async-start | bytes 3145728 | tf_op jit(solution)/shard_map/all_to_all | solution.py:183
  108.3 2.3 %fusion.51 = f32[1024,768]{1,0:T(8,128)S(1)} fusion(bf16[512,1024]{1,0:T(8,128)(2,1)} %copy-done.1, bf16[512,768]{1,0:T(8,128)(2,1)S(1)} %bitcast.194), kind=kOutput, calls=%fused_computation.187 | convolution fusion | flops 805306368 | bytes 4980736 | tf_op jit(solution)/shard_map/dot_general | solution.py:188
  110.6 1.1 multiply_convert_fusion
  112.0 1.6 %collective-permute-start.7 = (bf16[256,768]{1,0:T(8,128)(2,1)S(1)}, bf16[256,768]{1,0:T(8,128)(2,1)S(1)}, u32[]{:S(2)}, u32[]{:S(2)}) collective-permute-start(bf16[256,768]{1,0:T(8,128)(2,1)S(1)} %get-tuple-element.41), channel_id=1, source_target_pairs={{0,2},{1,3},{2,0},{3,1},{4,6},{5,7},{6,4},{7,5},{8,10},{9,11},{10,... | collective-permute-start | bytes 1179656 | tf_op jit(solution)/shard_map/ppermute | solution.py:196
  113.6 0.2 collective-permute-start.6
  113.9 0.6 maximum_add_fusion
  114.5 5.9 %collective-permute-done.8 = bf16[256,768]{1,0:T(8,128)(2,1)S(1)} collective-permute-done((bf16[256,768]{1,0:T(8,128)(2,1)S(1)}, bf16[256,768]{1,0:T(8,128)(2,1)S(1)}, u32[]{:S(2)}, u32[]{:S(2)}) %collective-permute-start.8) | collective-permute-done | bytes 393248 | tf_op jit(solution)/shard_map/ppermute | solution.py:196
  120.4 11.5 %collective-permute-done.7 = bf16[256,768]{1,0:T(8,128)(2,1)S(1)} collective-permute-done((bf16[256,768]{1,0:T(8,128)(2,1)S(1)}, bf16[256,768]{1,0:T(8,128)(2,1)S(1)}, u32[]{:S(2)}, u32[]{:S(2)}) %collective-permute-start.7) | collective-permute-done | bytes 393248 | tf_op jit(solution)/shard_map/ppermute | solution.py:196
  131.9 1.1 fusion.5
  133.0 8.9 %all-to-all-done.2 = bf16[8,128,768]{2,1,0:T(8,128)(2,1)} async-done(((bf16[8,128,768]{2,1,0:T(8,128)(2,1)}), bf16[8,128,768]{2,1,0:T(8,128)(2,1)}, u32[]{:S(2)}, u32[]{:S(2)}) %all-to-all-start.2) | async-done | bytes 1572896 | tf_op jit(solution)/shard_map/all_to_all | solution.py:183
  141.9 2.4 %convert_reduce_fusion = f32[128,768]{1,0:T(8,128)} fusion(bf16[8,128,768]{2,1,0:T(8,128)(2,1)} %all-to-all-done.2), kind=kLoop, calls=%fused_computation.6 | loop fusion | flops 1474560 | bytes 1966080 | tf_op jit(solution)/shard_map/reduce_sum | solution.py:198
  (147 shorter events, 2.6 us)
Async XLA Ops:
  0.6 29.2 %copy-start = (bf16[1024,768]{1,0:T(8,128)(2,1)S(1)}, bf16[1024,768]{1,0:T(8,128)(2,1)}, u32[]{:S(2)}) copy-start(bf16[1024,768]{1,0:T(8,128)(2,1)} %param.8) | copy-start | bytes 4718596
  0.6 16.4 %copy-start.18 = (s32[256]{0:T(256)S(1)}, s32[256]{0:T(256)}, u32[]{:S(2)}) copy-start(s32[256]{0:T(256)} %param.10) | copy-start | bytes 3076
  1.7 25.9 %collective-permute-start = (bf16[1,64,768]{2,1,0:T(8,128)(2,1)S(1)}, bf16[1,64,768]{2,1,0:T(8,128)(2,1)S(1)}, u32[]{:S(2)}, u32[]{:S(2)}) collective-permute-start(bf16[1,64,768]{2,1,0:T(8,128)(2,1)S(1)} %get-tuple-element.58), channel_id=1, source_target_pairs={{0,16},{4,20},{8,24},{12,28},{16,0},{20,4},{24,8},{28,12},{1,17},{... | collective-permute-start | bytes 294920 | tf_op jit(solution)/shard_map/ppermute | solution.py:55
  5.8 21.8 %collective-permute-start.3 = (bf16[1,64,768]{2,1,0:T(8,128)(2,1)S(1)}, bf16[1,64,768]{2,1,0:T(8,128)(2,1)S(1)}, u32[]{:S(2)}, u32[]{:S(2)}) collective-permute-start(bf16[1,64,768]{2,1,0:T(8,128)(2,1)S(1)} %get-tuple-element.59), channel_id=1, source_target_pairs={{0,16},{4,20},{8,24},{12,28},{16,0},{20,4},{24,8},{28,12},{1,17},{... | collective-permute-start | bytes 294920 | tf_op jit(solution)/shard_map/ppermute | solution.py:55
  16.7 10.9 %copy-start.4 = (bf16[128,768]{1,0:T(8,128)(2,1)S(1)}, bf16[128,768]{1,0:T(8,128)(2,1)}, u32[]{:S(2)}) copy-start(bf16[128,768]{1,0:T(8,128)(2,1)} %param.6) | copy-start | bytes 589828
  21.0 23.2 %all-to-all-start = ((f32[8,128,80]{1,2,0:T(8,128)}), f32[8,128,80]{1,2,0:T(8,128)S(1)}, u32[]{:S(2)}, u32[]{:S(2)}) async-start(f32[8,128,80]{1,2,0:T(8,128)} %pad_maximum_fusion.5), calls=%async_computation | async-start | bytes 655360 | tf_op jit(solution)/shard_map/all_to_all | solution.py:135
  27.6 2.6 %copy-start.44 = (s32[32]{0:T(128)}, s32[32]{0:T(128)S(1)}, u32[]{:S(2)}) copy-start(s32[32]{0:T(128)S(1)} %convert_subtract_fusion) | copy-start | bytes 388
  27.7 12.5 %collective-permute-start.4 = (bf16[2,64,768]{2,1,0:T(8,128)(2,1)S(1)}, bf16[2,64,768]{2,1,0:T(8,128)(2,1)S(1)}, u32[]{:S(2)}, u32[]{:S(2)}) collective-permute-start(bf16[2,64,768]{2,1,0:T(8,128)(2,1)S(1)} %maximum_bitcast_fusion.1), channel_id=1, source_target_pairs={{0,8},{4,12},{8,0},{12,4},{16,24},{20,28},{24,16},{28,20},{1,9},{5... | collective-permute-start | bytes 589832 | tf_op jit(solution)/shard_map/ppermute | solution.py:55
  30.2 12.3 %collective-permute-start.1 = (bf16[2,64,768]{2,1,0:T(8,128)(2,1)S(1)}, bf16[2,64,768]{2,1,0:T(8,128)(2,1)S(1)}, u32[]{:S(2)}, u32[]{:S(2)}) collective-permute-start(bf16[2,64,768]{2,1,0:T(8,128)(2,1)S(1)} %maximum_bitcast_fusion), channel_id=1, source_target_pairs={{0,8},{4,12},{8,0},{12,4},{16,24},{20,28},{24,16},{28,20},{1,9},{5... | collective-permute-start | bytes 589832 | tf_op jit(solution)/shard_map/ppermute | solution.py:55
  40.3 11.7 %collective-permute-start.5 = (bf16[4,64,768]{2,1,0:T(8,128)(2,1)S(1)}, bf16[4,64,768]{2,1,0:T(8,128)(2,1)}, u32[]{:S(2)}, u32[]{:S(2)}) collective-permute-start(bf16[4,64,768]{2,1,0:T(8,128)(2,1)S(1)} %bitcast.197), channel_id=1, source_target_pairs={{0,4},{4,0},{8,12},{12,8},{16,20},{20,16},{24,28},{28,24},{1,5},{5... | collective-permute-start | bytes 1179656 | tf_op jit(solution)/shard_map/ppermute | solution.py:55
  42.6 13.6 %collective-permute-start.2 = (bf16[4,64,768]{2,1,0:T(8,128)(2,1)S(1)}, bf16[4,64,768]{2,1,0:T(8,128)(2,1)}, u32[]{:S(2)}, u32[]{:S(2)}) collective-permute-start(bf16[4,64,768]{2,1,0:T(8,128)(2,1)S(1)} %bitcast.198), channel_id=1, source_target_pairs={{0,4},{4,0},{8,12},{12,8},{16,20},{20,16},{24,28},{28,24},{1,5},{5... | collective-permute-start | bytes 1179656 | tf_op jit(solution)/shard_map/ppermute | solution.py:55
  44.5 7.5 %copy-start.7 = (f32[512,80]{0,1:T(8,128)}, f32[512,80]{0,1:T(8,128)S(1)}, u32[]{:S(2)}) copy-start(f32[512,80]{0,1:T(8,128)S(1)} %reshape.278) | copy-start | bytes 491524
  44.8 7.2 %copy-start.5 = (f32[512,80]{0,1:T(8,128)}, f32[512,80]{0,1:T(8,128)S(1)}, u32[]{:S(2)}) copy-start(f32[512,80]{0,1:T(8,128)S(1)} %reshape.275) | copy-start | bytes 491524
  44.8 7.2 %copy-start.14 = (s32[512,8]{0,1:T(8,128)}, s32[512,8]{0,1:T(8,128)S(1)}, u32[]{:S(2)}) copy-start(s32[512,8]{0,1:T(8,128)S(1)} %get-tuple-element.111) | copy-start | bytes 49156
  44.9 13.1 %copy-start.36 = (s32[512,1]{0,1:T(1,128)}, s32[512,1]{0,1:T(1,128)S(1)}, u32[]{:S(2)}) copy-start(s32[512,1]{0,1:T(1,128)S(1)} %get-tuple-element.90) | copy-start | bytes 6148
  44.9 13.1 %copy-start.37 = (s32[512,1]{0,1:T(1,128)}, s32[512,1]{0,1:T(1,128)S(1)}, u32[]{:S(2)}) copy-start(s32[512,1]{0,1:T(1,128)S(1)} %get-tuple-element.91) | copy-start | bytes 6148
  44.9 13.1 %copy-start.38 = (s32[512,1]{0,1:T(1,128)}, s32[512,1]{0,1:T(1,128)S(1)}, u32[]{:S(2)}) copy-start(s32[512,1]{0,1:T(1,128)S(1)} %get-tuple-element.92) | copy-start | bytes 6148
  44.9 13.1 %copy-start.39 = (s32[512,1]{0,1:T(1,128)}, s32[512,1]{0,1:T(1,128)S(1)}, u32[]{:S(2)}) copy-start(s32[512,1]{0,1:T(1,128)S(1)} %get-tuple-element.93) | copy-start | bytes 6148
  44.9 13.1 %copy-start.40 = (s32[512,1]{0,1:T(1,128)}, s32[512,1]{0,1:T(1,128)S(1)}, u32[]{:S(2)}) copy-start(s32[512,1]{0,1:T(1,128)S(1)} %get-tuple-element.94) | copy-start | bytes 6148
  44.9 13.1 %copy-start.41 = (s32[512,1]{0,1:T(1,128)}, s32[512,1]{0,1:T(1,128)S(1)}, u32[]{:S(2)}) copy-start(s32[512,1]{0,1:T(1,128)S(1)} %get-tuple-element.95) | copy-start | bytes 6148
  44.9 13.1 %copy-start.42 = (s32[512,1]{0,1:T(1,128)}, s32[512,1]{0,1:T(1,128)S(1)}, u32[]{:S(2)}) copy-start(s32[512,1]{0,1:T(1,128)S(1)} %get-tuple-element.96) | copy-start | bytes 6148
  44.9 13.1 %copy-start.43 = (s32[512,1]{0,1:T(1,128)}, s32[512,1]{0,1:T(1,128)S(1)}, u32[]{:S(2)}) copy-start(s32[512,1]{0,1:T(1,128)S(1)} %get-tuple-element.97) | copy-start | bytes 6148
  58.0 5.2 %copy-start.10 = (f32[512,32]{0,1:T(8,128)}, f32[512,32]{0,1:T(8,128)S(1)}, u32[]{:S(2)}) copy-start(f32[512,32]{0,1:T(8,128)S(1)} %get-tuple-element.105) | copy-start | bytes 196612
  58.0 5.1 %copy-start.8 = (f32[512,80]{0,1:T(8,128)S(1)}, f32[512,80]{0,1:T(8,128)}, u32[]{:S(2)}) copy-start(f32[512,80]{0,1:T(8,128)} %copy-done.7) | copy-start | bytes 491524
  63.1 1.3 copy-start.15
  63.1 3.0 %copy-start.16 = (f32[512]{0:T(512)}, f32[512]{0:T(512)S(1)}, u32[]{:S(2)}) copy-start(f32[512]{0:T(512)S(1)} %max.36) | copy-start | bytes 6148
  63.8 2.3 %copy-start.20 = (s32[512,1]{0,1:T(1,128)S(1)}, s32[512,1]{0,1:T(1,128)}, u32[]{:S(2)}) copy-start(s32[512,1]{0,1:T(1,128)} %get-tuple-element.82) | copy-start | bytes 6148
  63.8 2.3 %copy-start.22 = (s32[512,1]{0,1:T(1,128)S(1)}, s32[512,1]{0,1:T(1,128)}, u32[]{:S(2)}) copy-start(s32[512,1]{0,1:T(1,128)} %get-tuple-element.83) | copy-start | bytes 6148
  63.8 2.3 %copy-start.24 = (s32[512,1]{0,1:T(1,128)S(1)}, s32[512,1]{0,1:T(1,128)}, u32[]{:S(2)}) copy-start(s32[512,1]{0,1:T(1,128)} %get-tuple-element.84) | copy-start | bytes 6148
  63.8 2.3 %copy-start.26 = (s32[512,1]{0,1:T(1,128)S(1)}, s32[512,1]{0,1:T(1,128)}, u32[]{:S(2)}) copy-start(s32[512,1]{0,1:T(1,128)} %get-tuple-element.85) | copy-start | bytes 6148
  63.8 2.3 %copy-start.28 = (s32[512,1]{0,1:T(1,128)S(1)}, s32[512,1]{0,1:T(1,128)}, u32[]{:S(2)}) copy-start(s32[512,1]{0,1:T(1,128)} %get-tuple-element.86) | copy-start | bytes 6148
  63.8 2.4 %copy-start.30 = (s32[512,1]{0,1:T(1,128)S(1)}, s32[512,1]{0,1:T(1,128)}, u32[]{:S(2)}) copy-start(s32[512,1]{0,1:T(1,128)} %get-tuple-element.87) | copy-start | bytes 6148
  63.8 2.4 %copy-start.32 = (s32[512,1]{0,1:T(1,128)S(1)}, s32[512,1]{0,1:T(1,128)}, u32[]{:S(2)}) copy-start(s32[512,1]{0,1:T(1,128)} %get-tuple-element.88) | copy-start | bytes 6148
  63.8 2.4 %copy-start.34 = (s32[512,1]{0,1:T(1,128)S(1)}, s32[512,1]{0,1:T(1,128)}, u32[]{:S(2)}) copy-start(s32[512,1]{0,1:T(1,128)} %get-tuple-element.89) | copy-start | bytes 6148
  66.1 8.4 %copy-start.6 = (f32[512,80]{0,1:T(8,128)S(1)}, f32[512,80]{0,1:T(8,128)}, u32[]{:S(2)}) copy-start(f32[512,80]{0,1:T(8,128)} %copy-done.5) | copy-start | bytes 491524
  66.2 25.6 %copy-start.9 = (f32[512,80]{0,1:T(8,128)S(1)}, f32[512,80]{0,1:T(8,128)}, u32[]{:S(2)}) copy-start(f32[512,80]{0,1:T(8,128)} %copy-done.7) | copy-start | bytes 491524
  66.2 26.3 %copy-start.11 = (f32[512,32]{0,1:T(8,128)S(1)}, f32[512,32]{0,1:T(8,128)}, u32[]{:S(2)}) copy-start(f32[512,32]{0,1:T(8,128)} %copy-done.10) | copy-start | bytes 196612
  96.8 1.1 copy-start.2
  96.8 1.1 copy-start.13
  96.8 1.2 copy-start.12
  96.8 1.2 copy-start.21
  96.9 1.2 copy-start.23
  96.9 1.2 copy-start.25
  96.9 1.2 copy-start.27
  96.9 1.2 copy-start.29
  96.9 1.2 copy-start.31
  96.9 1.2 copy-start.33
  96.9 1.2 copy-start.35
  96.9 1.2 copy-start.45
  101.5 1.0 copy-start.1
  103.7 38.1 %all-to-all-start.2 = ((bf16[8,128,768]{2,1,0:T(8,128)(2,1)}), bf16[8,128,768]{2,1,0:T(8,128)(2,1)}, u32[]{:S(2)}, u32[]{:S(2)}) async-start(bf16[8,128,768]{2,1,0:T(8,128)(2,1)} %pad_maximum_fusion), calls=%async_computation.2 | async-start | bytes 3145728 | tf_op jit(solution)/shard_map/all_to_all | solution.py:183
  108.3 2.4 %copy-start.3 = (bf16[512,1024]{1,0:T(8,128)(2,1)S(1)}, bf16[512,1024]{1,0:T(8,128)(2,1)}, u32[]{:S(2)}) copy-start(bf16[512,1024]{1,0:T(8,128)(2,1)} %copy-done.2) | copy-start | bytes 3145732
  111.8 2.0 %copy-start.17 = (f32[1024]{0:T(1024)S(1)}, f32[1024]{0:T(1024)}, u32[]{:S(2)}) copy-start(f32[1024]{0:T(1024)} %get-tuple-element.31) | copy-start | bytes 12292
  111.8 2.1 %copy-start.19 = (f32[128]{0:T(128)S(1)}, f32[128]{0:T(128)}, u32[]{:S(2)}) copy-start(f32[128]{0:T(128)} %get-tuple-element.63) | copy-start | bytes 1540
  111.9 8.5 %collective-permute-start.8 = (bf16[256,768]{1,0:T(8,128)(2,1)S(1)}, bf16[256,768]{1,0:T(8,128)(2,1)S(1)}, u32[]{:S(2)}, u32[]{:S(2)}) collective-permute-start(bf16[256,768]{1,0:T(8,128)(2,1)S(1)} %get-tuple-element.40), channel_id=1, source_target_pairs={{0,3},{1,0},{2,1},{3,2},{4,7},{5,4},{6,5},{7,6},{8,11},{9,8},{10,9... | collective-permute-start | bytes 1179656 | tf_op jit(solution)/shard_map/ppermute | solution.py:196
  112.0 19.9 %collective-permute-start.7 = (bf16[256,768]{1,0:T(8,128)(2,1)S(1)}, bf16[256,768]{1,0:T(8,128)(2,1)S(1)}, u32[]{:S(2)}, u32[]{:S(2)}) collective-permute-start(bf16[256,768]{1,0:T(8,128)(2,1)S(1)} %get-tuple-element.41), channel_id=1, source_target_pairs={{0,2},{1,3},{2,0},{3,1},{4,6},{5,7},{6,4},{7,5},{8,10},{9,11},{10,... | collective-permute-start | bytes 1179656 | tf_op jit(solution)/shard_map/ppermute | solution.py:196
  113.6 18.3 %collective-permute-start.6 = (bf16[256,768]{1,0:T(8,128)(2,1)S(1)}, bf16[256,768]{1,0:T(8,128)(2,1)S(1)}, u32[]{:S(2)}, u32[]{:S(2)}) collective-permute-start(bf16[256,768]{1,0:T(8,128)(2,1)S(1)} %get-tuple-element.39), channel_id=1, source_target_pairs={{0,1},{1,2},{2,3},{3,0},{4,5},{5,6},{6,7},{7,4},{8,9},{9,10},{10,1... | collective-permute-start | bytes 1179656 | tf_op jit(solution)/shard_map/ppermute | solution.py:196

commit v3 on v1

--- a/solution.py
+++ b/solution.py
@@ -44,6 +44,23 @@
     return entropy, count, target_sum, cold_rows, cold_target
 
 
+def in_order(blocks, index):
+    bit = 1
+    while bit < len(blocks):
+        swap = (index // bit) % 2 == 1
+        blocks = [jnp.where(swap, blocks[i ^ bit], blocks[i]) for i in range(len(blocks))]
+        bit *= 2
+    return blocks
+
+
+def by_pairs(groups):
+    return 4 <= groups <= 16 and groups & (groups - 1) == 0
+
+
+def swap_with(block, distance, groups):
+    return lax.ppermute(block, "corpus", [(i, i ^ distance) for i in range(groups)])
+
+
 def shards(queries, teacher, slab, candidates, hot_ids, location):
     groups = lax.axis_size("corpus")
     reps = lax.axis_size("rep")
@@ -54,7 +71,9 @@
     scale = 2.0 / math.sqrt(feat_dim)
     f32 = jnp.float32
 
-    all_queries = lax.all_gather(queries, "corpus", axis=0, tiled=True)
+    if by_pairs(groups):
+        far = [swap_with(queries, 2 * d, groups) for d in range(groups // 2 - 1, 0, -1)][::-1]
+        near = swap_with(queries, 1, groups)
     entropy, count, target_sum, cold_rows, cold_target = prepare(
         teacher, candidates, hot_ids, location
     )
@@ -64,8 +83,22 @@
         jnp.broadcast_to(cold_rows.astype(f32)[None], (groups, q_rows, COLD)),
         jnp.broadcast_to(cold_target[None], (groups, q_rows, COLD)),
     ]
+    message = jnp.concatenate(parts, axis=2)
+    if by_pairs(groups):
+        message, far = lax.optimization_barrier((message, far))
+        passed = swap_with(jnp.stack(far), 1, groups)
+        upper = me % 2 == 1
+        mine_all = [queries, *far]
+        others = [near, *[passed[d] for d in range(len(far))]]
+        lower_half = [jnp.where(upper, o, m) for m, o in zip(mine_all, others)]
+        upper_half = [jnp.where(upper, m, o) for m, o in zip(mine_all, others)]
+        lower_half = in_order(lower_half, me // 2)
+        upper_half = in_order(upper_half, me // 2)
+        all_queries = jnp.concatenate([b for pair in zip(lower_half, upper_half) for b in pair])
+    else:
+        all_queries = lax.all_gather(queries, "corpus", axis=0, tiled=True)
     message = lax.all_to_all(
-        jnp.concatenate(parts, axis=2), "corpus", split_axis=0, concat_axis=0, tiled=True
+        message, "corpus", split_axis=0, concat_axis=0, tiled=True
     ).reshape(groups * q_rows, -1)
     count = message[:, :hot_each]
     target_sum = message[:, hot_each : 2 * hot_each]

time: 138 us -> 120 us (0.87)
  between operations: 14.4 us -> 1.07 us
  waiting for transfers between devices: 49.6 us -> 37.9 us
  starting transfers between devices: 14.1 us -> 20.9 us
  matrix products: 24.8 us -> 22.6 us
    all_gather x1 -> x0, waiting for transfers between devices: 15.9 us -> none  [shards(): all_queries = lax.all_gather(queries, 'corpus', axis=0, tiled=True)]
    ppermute x0 -> x5, starting transfers between devices: none -> 9.41 us  [swap_with(): lax.ppermute(block, 'corpus', [(i, i ^ distance) for i in range(groups)])]
    ppermute x0 -> x5, waiting for transfers between devices: none -> 8.96 us  [swap_with(): lax.ppermute(block, 'corpus', [(i, i ^ distance) for i in range(groups)])]
    all_to_all x1, waiting for transfers between devices: 9.25 us -> 5.86 us  [shards(): lax.all_to_all(message, 'corpus', split_axis=0, concat_axis=0, tiled=True)]
    unnamed x0 -> x7, other arithmetic: none -> 2.83 us
    all_to_all x1, starting transfers between devices: 7.25 us -> 4.94 us  [shards(): lax.all_to_all(message, 'corpus', split_axis=0, concat_axis=0, tiled=True)]
    dot_general x1, matrix products: 8.68 us -> 7.1 us  [shards(): lax.dot_general(all_queries, slab, across, preferred_element_type=f32)]
  transfers between devices with their start and end apart: 6 -> 10, of which waited for: 6 -> 6; matrix products, arithmetic and copies ran while one was open for 18% -> 20% of each run, Pallas kernels for 0% -> 0%
where the time goes in v3:
time: 120 us; the launch traced here: 119 us
  waiting for transfers between devices  37.9 us (32%)
  matrix products  22.6 us (19%)
  starting transfers between devices  20.9 us (17%)
  other arithmetic  20.6 us (17%)
  blocking collectives  11.8 us (10%)
  local copies, waits for them, and re-layouts  3.82 us (3%)
    ppermute x3, waiting for transfers between devices, shards(): lax.ppermute(outgoing, 'rep', [(r, (r + step) % reps) for r in range(reps)])  15.5 us
    all_to_all x1, blocking collectives, shards(): lax.all_to_all(jnp.broadcast_to(stats[None], (groups, *stats.shape)), 'co...  11.8 us
    ppermute x5, starting transfers between devices, swap_with(): lax.ppermute(block, 'corpus', [(i, i ^ distance) for i in range(groups)])  9.41 us
    ppermute x5, waiting for transfers between devices, swap_with(): lax.ppermute(block, 'corpus', [(i, i ^ distance) for i in range(groups)])  8.96 us
    all_to_all x1, waiting for transfers between devices, shards(): lax.all_to_all(query_part.astype(jnp.bfloat16).reshape(groups, q_rows, fe...  7.51 us
    dot_general x1, matrix products, shards(): lax.dot_general(all_queries, slab, across, preferred_element_type=f32)  7.1 us
    all_to_all x1, waiting for transfers between devices, shards(): lax.all_to_all(message, 'corpus', split_axis=0, concat_axis=0, tiled=True)  5.86 us
    dot_general x1, matrix products, shards(): weight = jnp.dot(hot_weight, place, preferred_element_type=f32)  5.5 us
  transfers between devices with their start and end apart: 10, of which 6 were waited for; matrix products, arithmetic and copies ran while one was open for 20% of the time, Pallas kernels for 0%

profile of v3, /device:TPU:0, one launch (start us, length us, event | category | flops | bytes accessed | tf_op | source)
XLA Modules:
  0.0 118.7 jit_solution(17985395229764447033)
XLA Ops:
  0.6 0.0 copy-start
  0.6 0.0 copy-start.3
  0.7 3.1 %collective-permute-start = (bf16[128,768]{1,0:T(8,128)(2,1)}, bf16[128,768]{1,0:T(8,128)(2,1)S(1)}, u32[]{:S(2)}, u32[]{:S(2)}) collective-permute-start(bf16[128,768]{1,0:T(8,128)(2,1)} %param.6), channel_id=1, source_target_pairs={{0,8},{4,12},{8,0},{12,4},{16,24},{20,28},{24,16},{28,20},{1,9},{5... | collective-permute-start | bytes 589832 | tf_op jit(solution)/shard_map/ppermute | solution.py:61
  3.7 2.6 %collective-permute-start.1 = (bf16[128,768]{1,0:T(8,128)(2,1)}, bf16[128,768]{1,0:T(8,128)(2,1)S(1)}, u32[]{:S(2)}, u32[]{:S(2)}) collective-permute-start(bf16[128,768]{1,0:T(8,128)(2,1)} %param.6), channel_id=1, source_target_pairs={{0,16},{4,20},{8,24},{12,28},{16,0},{20,4},{24,8},{28,12},{1,17},{... | collective-permute-start | bytes 589832 | tf_op jit(solution)/shard_map/ppermute | solution.py:61
  6.3 0.0 collective-permute-start.2
  6.3 1.7 %collective-permute-start.4 = (bf16[128,768]{1,0:T(8,128)(2,1)}, bf16[128,768]{1,0:T(8,128)(2,1)}, u32[]{:S(2)}, u32[]{:S(2)}) collective-permute-start(bf16[128,768]{1,0:T(8,128)(2,1)} %param.6), channel_id=1, source_target_pairs={{0,4},{4,0},{8,12},{12,8},{16,20},{20,16},{24,28},{28,24},{1,5},{5... | collective-permute-start | bytes 589832 | tf_op jit(solution)/shard_map/ppermute | solution.py:61
  8.0 0.8 copy.34
  8.9 4.4 %compare_reduce_fusion = pred[128,64]{1,0:T(8,128)(4,1)S(1)} fusion(s32[256]{0:T(256)} %param.10, s32[128,64]{1,0:T(8,128)S(1)} %copy.34), kind=kLoop, calls=%fused_computation | loop fusion | flops 4186112 | bytes 41984 | tf_op jit(solution)/shard_map/reduce_or | solution.py:35
  13.3 0.1 copy.38
  13.4 0.2 fusion.3
  13.6 0.8 select_reduce_fusion.9
  14.4 0.8 reduce_max.36
  15.1 0.8 exponential_reduce_fusion
  15.9 0.8 subtract_exponential_fusion
  16.8 0.1 copy.36
  16.9 0.1 copy.39
  17.0 0.1 broadcast_in_dim_reshape.4
  17.1 0.8 fusion.16
  17.9 0.5 fusion.8
  18.4 0.1 fusion.7
  18.5 0.1 convert_element_type.85
  18.6 3.0 %fusion = (f32[128,256]{1,0:T(8,128)S(1)}, f32[128,256]{1,0:T(8,128)S(1)}) fusion(s32[256]{0:T(256)S(1)} %copy-done.3, s32[128,64]{1,0:T(8,128)S(1)} %copy.34, f32[128,64]{1,0:T(8,128)S(1)} %copy.36), kind=kLoop, calls=%fused_computation.3 | loop fusion | flops 10420224 | bytes 328704 | tf_op jit(solution)/shard_map/reduce_sum | solution.py:33
  21.6 0.1 copy.35
  21.7 0.1 copy.37
  21.8 0.1 and_select_fusion.1
  21.9 0.7 pad_maximum_fusion.1
  22.6 0.1 and_select_fusion
  22.7 0.0 collective-permute-done
  22.7 4.9 %all-to-all-start = ((f32[8,128,80]{1,2,0:T(8,128)}), f32[8,128,80]{1,2,0:T(8,128)S(1)}, u32[]{:S(2)}, u32[]{:S(2)}) async-start(f32[8,128,80]{1,2,0:T(8,128)} %pad_maximum_fusion.1), calls=%async_computation | async-start | bytes 655360 | tf_op jit(solution)/shard_map/all_to_all | solution.py:100
  27.7 0.2 fusion.25
  27.9 0.2 fusion.29
  28.1 0.9 pad_maximum_fusion
  28.9 2.0 %collective-permute-start.3 = (bf16[3,128,768]{2,1,0:T(8,128)(2,1)}, bf16[3,128,768]{2,1,0:T(8,128)(2,1)S(1)}, u32[]{:S(2)}, u32[]{:S(2)}) collective-permute-start(bf16[3,128,768]{2,1,0:T(8,128)(2,1)} %pad_maximum_fusion), channel_id=1, source_target_pairs={{0,4},{4,0},{8,12},{12,8},{16,20},{20,16},{24,28},{28,24},{1,5},{5... | collective-permute-start | bytes 1769480 | tf_op jit(solution)/shard_map/ppermute | solution.py:61
  31.0 5.9 %all-to-all-done = f32[8,128,80]{1,2,0:T(8,128)S(1)} async-done(((f32[8,128,80]{1,2,0:T(8,128)}), f32[8,128,80]{1,2,0:T(8,128)S(1)}, u32[]{:S(2)}, u32[]{:S(2)}) %all-to-all-start) | async-done | bytes 327712 | tf_op jit(solution)/shard_map/all_to_all | solution.py:100
  36.9 9.0 %collective-permute-done.3 = bf16[3,128,768]{2,1,0:T(8,128)(2,1)S(1)} collective-permute-done((bf16[3,128,768]{2,1,0:T(8,128)(2,1)}, bf16[3,128,768]{2,1,0:T(8,128)(2,1)S(1)}, u32[]{:S(2)}, u32[]{:S(2)}) %collective-permute-start.3) | collective-permute-done | bytes 589856 | tf_op jit(solution)/shard_map/ppermute | solution.py:61
  45.9 1.2 select_dynamic-update-slice_fusion.7
  47.0 1.2 select_dynamic-update-slice_fusion.6
  48.2 0.1 select_dynamic-update-slice_fusion.5
  48.3 0.1 select_dynamic-update-slice_fusion.4
  48.4 0.1 select_dynamic-update-slice_fusion.3
  48.5 0.1 select_dynamic-update-slice_fusion.2
  48.6 0.1 select_dynamic-update-slice_fusion.1
  48.8 0.1 select_dynamic-update-slice_fusion
  48.9 7.1 %select_reduce_fusion = (f32[1024]{0:T(1024)S(1)}, f32[1024]{0:T(1024)S(1)}, f32[1024]{0:T(1024)S(1)}, f32[1024]{0:T(1024)S(1)}, f32[1024]{0:T(1024)S(1)}, /*ind...) fusion(s32[1024]{0:T(1024)S(1)} %bitcast.147, s32[1024]{0:T(1024)S(1)} %bitcast.145, s32[1024]{0:T(1024)S(1)} %bitcast.143, ...), kind=kOutput, calls=%fused_computation.6 | convolution fusion | flops 1636818944 | bytes 3211264 | tf_op jit(solution)/shard_map/dot_general | solution.py:116
  56.0 0.1 stack.57
  56.1 2.3 %fusion.39 = (f32[1024]{0:T(1024)S(1)}, f32[1024,32]{0,1:T(8,128)S(1)}) fusion(bf16[1024,768]{1,0:T(8,128)(2,1)} %copy-done.1, bf16[1024,768]{1,0:T(8,128)(2,1)S(1)} %copy-done, s32[32]{0:T(128)S(1)} %convert_subtract_fusion), kind=kOutput, calls=%fused_computation.151 | convolution fusion | flops 100785152 | bytes 3281024 | tf_op jit(solution)/shard_map/dot_general | solution.py:115
  58.4 0.1 multiply_reduce_fusion.1
  58.6 11.8 %all_to_all.15 = f32[8,3,1024]{2,1,0:T(4,128)S(1)} all-to-all(f32[8,3,1024]{2,1,0:T(4,128)S(1)} %broadcast_in_dim.208), channel_id=1, replica_groups=mesh['corpus'=8,'rep'=4] {'corpus'}, dimensions={0} | all-to-all | bytes 196608 | tf_op jit(solution)/shard_map/all_to_all | solution.py:136
  70.3 0.1 slice_reduce_fusion
  70.6 5.5 %add_convert_fusion = bf16[1024,1024]{0,1:T(8,128)(2,1)S(1)} fusion(f32[1024]{0:T(1024)S(1)} %bitcast.150, f32[1024]{0:T(1024)S(1)} %bitcast.151, f32[1024]{0:T(1024)S(1)} %bitcast.152, f32[1024]{0:T(1024)S(1)} %bitcast.153, f32[1024]{0:T(1024)S(1)} %bitcast.154, f32[1024]{0:T(1024)S(1)} %bitcast.155, f32[1024]{0:T(1024)S(1)} %bitcast.156, ...), kind=kOutput, calls=%fused_computation.5 | convolution fusion | flops 93519872 | bytes 2560512 | tf_op jit(solution)/shard_map/dot_general | solution.py:151
  76.1 3.0 %multiply_convert_fusion.1 = bf16[1024,768]{1,0:T(8,128)(2,1)} fusion(bf16[1024,1024]{0,1:T(8,128)(2,1)S(1)} %add_convert_fusion, bf16[1024,768]{1,0:T(8,128)(2,1)S(1)} %copy-done), kind=kOutput, calls=%fused_computation.24 | convolution fusion | flops 1612185600 | bytes 5242880 | tf_op jit(solution)/shard_map/dot_general | solution.py:158
  79.1 3.6 %all-to-all-start.2 = ((bf16[8,128,768]{2,1,0:T(8,128)(2,1)}), bf16[8,128,768]{2,1,0:T(8,128)(2,1)S(1)}, u32[]{:S(2)}, u32[]{:S(2)}) async-start(bf16[8,128,768]{2,1,0:T(8,128)(2,1)} %bitcast.125), calls=%async_computation.2 | async-start | bytes 3145728 | tf_op jit(solution)/shard_map/all_to_all | solution.py:159
  82.8 3.8 %multiply_convert_fusion = bf16[1024,768]{1,0:T(8,128)(2,1)S(1)} fusion(bf16[1024,1024]{0,1:T(8,128)(2,1)} %copy-done.4, bf16[1024,768]{1,0:T(8,128)(2,1)} %copy-done.1), kind=kOutput, calls=%fused_computation.22 | convolution fusion | flops 1612185600 | bytes 5242880 | tf_op jit(solution)/shard_map/dot_general | solution.py:163
  86.6 1.1 copy-done.2
  87.8 1.0 dynamic-slice_bitcast_fusion.2
  88.7 1.5 %collective-permute-start.6 = (bf16[256,768]{1,0:T(8,128)(2,1)}, bf16[256,768]{1,0:T(8,128)(2,1)}, u32[]{:S(2)}, u32[]{:S(2)}) collective-permute-start(bf16[256,768]{1,0:T(8,128)(2,1)} %get-tuple-element.45), channel_id=1, source_target_pairs={{0,2},{1,3},{2,0},{3,1},{4,6},{5,7},{6,4},{7,5},{8,10},{9,11},{10,... | collective-permute-start | bytes 1179656 | tf_op jit(solution)/shard_map/ppermute | solution.py:171
  90.3 1.4 %collective-permute-start.7 = (bf16[256,768]{1,0:T(8,128)(2,1)S(1)}, bf16[256,768]{1,0:T(8,128)(2,1)}, u32[]{:S(2)}, u32[]{:S(2)}) collective-permute-start(bf16[256,768]{1,0:T(8,128)(2,1)S(1)} %get-tuple-element.44), channel_id=1, source_target_pairs={{0,3},{1,0},{2,1},{3,2},{4,7},{5,4},{6,5},{7,6},{8,11},{9,8},{10,9... | collective-permute-start | bytes 1179656 | tf_op jit(solution)/shard_map/ppermute | solution.py:171
  91.7 0.6 dynamic-slice_add_fusion
  92.3 7.6 %collective-permute-done.5 = bf16[256,768]{1,0:T(8,128)(2,1)} collective-permute-done((bf16[256,768]{1,0:T(8,128)(2,1)}, bf16[256,768]{1,0:T(8,128)(2,1)}, u32[]{:S(2)}, u32[]{:S(2)}) %collective-permute-start.5) | collective-permute-done | bytes 393248 | tf_op jit(solution)/shard_map/ppermute | solution.py:171
  99.9 1.1 collective-permute-done.6
  101.0 6.8 %collective-permute-done.7 = bf16[256,768]{1,0:T(8,128)(2,1)} collective-permute-done((bf16[256,768]{1,0:T(8,128)(2,1)S(1)}, bf16[256,768]{1,0:T(8,128)(2,1)}, u32[]{:S(2)}, u32[]{:S(2)}) %collective-permute-start.7) | collective-permute-done | bytes 393248 | tf_op jit(solution)/shard_map/ppermute | solution.py:171
  107.8 2.4 %fusion.5 = f32[256,768]{1,0:T(8,128)} fusion(bf16[256,768]{1,0:T(8,128)(2,1)} %collective-permute-done.7, bf16[256,768]{1,0:T(8,128)(2,1)} %collective-permute-done.6, bf16[256,768]{1,0:T(8,128)(2,1)} %collective-permute-done.5, bf16[4,256,768]{2,1,0:T(8,128)(2,1)} %bitcast.127, s32[]{:T(128)S(6)} %select_n.366), kind=kLoop, calls=%fused_computation.32 | loop fusion | flops 1376256 | bytes 2359300 | tf_op jit(solution)/shard_map/add | solution.py:172
  110.2 7.5 %all-to-all-done.2 = bf16[8,128,768]{2,1,0:T(8,128)(2,1)S(1)} async-done(((bf16[8,128,768]{2,1,0:T(8,128)(2,1)}), bf16[8,128,768]{2,1,0:T(8,128)(2,1)S(1)}, u32[]{:S(2)}, u32[]{:S(2)}) %all-to-all-start.2) | async-done | bytes 1572896 | tf_op jit(solution)/shard_map/all_to_all | solution.py:159
  117.7 1.0 convert_reduce_fusion
  (33 shorter events, 0.4 us)
Async XLA Ops:
  0.6 48.2 %copy-start = (bf16[1024,768]{1,0:T(8,128)(2,1)S(1)}, bf16[1024,768]{1,0:T(8,128)(2,1)}, u32[]{:S(2)}) copy-start(bf16[1024,768]{1,0:T(8,128)(2,1)} %param.8) | copy-start | bytes 4718596
  0.6 18.0 %copy-start.3 = (s32[256]{0:T(256)S(1)}, s32[256]{0:T(256)}, u32[]{:S(2)}) copy-start(s32[256]{0:T(256)} %param.10) | copy-start | bytes 3076
  0.7 22.1 %collective-permute-start = (bf16[128,768]{1,0:T(8,128)(2,1)}, bf16[128,768]{1,0:T(8,128)(2,1)S(1)}, u32[]{:S(2)}, u32[]{:S(2)}) collective-permute-start(bf16[128,768]{1,0:T(8,128)(2,1)} %param.6), channel_id=1, source_target_pairs={{0,8},{4,12},{8,0},{12,4},{16,24},{20,28},{24,16},{28,20},{1,9},{5... | collective-permute-start | bytes 589832 | tf_op jit(solution)/shard_map/ppermute | solution.py:61
  3.7 19.0 %collective-permute-start.1 = (bf16[128,768]{1,0:T(8,128)(2,1)}, bf16[128,768]{1,0:T(8,128)(2,1)S(1)}, u32[]{:S(2)}, u32[]{:S(2)}) collective-permute-start(bf16[128,768]{1,0:T(8,128)(2,1)} %param.6), channel_id=1, source_target_pairs={{0,16},{4,20},{8,24},{12,28},{16,0},{20,4},{24,8},{28,12},{1,17},{... | collective-permute-start | bytes 589832 | tf_op jit(solution)/shard_map/ppermute | solution.py:61
  6.3 16.4 %collective-permute-start.2 = (bf16[128,768]{1,0:T(8,128)(2,1)}, bf16[128,768]{1,0:T(8,128)(2,1)S(1)}, u32[]{:S(2)}, u32[]{:S(2)}) collective-permute-start(bf16[128,768]{1,0:T(8,128)(2,1)} %param.6), channel_id=1, source_target_pairs={{0,24},{4,28},{8,16},{12,20},{16,8},{20,12},{24,0},{28,4},{1,25},{... | collective-permute-start | bytes 589832 | tf_op jit(solution)/shard_map/ppermute | solution.py:61
  6.3 30.6 %collective-permute-start.4 = (bf16[128,768]{1,0:T(8,128)(2,1)}, bf16[128,768]{1,0:T(8,128)(2,1)}, u32[]{:S(2)}, u32[]{:S(2)}) collective-permute-start(bf16[128,768]{1,0:T(8,128)(2,1)} %param.6), channel_id=1, source_target_pairs={{0,4},{4,0},{8,12},{12,8},{16,20},{20,16},{24,28},{28,24},{1,5},{5... | collective-permute-start | bytes 589832 | tf_op jit(solution)/shard_map/ppermute | solution.py:61
  22.7 14.1 %all-to-all-start = ((f32[8,128,80]{1,2,0:T(8,128)}), f32[8,128,80]{1,2,0:T(8,128)S(1)}, u32[]{:S(2)}, u32[]{:S(2)}) async-start(f32[8,128,80]{1,2,0:T(8,128)} %pad_maximum_fusion.1), calls=%async_computation | async-start | bytes 655360 | tf_op jit(solution)/shard_map/all_to_all | solution.py:100
  28.9 16.9 %collective-permute-start.3 = (bf16[3,128,768]{2,1,0:T(8,128)(2,1)}, bf16[3,128,768]{2,1,0:T(8,128)(2,1)S(1)}, u32[]{:S(2)}, u32[]{:S(2)}) collective-permute-start(bf16[3,128,768]{2,1,0:T(8,128)(2,1)} %pad_maximum_fusion), channel_id=1, source_target_pairs={{0,4},{4,0},{8,12},{12,8},{16,20},{20,16},{24,28},{28,24},{1,5},{5... | collective-permute-start | bytes 1769480 | tf_op jit(solution)/shard_map/ppermute | solution.py:61
  48.9 7.1 %copy-start.1 = (bf16[1024,768]{1,0:T(8,128)(2,1)}, bf16[1024,768]{1,0:T(8,128)(2,1)S(1)}, u32[]{:S(2)}) copy-start(bf16[1024,768]{1,0:T(8,128)(2,1)S(1)} %select_dynamic-update-slice_fusion) | copy-start | bytes 4718596
  76.1 3.1 %copy-start.4 = (bf16[1024,1024]{0,1:T(8,128)(2,1)}, bf16[1024,1024]{0,1:T(8,128)(2,1)S(1)}, u32[]{:S(2)}) copy-start(bf16[1024,1024]{0,1:T(8,128)(2,1)S(1)} %add_convert_fusion) | copy-start | bytes 6291460
  79.1 38.6 %all-to-all-start.2 = ((bf16[8,128,768]{2,1,0:T(8,128)(2,1)}), bf16[8,128,768]{2,1,0:T(8,128)(2,1)S(1)}, u32[]{:S(2)}, u32[]{:S(2)}) async-start(bf16[8,128,768]{2,1,0:T(8,128)(2,1)} %bitcast.125), calls=%async_computation.2 | async-start | bytes 3145728 | tf_op jit(solution)/shard_map/all_to_all | solution.py:159
  86.6 1.2 copy-start.2
  88.7 11.2 %collective-permute-start.5 = (bf16[256,768]{1,0:T(8,128)(2,1)}, bf16[256,768]{1,0:T(8,128)(2,1)}, u32[]{:S(2)}, u32[]{:S(2)}) collective-permute-start(bf16[256,768]{1,0:T(8,128)(2,1)} %get-tuple-element.43), channel_id=1, source_target_pairs={{0,1},{1,2},{2,3},{3,0},{4,5},{5,6},{6,7},{7,4},{8,9},{9,10},{10,1... | collective-permute-start | bytes 1179656 | tf_op jit(solution)/shard_map/ppermute | solution.py:171
  88.7 12.3 %collective-permute-start.6 = (bf16[256,768]{1,0:T(8,128)(2,1)}, bf16[256,768]{1,0:T(8,128)(2,1)}, u32[]{:S(2)}, u32[]{:S(2)}) collective-permute-start(bf16[256,768]{1,0:T(8,128)(2,1)} %get-tuple-element.45), channel_id=1, source_target_pairs={{0,2},{1,3},{2,0},{3,1},{4,6},{5,7},{6,4},{7,5},{8,10},{9,11},{10,... | collective-permute-start | bytes 1179656 | tf_op jit(solution)/shard_map/ppermute | solution.py:171
  90.3 17.5 %collective-permute-start.7 = (bf16[256,768]{1,0:T(8,128)(2,1)S(1)}, bf16[256,768]{1,0:T(8,128)(2,1)}, u32[]{:S(2)}, u32[]{:S(2)}) collective-permute-start(bf16[256,768]{1,0:T(8,128)(2,1)S(1)} %get-tuple-element.44), channel_id=1, source_target_pairs={{0,3},{1,0},{2,1},{3,2},{4,7},{5,4},{6,5},{7,6},{8,11},{9,8},{10,9... | collective-permute-start | bytes 1179656 | tf_op jit(solution)/shard_map/ppermute | solution.py:171

commit v4 on v3

--- a/solution.py
+++ b/solution.py
@@ -156,10 +156,33 @@
     weight = weight.astype(jnp.bfloat16)
 
     query_part = scale * jnp.dot(weight, slab, preferred_element_type=f32)
-    query_parts = lax.all_to_all(
-        query_part.astype(jnp.bfloat16).reshape(groups, q_rows, feat_dim),
-        "corpus", split_axis=0, concat_axis=0, tiled=True,
-    )
+    if by_pairs(groups):
+        query_part = query_part.reshape(groups // 2, 2, q_rows, feat_dim)
+        give, keep = query_part[:, 0], query_part[:, 1]
+        upper = me % 2 == 1
+        give, keep = jnp.where(upper, give, keep), jnp.where(upper, keep, give)
+        give = give.astype(jnp.bfloat16)
+        query_grad = None
+        halfway = []
+        for d in range(groups // 2 - 1, -1, -1):
+            target = (me // 2) ^ d
+            block = lax.dynamic_index_in_dim(give, target, 0, keepdims=False)
+            halfway.append((d, target, swap_with(block, 1, groups)))
+        far_parts = []
+        for d, target, arrived in halfway:
+            both = lax.dynamic_index_in_dim(keep, target, 0, keepdims=False) + arrived.astype(f32)
+            if d:
+                far_parts.append(swap_with(both.astype(jnp.bfloat16), 2 * d, groups))
+            else:
+                query_grad = both
+        for part in far_parts:
+            query_grad = query_grad + part.astype(f32)
+    else:
+        query_parts = lax.all_to_all(
+            query_part.astype(jnp.bfloat16).reshape(groups, q_rows, feat_dim),
+            "corpus", split_axis=0, concat_axis=0, tiled=True,
+        )
+        query_grad = jnp.sum(query_parts.astype(f32), axis=0)
     slab_part = scale * lax.dot_general(
         weight, all_queries, (((0,), (0,)), ((), ())), preferred_element_type=f32
     )
@@ -170,7 +193,6 @@
         outgoing = lax.dynamic_index_in_dim(slab_part, (rep + step) % reps, 0, keepdims=False)
         arrived = lax.ppermute(outgoing, "rep", [(r, (r + step) % reps) for r in range(reps)])
         slab_grad = slab_grad + arrived.astype(f32)
-    query_grad = jnp.sum(query_parts.astype(f32), axis=0)
     return (loss_rows, query_grad, slab_grad)
 
 

time: 120 us -> 119 us (level)
  blocking collectives: 11.8 us -> 0 us
  waiting for transfers between devices: 37.9 us -> 47.6 us
  starting transfers between devices: 20.9 us -> 28.1 us
  matrix products: 22.6 us -> 19.4 us
  local copies, waits for them, and re-layouts: 3.82 us -> 2.53 us
    ppermute x5 -> x12, waiting for transfers between devices: 8.96 us -> 34.4 us  [swap_with(): lax.ppermute(block, 'corpus', [(i, i ^ distance) for i in range(groups)])]
    ppermute x3, waiting for transfers between devices: 15.5 us -> 0.01 us  [shards(): lax.ppermute(outgoing, 'rep', [(r, (r + step) % reps) for r in range(reps)])]
    all_to_all x1 -> x0, blocking collectives: 11.8 us -> none  [shards(): lax.all_to_all(jnp.broadcast_to(stats[None], (groups, *stats.shape)), 'co...]
    ppermute x5 -> x12, starting transfers between devices: 9.41 us -> 15.5 us  [swap_with(): lax.ppermute(block, 'corpus', [(i, i ^ distance) for i in range(groups)])]
    dot_general x1, matrix products: 3.83 us -> 1.8 us  [shards(): lax.dot_general(weight, all_queries, (((0,), (0,)), ((), ())), preferred_...]
    add x1, other arithmetic: 2.41 us -> 1.06 us  [shards(): slab_grad = slab_grad + arrived.astype(f32)]
  transfers between devices with their start and end apart: 10 -> 17, of which waited for: 6 -> 9; matrix products, arithmetic and copies ran while one was open for 20% -> 15% of each run, Pallas kernels for 0% -> 0%
where the time goes in v4:
time: 119 us; the launch traced here: 118 us
  waiting for transfers between devices  47.6 us (40%)
  starting transfers between devices  28.1 us (24%)
  other arithmetic  19.6 us (16%)
  matrix products  19.4 us (16%)
  local copies, waits for them, and re-layouts  2.53 us (2%)
    ppermute x12, waiting for transfers between devices, swap_with(): lax.ppermute(block, 'corpus', [(i, i ^ distance) for i in range(groups)])  34.4 us
    ppermute x12, starting transfers between devices, swap_with(): lax.ppermute(block, 'corpus', [(i, i ^ distance) for i in range(groups)])  15.5 us
    all_to_all x1, waiting for transfers between devices, shards(): lax.all_to_all(jnp.broadcast_to(stats[None], (groups, *stats.shape)), 'co...  7.34 us
    dot_general x1, matrix products, shards(): lax.dot_general(all_queries, slab, across, preferred_element_type=f32)  7.1 us
    all_to_all x1, waiting for transfers between devices, shards(): lax.all_to_all(message, 'corpus', split_axis=0, concat_axis=0, tiled=True)  5.86 us
    dot_general x1, matrix products, shards(): weight = jnp.dot(hot_weight, place, preferred_element_type=f32)  5.5 us
    all_to_all x1, starting transfers between devices, shards(): lax.all_to_all(message, 'corpus', split_axis=0, concat_axis=0, tiled=True)  4.94 us
    all_to_all x1, starting transfers between devices, shards(): lax.all_to_all(jnp.broadcast_to(stats[None], (groups, *stats.shape)), 'co...  4.64 us
  transfers between devices with their start and end apart: 17, of which 9 were waited for; matrix products, arithmetic and copies ran while one was open for 15% of the time, Pallas kernels for 0%

profile of v4, /device:TPU:0, one launch (start us, length us, event | category | flops | bytes accessed | tf_op | source)
XLA Modules:
  0.0 118.3 jit_solution(16529383408125034682)
XLA Ops:
  0.7 3.1 %collective-permute-start = (bf16[128,768]{1,0:T(8,128)(2,1)}, bf16[128,768]{1,0:T(8,128)(2,1)S(1)}, u32[]{:S(2)}, u32[]{:S(2)}) collective-permute-start(bf16[128,768]{1,0:T(8,128)(2,1)} %param.6), channel_id=1, source_target_pairs={{0,8},{4,12},{8,0},{12,4},{16,24},{20,28},{24,16},{28,20},{1,9},{5... | collective-permute-start | bytes 589832 | tf_op jit(solution)/shard_map/ppermute | solution.py:61
  3.7 2.6 %collective-permute-start.1 = (bf16[128,768]{1,0:T(8,128)(2,1)}, bf16[128,768]{1,0:T(8,128)(2,1)S(1)}, u32[]{:S(2)}, u32[]{:S(2)}) collective-permute-start(bf16[128,768]{1,0:T(8,128)(2,1)} %param.6), channel_id=1, source_target_pairs={{0,16},{4,20},{8,24},{12,28},{16,0},{20,4},{24,8},{28,12},{1,17},{... | collective-permute-start | bytes 589832 | tf_op jit(solution)/shard_map/ppermute | solution.py:61
  6.3 1.7 %collective-permute-start.4 = (bf16[128,768]{1,0:T(8,128)(2,1)}, bf16[128,768]{1,0:T(8,128)(2,1)}, u32[]{:S(2)}, u32[]{:S(2)}) collective-permute-start(bf16[128,768]{1,0:T(8,128)(2,1)} %param.6), channel_id=1, source_target_pairs={{0,4},{4,0},{8,12},{12,8},{16,20},{20,16},{24,28},{28,24},{1,5},{5... | collective-permute-start | bytes 589832 | tf_op jit(solution)/shard_map/ppermute | solution.py:61
  8.0 0.8 copy.34
  8.9 4.4 %compare_reduce_fusion = pred[128,64]{1,0:T(8,128)(4,1)S(1)} fusion(s32[256]{0:T(256)} %param.10, s32[128,64]{1,0:T(8,128)S(1)} %copy.34), kind=kLoop, calls=%fused_computation | loop fusion | flops 4186112 | bytes 41984 | tf_op jit(solution)/shard_map/reduce_or | solution.py:35
  13.4 0.2 fusion.3
  13.6 0.8 select_reduce_fusion.9
  14.4 0.8 reduce_max.36
  15.1 0.8 exponential_reduce_fusion
  15.9 0.8 subtract_exponential_fusion
  16.8 0.1 copy.36
  16.9 0.1 copy.39
  17.0 0.1 broadcast_in_dim_reshape.4
  17.1 0.8 fusion.22
  17.9 0.5 fusion.8
  18.4 0.1 fusion.7
  18.6 3.0 %fusion = (f32[128,256]{1,0:T(8,128)S(1)}, f32[128,256]{1,0:T(8,128)S(1)}) fusion(s32[256]{0:T(256)S(1)} %copy-done.3, s32[128,64]{1,0:T(8,128)S(1)} %copy.34, f32[128,64]{1,0:T(8,128)S(1)} %copy.36), kind=kLoop, calls=%fused_computation.3 | loop fusion | flops 10420224 | bytes 328704 | tf_op jit(solution)/shard_map/reduce_sum | solution.py:33
  21.6 0.1 copy.35
  21.7 0.1 copy.37
  21.9 0.7 pad_maximum_fusion.1
  22.7 4.9 %all-to-all-start = ((f32[8,128,80]{1,2,0:T(8,128)}), f32[8,128,80]{1,2,0:T(8,128)S(1)}, u32[]{:S(2)}, u32[]{:S(2)}) async-start(f32[8,128,80]{1,2,0:T(8,128)} %pad_maximum_fusion.1), calls=%async_computation | async-start | bytes 655360 | tf_op jit(solution)/shard_map/all_to_all | solution.py:100
  27.7 0.2 fusion.31
  27.9 0.2 fusion.35
  28.1 0.9 pad_maximum_fusion
  28.9 2.0 %collective-permute-start.3 = (bf16[3,128,768]{2,1,0:T(8,128)(2,1)}, bf16[3,128,768]{2,1,0:T(8,128)(2,1)S(1)}, u32[]{:S(2)}, u32[]{:S(2)}) collective-permute-start(bf16[3,128,768]{2,1,0:T(8,128)(2,1)} %pad_maximum_fusion), channel_id=1, source_target_pairs={{0,4},{4,0},{8,12},{12,8},{16,20},{20,16},{24,28},{28,24},{1,5},{5... | collective-permute-start | bytes 1769480 | tf_op jit(solution)/shard_map/ppermute | solution.py:61
  31.0 5.9 %all-to-all-done = f32[8,128,80]{1,2,0:T(8,128)S(1)} async-done(((f32[8,128,80]{1,2,0:T(8,128)}), f32[8,128,80]{1,2,0:T(8,128)S(1)}, u32[]{:S(2)}, u32[]{:S(2)}) %all-to-all-start) | async-done | bytes 327712 | tf_op jit(solution)/shard_map/all_to_all | solution.py:100
  36.9 9.0 %collective-permute-done.3 = bf16[3,128,768]{2,1,0:T(8,128)(2,1)S(1)} collective-permute-done((bf16[3,128,768]{2,1,0:T(8,128)(2,1)}, bf16[3,128,768]{2,1,0:T(8,128)(2,1)S(1)}, u32[]{:S(2)}, u32[]{:S(2)}) %collective-permute-start.3) | collective-permute-done | bytes 589856 | tf_op jit(solution)/shard_map/ppermute | solution.py:61
  45.9 1.2 select_dynamic-update-slice_fusion.7
  47.0 1.2 select_dynamic-update-slice_fusion.6
  48.2 0.1 select_dynamic-update-slice_fusion.5
  48.3 0.1 select_dynamic-update-slice_fusion.4
  48.4 0.1 select_dynamic-update-slice_fusion.3
  48.5 0.1 select_dynamic-update-slice_fusion.2
  48.6 0.1 select_dynamic-update-slice_fusion.1
  48.8 0.1 select_dynamic-update-slice_fusion
  48.9 7.1 %select_reduce_fusion = (f32[1024]{0:T(1024)S(1)}, f32[1024]{0:T(1024)S(1)}, f32[1024]{0:T(1024)S(1)}, f32[1024]{0:T(1024)S(1)}, f32[1024]{0:T(1024)S(1)}, /*ind...) fusion(s32[1024]{0:T(1024)S(1)} %bitcast.176, s32[1024]{0:T(1024)S(1)} %bitcast.174, s32[1024]{0:T(1024)S(1)} %bitcast.172, ...), kind=kOutput, calls=%fused_computation.6 | convolution fusion | flops 1636818944 | bytes 3211264 | tf_op jit(solution)/shard_map/dot_general | solution.py:116
  56.1 2.3 %fusion.45 = (f32[1024]{0:T(1024)S(1)}, f32[1024,32]{0,1:T(8,128)S(1)}) fusion(bf16[1024,768]{1,0:T(8,128)(2,1)} %copy-done.1, bf16[1024,768]{1,0:T(8,128)(2,1)S(1)} %copy-done, s32[32]{0:T(128)S(1)} %convert_subtract_fusion), kind=kOutput, calls=%fused_computation.166 | convolution fusion | flops 100785152 | bytes 3281024 | tf_op jit(solution)/shard_map/dot_general | solution.py:115
  58.5 0.7 broadcast_in_dim.208
  59.2 4.6 %all-to-all-start.1 = ((f32[8,3,1024]{2,1,0:T(4,128)}), f32[8,3,1024]{2,1,0:T(4,128)S(1)}, u32[]{:S(2)}, u32[]{:S(2)}) async-start(f32[8,3,1024]{2,1,0:T(4,128)} %broadcast_in_dim.208), calls=%async_computation.1 | async-start | bytes 262144 | tf_op jit(solution)/shard_map/all_to_all | solution.py:136
  63.8 7.3 %all-to-all-done.1 = f32[8,3,1024]{2,1,0:T(4,128)S(1)} async-done(((f32[8,3,1024]{2,1,0:T(4,128)}), f32[8,3,1024]{2,1,0:T(4,128)S(1)}, u32[]{:S(2)}, u32[]{:S(2)}) %all-to-all-start.1) | async-done | bytes 98336 | tf_op jit(solution)/shard_map/all_to_all | solution.py:136
  71.2 0.1 slice_reduce_fusion
  71.4 5.5 %add_convert_fusion = bf16[1024,1024]{0,1:T(8,128)(2,1)S(1)} fusion(f32[1024]{0:T(1024)S(1)} %bitcast.179, f32[1024]{0:T(1024)S(1)} %bitcast.180, f32[1024]{0:T(1024)S(1)} %bitcast.181, f32[1024]{0:T(1024)S(1)} %bitcast.182, f32[1024]{0:T(1024)S(1)} %bitcast.183, f32[1024]{0:T(1024)S(1)} %bitcast.184, f32[1024]{0:T(1024)S(1)} %bitcast.185, ...), kind=kOutput, calls=%fused_computation.5 | convolution fusion | flops 93519872 | bytes 2560512 | tf_op jit(solution)/shard_map/dot_general | solution.py:151
  76.9 1.8 %multiply_convert_fusion = bf16[1024,768]{1,0:T(8,128)(2,1)S(1)} fusion(bf16[1024,1024]{0,1:T(8,128)(2,1)S(1)} %add_convert_fusion, bf16[1024,768]{1,0:T(8,128)(2,1)S(1)} %copy-done.2), kind=kOutput, calls=%fused_computation.22 | convolution fusion | flops 1612185600 | bytes 5242880 | tf_op jit(solution)/shard_map/dot_general | solution.py:186
  78.7 1.9 %convolution_multiply_fusion = f32[1024,768]{1,0:T(8,128)S(1)} fusion(bf16[1024,1024]{0,1:T(8,128)(2,1)S(1)} %add_convert_fusion, bf16[1024,768]{1,0:T(8,128)(2,1)S(1)} %copy-done), kind=kOutput, calls=%fused_computation.23 | convolution fusion | flops 1611399168 | bytes 6815744 | tf_op jit(solution)/shard_map/dot_general | solution.py:158
  80.8 1.6 %collective-permute-start.13 = (bf16[256,768]{1,0:T(8,128)(2,1)S(1)}, bf16[256,768]{1,0:T(8,128)(2,1)S(1)}, u32[]{:S(2)}, u32[]{:S(2)}) collective-permute-start(bf16[256,768]{1,0:T(8,128)(2,1)S(1)} %get-tuple-element.45), channel_id=1, source_target_pairs={{0,2},{1,3},{2,0},{3,1},{4,6},{5,7},{6,4},{7,5},{8,10},{9,11},{10,... | collective-permute-start | bytes 1179656 | tf_op jit(solution)/shard_map/ppermute | solution.py:194
  82.4 1.4 %collective-permute-start.14 = (bf16[256,768]{1,0:T(8,128)(2,1)S(1)}, bf16[256,768]{1,0:T(8,128)(2,1)S(1)}, u32[]{:S(2)}, u32[]{:S(2)}) collective-permute-start(bf16[256,768]{1,0:T(8,128)(2,1)S(1)} %get-tuple-element.44), channel_id=1, source_target_pairs={{0,3},{1,0},{2,1},{3,2},{4,7},{5,4},{6,5},{7,6},{8,11},{9,8},{10,9... | collective-permute-start | bytes 1179656 | tf_op jit(solution)/shard_map/ppermute | solution.py:194
  83.8 0.1 select_convert_fusion
  84.0 0.3 collective-permute-start.10
  84.3 1.8 %collective-permute-start.6 = (bf16[128,768]{1,0:T(8,128)(2,1)S(1)}, bf16[128,768]{1,0:T(8,128)(2,1)S(1)}, u32[]{:S(2)}, u32[]{:S(2)}) collective-permute-start(bf16[128,768]{1,0:T(8,128)(2,1)S(1)} %get-tuple-element.52), channel_id=1, source_target_pairs={{0,4},{4,0},{8,12},{12,8},{16,20},{20,16},{24,28},{28,24},{1,5},{5... | collective-permute-start | bytes 589832 | tf_op jit(solution)/shard_map/ppermute | solution.py:61
  86.1 0.2 slice_select_fusion
  86.3 5.6 %collective-permute-done.10 = bf16[128,768]{1,0:T(8,128)(2,1)S(1)} collective-permute-done((bf16[128,768]{1,0:T(8,128)(2,1)S(1)}, bf16[128,768]{1,0:T(8,128)(2,1)S(1)}, u32[]{:S(2)}, u32[]{:S(2)}) %collective-permute-start.10) | collective-permute-done | bytes 196640 | tf_op jit(solution)/shard_map/ppermute | solution.py:61
  91.9 0.2 collective-permute-start.8
  92.1 0.6 dynamic-slice_add_fusion
  92.7 3.4 %collective-permute-done.6 = bf16[128,768]{1,0:T(8,128)(2,1)S(1)} collective-permute-done((bf16[128,768]{1,0:T(8,128)(2,1)S(1)}, bf16[128,768]{1,0:T(8,128)(2,1)S(1)}, u32[]{:S(2)}, u32[]{:S(2)}) %collective-permute-start.6) | collective-permute-done | bytes 196640 | tf_op jit(solution)/shard_map/ppermute | solution.py:61
  96.1 0.2 collective-permute-start.5
  96.3 4.0 %collective-permute-done.8 = bf16[128,768]{1,0:T(8,128)(2,1)S(1)} collective-permute-done((bf16[128,768]{1,0:T(8,128)(2,1)S(1)}, bf16[128,768]{1,0:T(8,128)(2,1)S(1)}, u32[]{:S(2)}, u32[]{:S(2)}) %collective-permute-start.8) | collective-permute-done | bytes 196640 | tf_op jit(solution)/shard_map/ppermute | solution.py:61
  100.3 0.1 fusion.11
  100.6 1.8 %collective-permute-start.7 = (bf16[128,768]{1,0:T(8,128)(2,1)S(1)}, bf16[128,768]{1,0:T(8,128)(2,1)S(1)}, u32[]{:S(2)}, u32[]{:S(2)}) collective-permute-start(bf16[128,768]{1,0:T(8,128)(2,1)S(1)} %get-tuple-element.46), channel_id=1, source_target_pairs={{0,24},{4,28},{8,16},{12,20},{16,8},{20,12},{24,0},{28,4},{1,25},{... | collective-permute-start | bytes 589832 | tf_op jit(solution)/shard_map/ppermute | solution.py:61
  102.4 1.6 %collective-permute-start.9 = (bf16[128,768]{1,0:T(8,128)(2,1)S(1)}, bf16[128,768]{1,0:T(8,128)(2,1)S(1)}, u32[]{:S(2)}, u32[]{:S(2)}) collective-permute-start(bf16[128,768]{1,0:T(8,128)(2,1)S(1)} %get-tuple-element.48), channel_id=1, source_target_pairs={{0,16},{4,20},{8,24},{12,28},{16,0},{20,4},{24,8},{28,12},{1,17},{... | collective-permute-start | bytes 589832 | tf_op jit(solution)/shard_map/ppermute | solution.py:61
  104.0 1.1 fusion.5
  105.1 1.1 collective-permute-done.11
  106.2 3.7 %collective-permute-done.7 = bf16[128,768]{1,0:T(8,128)(2,1)S(1)} collective-permute-done((bf16[128,768]{1,0:T(8,128)(2,1)S(1)}, bf16[128,768]{1,0:T(8,128)(2,1)S(1)}, u32[]{:S(2)}, u32[]{:S(2)}) %collective-permute-start.7) | collective-permute-done | bytes 196640 | tf_op jit(solution)/shard_map/ppermute | solution.py:61
  109.9 7.5 %collective-permute-done.9 = bf16[128,768]{1,0:T(8,128)(2,1)S(1)} collective-permute-done((bf16[128,768]{1,0:T(8,128)(2,1)S(1)}, bf16[128,768]{1,0:T(8,128)(2,1)S(1)}, u32[]{:S(2)}, u32[]{:S(2)}) %collective-permute-start.9) | collective-permute-done | bytes 196640 | tf_op jit(solution)/shard_map/ppermute | solution.py:61
  117.5 0.9 fusion.14
  (48 shorter events, 1.1 us)
Async XLA Ops:
  0.6 48.2 %copy-start = (bf16[1024,768]{1,0:T(8,128)(2,1)S(1)}, bf16[1024,768]{1,0:T(8,128)(2,1)}, u32[]{:S(2)}) copy-start(bf16[1024,768]{1,0:T(8,128)(2,1)} %param.8) | copy-start | bytes 4718596
  0.6 18.0 %copy-start.3 = (s32[256]{0:T(256)S(1)}, s32[256]{0:T(256)}, u32[]{:S(2)}) copy-start(s32[256]{0:T(256)} %param.10) | copy-start | bytes 3076
  0.7 22.1 %collective-permute-start = (bf16[128,768]{1,0:T(8,128)(2,1)}, bf16[128,768]{1,0:T(8,128)(2,1)S(1)}, u32[]{:S(2)}, u32[]{:S(2)}) collective-permute-start(bf16[128,768]{1,0:T(8,128)(2,1)} %param.6), channel_id=1, source_target_pairs={{0,8},{4,12},{8,0},{12,4},{16,24},{20,28},{24,16},{28,20},{1,9},{5... | collective-permute-start | bytes 589832 | tf_op jit(solution)/shard_map/ppermute | solution.py:61
  3.7 19.0 %collective-permute-start.1 = (bf16[128,768]{1,0:T(8,128)(2,1)}, bf16[128,768]{1,0:T(8,128)(2,1)S(1)}, u32[]{:S(2)}, u32[]{:S(2)}) collective-permute-start(bf16[128,768]{1,0:T(8,128)(2,1)} %param.6), channel_id=1, source_target_pairs={{0,16},{4,20},{8,24},{12,28},{16,0},{20,4},{24,8},{28,12},{1,17},{... | collective-permute-start | bytes 589832 | tf_op jit(solution)/shard_map/ppermute | solution.py:61
  6.3 16.4 %collective-permute-start.2 = (bf16[128,768]{1,0:T(8,128)(2,1)}, bf16[128,768]{1,0:T(8,128)(2,1)S(1)}, u32[]{:S(2)}, u32[]{:S(2)}) collective-permute-start(bf16[128,768]{1,0:T(8,128)(2,1)} %param.6), channel_id=1, source_target_pairs={{0,24},{4,28},{8,16},{12,20},{16,8},{20,12},{24,0},{28,4},{1,25},{... | collective-permute-start | bytes 589832 | tf_op jit(solution)/shard_map/ppermute | solution.py:61
  6.3 30.6 %collective-permute-start.4 = (bf16[128,768]{1,0:T(8,128)(2,1)}, bf16[128,768]{1,0:T(8,128)(2,1)}, u32[]{:S(2)}, u32[]{:S(2)}) collective-permute-start(bf16[128,768]{1,0:T(8,128)(2,1)} %param.6), channel_id=1, source_target_pairs={{0,4},{4,0},{8,12},{12,8},{16,20},{20,16},{24,28},{28,24},{1,5},{5... | collective-permute-start | bytes 589832 | tf_op jit(solution)/shard_map/ppermute | solution.py:61
  22.7 14.1 %all-to-all-start = ((f32[8,128,80]{1,2,0:T(8,128)}), f32[8,128,80]{1,2,0:T(8,128)S(1)}, u32[]{:S(2)}, u32[]{:S(2)}) async-start(f32[8,128,80]{1,2,0:T(8,128)} %pad_maximum_fusion.1), calls=%async_computation | async-start | bytes 655360 | tf_op jit(solution)/shard_map/all_to_all | solution.py:100
  28.9 16.9 %collective-permute-start.3 = (bf16[3,128,768]{2,1,0:T(8,128)(2,1)}, bf16[3,128,768]{2,1,0:T(8,128)(2,1)S(1)}, u32[]{:S(2)}, u32[]{:S(2)}) collective-permute-start(bf16[3,128,768]{2,1,0:T(8,128)(2,1)} %pad_maximum_fusion), channel_id=1, source_target_pairs={{0,4},{4,0},{8,12},{12,8},{16,20},{20,16},{24,28},{28,24},{1,5},{5... | collective-permute-start | bytes 1769480 | tf_op jit(solution)/shard_map/ppermute | solution.py:61
  48.9 7.1 %copy-start.1 = (bf16[1024,768]{1,0:T(8,128)(2,1)}, bf16[1024,768]{1,0:T(8,128)(2,1)S(1)}, u32[]{:S(2)}) copy-start(bf16[1024,768]{1,0:T(8,128)(2,1)S(1)} %select_dynamic-update-slice_fusion) | copy-start | bytes 4718596
  59.2 12.0 %all-to-all-start.1 = ((f32[8,3,1024]{2,1,0:T(4,128)}), f32[8,3,1024]{2,1,0:T(4,128)S(1)}, u32[]{:S(2)}, u32[]{:S(2)}) async-start(f32[8,3,1024]{2,1,0:T(4,128)} %broadcast_in_dim.208), calls=%async_computation.1 | async-start | bytes 262144 | tf_op jit(solution)/shard_map/all_to_all | solution.py:136
  71.4 5.5 %copy-start.2 = (bf16[1024,768]{1,0:T(8,128)(2,1)S(1)}, bf16[1024,768]{1,0:T(8,128)(2,1)}, u32[]{:S(2)}) copy-start(bf16[1024,768]{1,0:T(8,128)(2,1)} %copy-done.1) | copy-start | bytes 4718596
  80.8 19.8 %collective-permute-start.12 = (bf16[256,768]{1,0:T(8,128)(2,1)S(1)}, bf16[256,768]{1,0:T(8,128)(2,1)S(1)}, u32[]{:S(2)}, u32[]{:S(2)}) collective-permute-start(bf16[256,768]{1,0:T(8,128)(2,1)S(1)} %get-tuple-element.43), channel_id=1, source_target_pairs={{0,1},{1,2},{2,3},{3,0},{4,5},{5,6},{6,7},{7,4},{8,9},{9,10},{10,1... | collective-permute-start | bytes 1179656 | tf_op jit(solution)/shard_map/ppermute | solution.py:194
  80.8 21.6 %collective-permute-start.13 = (bf16[256,768]{1,0:T(8,128)(2,1)S(1)}, bf16[256,768]{1,0:T(8,128)(2,1)S(1)}, u32[]{:S(2)}, u32[]{:S(2)}) collective-permute-start(bf16[256,768]{1,0:T(8,128)(2,1)S(1)} %get-tuple-element.45), channel_id=1, source_target_pairs={{0,2},{1,3},{2,0},{3,1},{4,6},{5,7},{6,4},{7,5},{8,10},{9,11},{10,... | collective-permute-start | bytes 1179656 | tf_op jit(solution)/shard_map/ppermute | solution.py:194
  82.4 21.6 %collective-permute-start.14 = (bf16[256,768]{1,0:T(8,128)(2,1)S(1)}, bf16[256,768]{1,0:T(8,128)(2,1)S(1)}, u32[]{:S(2)}, u32[]{:S(2)}) collective-permute-start(bf16[256,768]{1,0:T(8,128)(2,1)S(1)} %get-tuple-element.44), channel_id=1, source_target_pairs={{0,3},{1,0},{2,1},{3,2},{4,7},{5,4},{6,5},{7,6},{8,11},{9,8},{10,9... | collective-permute-start | bytes 1179656 | tf_op jit(solution)/shard_map/ppermute | solution.py:194
  84.0 7.9 %collective-permute-start.10 = (bf16[128,768]{1,0:T(8,128)(2,1)S(1)}, bf16[128,768]{1,0:T(8,128)(2,1)S(1)}, u32[]{:S(2)}, u32[]{:S(2)}) collective-permute-start(bf16[128,768]{1,0:T(8,128)(2,1)S(1)} %get-tuple-element.50), channel_id=1, source_target_pairs={{0,4},{4,0},{8,12},{12,8},{16,20},{20,16},{24,28},{28,24},{1,5},{5... | collective-permute-start | bytes 589832 | tf_op jit(solution)/shard_map/ppermute | solution.py:61
  84.3 11.8 %collective-permute-start.6 = (bf16[128,768]{1,0:T(8,128)(2,1)S(1)}, bf16[128,768]{1,0:T(8,128)(2,1)S(1)}, u32[]{:S(2)}, u32[]{:S(2)}) collective-permute-start(bf16[128,768]{1,0:T(8,128)(2,1)S(1)} %get-tuple-element.52), channel_id=1, source_target_pairs={{0,4},{4,0},{8,12},{12,8},{16,20},{20,16},{24,28},{28,24},{1,5},{5... | collective-permute-start | bytes 589832 | tf_op jit(solution)/shard_map/ppermute | solution.py:61
  91.9 8.4 %collective-permute-start.8 = (bf16[128,768]{1,0:T(8,128)(2,1)S(1)}, bf16[128,768]{1,0:T(8,128)(2,1)S(1)}, u32[]{:S(2)}, u32[]{:S(2)}) collective-permute-start(bf16[128,768]{1,0:T(8,128)(2,1)S(1)} %get-tuple-element.51), channel_id=1, source_target_pairs={{0,4},{4,0},{8,12},{12,8},{16,20},{20,16},{24,28},{28,24},{1,5},{5... | collective-permute-start | bytes 589832 | tf_op jit(solution)/shard_map/ppermute | solution.py:61
  96.1 9.0 %collective-permute-start.5 = (bf16[128,768]{1,0:T(8,128)(2,1)S(1)}, bf16[128,768]{1,0:T(8,128)(2,1)S(1)}, u32[]{:S(2)}, u32[]{:S(2)}) collective-permute-start(bf16[128,768]{1,0:T(8,128)(2,1)S(1)} %get-tuple-element.49), channel_id=1, source_target_pairs={{0,4},{4,0},{8,12},{12,8},{16,20},{20,16},{24,28},{28,24},{1,5},{5... | collective-permute-start | bytes 589832 | tf_op jit(solution)/shard_map/ppermute | solution.py:61
  100.5 5.7 %collective-permute-start.11 = (bf16[128,768]{1,0:T(8,128)(2,1)S(1)}, bf16[128,768]{1,0:T(8,128)(2,1)S(1)}, u32[]{:S(2)}, u32[]{:S(2)}) collective-permute-start(bf16[128,768]{1,0:T(8,128)(2,1)S(1)} %get-tuple-element.47), channel_id=1, source_target_pairs={{0,8},{4,12},{8,0},{12,4},{16,24},{20,28},{24,16},{28,20},{1,9},{5... | collective-permute-start | bytes 589832 | tf_op jit(solution)/shard_map/ppermute | solution.py:61
  100.6 9.4 %collective-permute-start.7 = (bf16[128,768]{1,0:T(8,128)(2,1)S(1)}, bf16[128,768]{1,0:T(8,128)(2,1)S(1)}, u32[]{:S(2)}, u32[]{:S(2)}) collective-permute-start(bf16[128,768]{1,0:T(8,128)(2,1)S(1)} %get-tuple-element.46), channel_id=1, source_target_pairs={{0,24},{4,28},{8,16},{12,20},{16,8},{20,12},{24,0},{28,4},{1,25},{... | collective-permute-start | bytes 589832 | tf_op jit(solution)/shard_map/ppermute | solution.py:61
  102.4 15.1 %collective-permute-start.9 = (bf16[128,768]{1,0:T(8,128)(2,1)S(1)}, bf16[128,768]{1,0:T(8,128)(2,1)S(1)}, u32[]{:S(2)}, u32[]{:S(2)}) collective-permute-start(bf16[128,768]{1,0:T(8,128)(2,1)S(1)} %get-tuple-element.48), channel_id=1, source_target_pairs={{0,16},{4,20},{8,24},{12,28},{16,0},{20,4},{24,8},{28,12},{1,17},{... | collective-permute-start | bytes 589832 | tf_op jit(solution)/shard_map/ppermute | solution.py:61

commit v5 on v4

--- a/solution.py
+++ b/solution.py
@@ -168,6 +168,9 @@
             target = (me // 2) ^ d
             block = lax.dynamic_index_in_dim(give, target, 0, keepdims=False)
             halfway.append((d, target, swap_with(block, 1, groups)))
+        d, target, arrived = halfway[0]
+        weight, arrived = lax.optimization_barrier((weight, arrived))
+        halfway[0] = (d, target, arrived)
         far_parts = []
         for d, target, arrived in halfway:
             both = lax.dynamic_index_in_dim(keep, target, 0, keepdims=False) + arrived.astype(f32)

time: 119 us -> 130 us (1.092)
  other arithmetic: 19.6 us -> 25 us
  matrix products: 19.4 us -> 21.7 us
  starting transfers between devices: 28.1 us -> 29.7 us
  waiting for transfers between devices: 47.6 us -> 49 us
    ppermute x3, waiting for transfers between devices: 0.01 us -> 14.2 us  [shards(): lax.ppermute(outgoing, 'rep', [(r, (r + step) % reps) for r in range(reps)])]
    ppermute x12, waiting for transfers between devices: 34.4 us -> 21.8 us  [swap_with(): lax.ppermute(block, 'corpus', [(i, i ^ distance) for i in range(groups)])]
    unnamed x7, other arithmetic: 2.83 us -> 7.51 us
    ppermute x12, starting transfers between devices: 15.5 us -> 18 us  [swap_with(): lax.ppermute(block, 'corpus', [(i, i ^ distance) for i in range(groups)])]
    dot_general x1, matrix products: 1.8 us -> 3.2 us  [shards(): lax.dot_general(weight, all_queries, (((0,), (0,)), ((), ())), preferred_...]
  transfers between devices with their start and end apart: 17 -> 17, of which waited for: 9 -> 10; matrix products, arithmetic and copies ran while one was open for 15% -> 16% of each run, Pallas kernels for 0% -> 0%
where the time goes in v5:
time: 130 us; the launch traced here: 129 us
  waiting for transfers between devices  49 us (38%)
  starting transfers between devices  29.7 us (23%)
  other arithmetic  25 us (19%)
  matrix products  21.7 us (17%)
  local copies, waits for them, and re-layouts  2.52 us (2%)
    ppermute x12, waiting for transfers between devices, swap_with(): lax.ppermute(block, 'corpus', [(i, i ^ distance) for i in range(groups)])  21.8 us
    ppermute x12, starting transfers between devices, swap_with(): lax.ppermute(block, 'corpus', [(i, i ^ distance) for i in range(groups)])  18 us
    ppermute x3, waiting for transfers between devices, shards(): lax.ppermute(outgoing, 'rep', [(r, (r + step) % reps) for r in range(reps)])  14.2 us
    dot_general x1, matrix products, shards(): lax.dot_general(all_queries, slab, across, preferred_element_type=f32)  7.98 us
    unnamed x7, other arithmetic  7.51 us
    all_to_all x1, waiting for transfers between devices, shards(): lax.all_to_all(jnp.broadcast_to(stats[None], (groups, *stats.shape)), 'co...  7.34 us
    all_to_all x1, waiting for transfers between devices, shards(): lax.all_to_all(message, 'corpus', split_axis=0, concat_axis=0, tiled=True)  5.69 us
    dot_general x1, matrix products, shards(): weight = jnp.dot(hot_weight, place, preferred_element_type=f32)  5.5 us
  transfers between devices with their start and end apart: 17, of which 10 were waited for; matrix products, arithmetic and copies ran while one was open for 16% of the time, Pallas kernels for 0%

profile of v5, /device:TPU:0, one launch (start us, length us, event | category | flops | bytes accessed | tf_op | source)
XLA Modules:
  0.0 129.0 jit_solution(8888817025591807731)
XLA Ops:
  0.7 3.0 %collective-permute-start.4 = (bf16[128,768]{1,0:T(8,128)(2,1)}, bf16[128,768]{1,0:T(8,128)(2,1)}, u32[]{:S(2)}, u32[]{:S(2)}) collective-permute-start(bf16[128,768]{1,0:T(8,128)(2,1)} %param.6), channel_id=1, source_target_pairs={{0,4},{4,0},{8,12},{12,8},{16,20},{20,16},{24,28},{28,24},{1,5},{5... | collective-permute-start | bytes 589832 | tf_op jit(solution)/shard_map/ppermute | solution.py:61
  3.7 1.6 %collective-permute-start = (bf16[128,768]{1,0:T(8,128)(2,1)}, bf16[128,768]{1,0:T(8,128)(2,1)S(1)}, u32[]{:S(2)}, u32[]{:S(2)}) collective-permute-start(bf16[128,768]{1,0:T(8,128)(2,1)} %param.6), channel_id=1, source_target_pairs={{0,8},{4,12},{8,0},{12,4},{16,24},{20,28},{24,16},{28,20},{1,9},{5... | collective-permute-start | bytes 589832 | tf_op jit(solution)/shard_map/ppermute | solution.py:61
  5.2 2.6 %collective-permute-start.1 = (bf16[128,768]{1,0:T(8,128)(2,1)}, bf16[128,768]{1,0:T(8,128)(2,1)S(1)}, u32[]{:S(2)}, u32[]{:S(2)}) collective-permute-start(bf16[128,768]{1,0:T(8,128)(2,1)} %param.6), channel_id=1, source_target_pairs={{0,16},{4,20},{8,24},{12,28},{16,0},{20,4},{24,8},{28,12},{1,17},{... | collective-permute-start | bytes 589832 | tf_op jit(solution)/shard_map/ppermute | solution.py:61
  7.8 0.2 collective-permute-start.2
  8.0 0.8 reduce_max.36
  8.8 0.8 exponential_reduce_fusion
  9.6 0.8 subtract_exponential_fusion
  10.4 0.8 copy.34
  11.3 4.4 %compare_reduce_fusion = pred[128,64]{1,0:T(8,128)(4,1)S(1)} fusion(s32[256]{0:T(256)} %param.10, s32[128,64]{1,0:T(8,128)S(1)} %copy.34), kind=kLoop, calls=%fused_computation | loop fusion | flops 4186112 | bytes 41984 | tf_op jit(solution)/shard_map/reduce_or | solution.py:35
  15.7 0.2 fusion.3
  15.9 0.8 select_reduce_fusion.9
  16.8 0.1 copy.36
  16.9 0.1 copy.39
  17.0 0.1 broadcast_in_dim_reshape.4
  17.1 0.8 fusion.22
  17.9 0.5 fusion.8
  18.4 0.1 fusion.7
  18.6 3.0 %fusion = (f32[128,256]{1,0:T(8,128)S(1)}, f32[128,256]{1,0:T(8,128)S(1)}) fusion(s32[256]{0:T(256)S(1)} %copy-done.1, s32[128,64]{1,0:T(8,128)S(1)} %copy.34, f32[128,64]{1,0:T(8,128)S(1)} %copy.36), kind=kLoop, calls=%fused_computation.3 | loop fusion | flops 10420224 | bytes 328704 | tf_op jit(solution)/shard_map/reduce_sum | solution.py:33
  21.7 0.1 copy.35
  21.9 0.7 pad_maximum_fusion.1
  22.7 5.2 %all-to-all-start = ((f32[8,128,80]{1,2,0:T(8,128)}), f32[8,128,80]{1,2,0:T(8,128)S(1)}, u32[]{:S(2)}, u32[]{:S(2)}) async-start(f32[8,128,80]{1,2,0:T(8,128)} %pad_maximum_fusion.1), calls=%async_computation | async-start | bytes 655360 | tf_op jit(solution)/shard_map/all_to_all | solution.py:100
  28.0 0.2 fusion.31
  28.2 0.2 fusion.35
  28.3 0.9 pad_maximum_fusion
  29.2 2.0 %collective-permute-start.3 = (bf16[3,128,768]{2,1,0:T(8,128)(2,1)}, bf16[3,128,768]{2,1,0:T(8,128)(2,1)S(1)}, u32[]{:S(2)}, u32[]{:S(2)}) collective-permute-start(bf16[3,128,768]{2,1,0:T(8,128)(2,1)} %pad_maximum_fusion), channel_id=1, source_target_pairs={{0,4},{4,0},{8,12},{12,8},{16,20},{20,16},{24,28},{28,24},{1,5},{5... | collective-permute-start | bytes 1769480 | tf_op jit(solution)/shard_map/ppermute | solution.py:61
  31.3 5.7 %all-to-all-done = f32[8,128,80]{1,2,0:T(8,128)S(1)} async-done(((f32[8,128,80]{1,2,0:T(8,128)}), f32[8,128,80]{1,2,0:T(8,128)S(1)}, u32[]{:S(2)}, u32[]{:S(2)}) %all-to-all-start) | async-done | bytes 327712 | tf_op jit(solution)/shard_map/all_to_all | solution.py:100
  37.0 9.0 %collective-permute-done.3 = bf16[3,128,768]{2,1,0:T(8,128)(2,1)S(1)} collective-permute-done((bf16[3,128,768]{2,1,0:T(8,128)(2,1)}, bf16[3,128,768]{2,1,0:T(8,128)(2,1)S(1)}, u32[]{:S(2)}, u32[]{:S(2)}) %collective-permute-start.3) | collective-permute-done | bytes 589856 | tf_op jit(solution)/shard_map/ppermute | solution.py:61
  46.0 1.8 %select_dynamic-update-slice_fusion.7 = (bf16[1024,768]{1,0:T(8,128)(2,1)}, bf16[128,768]{1,0:T(8,128)(2,1)S(1)}, bf16[128,768]{1,0:T(8,128)(2,1)S(1)}, bf16[128,768]{1,0:T(8,128)(2,1)S(1)}, bf16[128,768]{1,0:T(8,128)(2,1)S(1)}) fusion(pred[]{:T(512)S(6)} %eq.129, pred[]{:T(512)S(6)} %eq.130, bf16[128,768]{1,0:T(8,128)(2,1)} %collective-permute-done.4, ...), kind=kLoop, calls=%fused_computation.75 | loop fusion | flops 688127 | bytes 2555907
  47.8 1.8 %select_dynamic-update-slice_fusion.6 = (bf16[1024,768]{1,0:T(8,128)(2,1)}, bf16[128,768]{1,0:T(8,128)(2,1)S(1)}, bf16[128,768]{1,0:T(8,128)(2,1)S(1)}, bf16[128,768]{1,0:T(8,128)(2,1)S(1)}, bf16[128,768]{1,0:T(8,128)(2,1)S(1)}) fusion(bf16[1024,768]{1,0:T(8,128)(2,1)} %get-tuple-element.42, pred[]{:T(512)S(6)} %eq.129, pred[]{:T(512)S(6)} %eq.130, ...), kind=kLoop, calls=%fused_computation.74 | loop fusion | flops 688128 | bytes 2555907
  49.6 0.8 select_dynamic-update-slice_fusion.5
  50.4 0.8 select_dynamic-update-slice_fusion.4
  51.2 0.8 select_dynamic-update-slice_fusion.3
  52.0 0.8 select_dynamic-update-slice_fusion.2
  52.7 0.8 select_dynamic-update-slice_fusion.1
  53.5 0.8 select_dynamic-update-slice_fusion
  54.3 2.3 %fusion.45 = (f32[1024]{0:T(1024)S(1)}, f32[1024,32]{0,1:T(8,128)S(1)}) fusion(bf16[1024,768]{1,0:T(8,128)(2,1)} %select_dynamic-update-slice_fusion, bf16[1024,768]{1,0:T(8,128)(2,1)S(1)} %copy-done, s32[32]{0:T(128)S(1)} %convert_subtract_fusion), kind=kOutput, calls=%fused_computation.166 | convolution fusion | flops 100785152 | bytes 3281024 | tf_op jit(solution)/shard_map/dot_general | solution.py:115
  56.6 8.0 %select_reduce_fusion = (f32[1024]{0:T(1024)S(1)}, f32[1024]{0:T(1024)S(1)}, f32[1024]{0:T(1024)S(1)}, f32[1024]{0:T(1024)S(1)}, f32[1024]{0:T(1024)S(1)}, /*ind...) fusion(s32[1024]{0:T(1024)S(1)} %bitcast.176, s32[1024]{0:T(1024)S(1)} %bitcast.174, s32[1024]{0:T(1024)S(1)} %bitcast.172, ...), kind=kOutput, calls=%fused_computation.6 | convolution fusion | flops 1636818944 | bytes 3211264 | tf_op jit(solution)/shard_map/dot_general | solution.py:116
  64.8 0.7 broadcast_in_dim.208
  65.5 4.7 %all-to-all-start.1 = ((f32[8,3,1024]{2,1,0:T(4,128)}), f32[8,3,1024]{2,1,0:T(4,128)S(1)}, u32[]{:S(2)}, u32[]{:S(2)}) async-start(f32[8,3,1024]{2,1,0:T(4,128)} %broadcast_in_dim.208), calls=%async_computation.1 | async-start | bytes 262144 | tf_op jit(solution)/shard_map/all_to_all | solution.py:136
  70.2 7.3 %all-to-all-done.1 = f32[8,3,1024]{2,1,0:T(4,128)S(1)} async-done(((f32[8,3,1024]{2,1,0:T(4,128)}), f32[8,3,1024]{2,1,0:T(4,128)S(1)}, u32[]{:S(2)}, u32[]{:S(2)}) %all-to-all-start.1) | async-done | bytes 98336 | tf_op jit(solution)/shard_map/all_to_all | solution.py:136
  77.6 0.1 slice_reduce_fusion
  77.8 5.5 %add_convert_fusion = bf16[1024,1024]{0,1:T(8,128)(2,1)S(1)} fusion(f32[1024]{0:T(1024)S(1)} %bitcast.179, f32[1024]{0:T(1024)S(1)} %bitcast.180, f32[1024]{0:T(1024)S(1)} %bitcast.181, f32[1024]{0:T(1024)S(1)} %bitcast.182, f32[1024]{0:T(1024)S(1)} %bitcast.183, f32[1024]{0:T(1024)S(1)} %bitcast.184, f32[1024]{0:T(1024)S(1)} %bitcast.185, ...), kind=kOutput, calls=%fused_computation.5 | convolution fusion | flops 93519872 | bytes 2560512 | tf_op jit(solution)/shard_map/dot_general | solution.py:151
  83.3 1.9 %convolution_multiply_fusion = f32[1024,768]{1,0:T(8,128)S(1)} fusion(bf16[1024,1024]{0,1:T(8,128)(2,1)S(1)} %add_convert_fusion, bf16[1024,768]{1,0:T(8,128)(2,1)S(1)} %copy-done), kind=kOutput, calls=%fused_computation.23 | convolution fusion | flops 1611399168 | bytes 6815744 | tf_op jit(solution)/shard_map/dot_general | solution.py:158
  85.2 0.1 select_convert_fusion
  85.4 0.3 collective-permute-start.6
  85.7 1.8 %collective-permute-start.10 = (bf16[128,768]{1,0:T(8,128)(2,1)S(1)}, bf16[128,768]{1,0:T(8,128)(2,1)S(1)}, u32[]{:S(2)}, u32[]{:S(2)}) collective-permute-start(bf16[128,768]{1,0:T(8,128)(2,1)S(1)} %get-tuple-element.54), channel_id=1, source_target_pairs={{0,4},{4,0},{8,12},{12,8},{16,20},{20,16},{24,28},{28,24},{1,5},{5... | collective-permute-start | bytes 589832 | tf_op jit(solution)/shard_map/ppermute | solution.py:61
  87.5 0.2 collective-permute-start.8
  87.7 1.8 %collective-permute-start.5 = (bf16[128,768]{1,0:T(8,128)(2,1)S(1)}, bf16[128,768]{1,0:T(8,128)(2,1)S(1)}, u32[]{:S(2)}, u32[]{:S(2)}) collective-permute-start(bf16[128,768]{1,0:T(8,128)(2,1)S(1)} %get-tuple-element.53), channel_id=1, source_target_pairs={{0,4},{4,0},{8,12},{12,8},{16,20},{20,16},{24,28},{28,24},{1,5},{5... | collective-permute-start | bytes 589832 | tf_op jit(solution)/shard_map/ppermute | solution.py:61
  89.5 0.2 slice_select_fusion
  89.7 3.6 %collective-permute-done.6 = bf16[128,768]{1,0:T(8,128)(2,1)S(1)} collective-permute-done((bf16[128,768]{1,0:T(8,128)(2,1)S(1)}, bf16[128,768]{1,0:T(8,128)(2,1)S(1)}, u32[]{:S(2)}, u32[]{:S(2)}) %collective-permute-start.6) | collective-permute-done | bytes 196640 | tf_op jit(solution)/shard_map/ppermute | solution.py:61
  93.3 4.2 %collective-permute-done.10 = bf16[128,768]{1,0:T(8,128)(2,1)S(1)} collective-permute-done((bf16[128,768]{1,0:T(8,128)(2,1)S(1)}, bf16[128,768]{1,0:T(8,128)(2,1)S(1)}, u32[]{:S(2)}, u32[]{:S(2)}) %collective-permute-start.10) | collective-permute-done | bytes 196640 | tf_op jit(solution)/shard_map/ppermute | solution.py:61
  97.5 2.5 %collective-permute-done.8 = bf16[128,768]{1,0:T(8,128)(2,1)S(1)} collective-permute-done((bf16[128,768]{1,0:T(8,128)(2,1)S(1)}, bf16[128,768]{1,0:T(8,128)(2,1)S(1)}, u32[]{:S(2)}, u32[]{:S(2)}) %collective-permute-start.8) | collective-permute-done | bytes 196640 | tf_op jit(solution)/shard_map/ppermute | solution.py:61
  100.1 0.1 fusion.11
  100.3 1.1 collective-permute-start.9
  101.4 3.3 %collective-permute-start.7 = (bf16[128,768]{1,0:T(8,128)(2,1)S(1)}, bf16[128,768]{1,0:T(8,128)(2,1)S(1)}, u32[]{:S(2)}, u32[]{:S(2)}) collective-permute-start(bf16[128,768]{1,0:T(8,128)(2,1)S(1)} %get-tuple-element.50), channel_id=1, source_target_pairs={{0,24},{4,28},{8,16},{12,20},{16,8},{20,12},{24,0},{28,4},{1,25},{... | collective-permute-start | bytes 589832 | tf_op jit(solution)/shard_map/ppermute | solution.py:61
  104.7 3.2 %multiply_convert_fusion = bf16[1024,768]{1,0:T(8,128)(2,1)S(1)} fusion(bf16[1024,1024]{0,1:T(8,128)(2,1)S(1)} %add_convert_fusion, bf16[1024,768]{1,0:T(8,128)(2,1)} %select_dynamic-update-slice_fusion), kind=kOutput, calls=%fused_computation.22 | convolution fusion | flops 1612185600 | bytes 5242880 | tf_op jit(solution)/shard_map/dot_general | solution.py:189
  108.1 1.6 %collective-permute-start.13 = (bf16[256,768]{1,0:T(8,128)(2,1)S(1)}, bf16[256,768]{1,0:T(8,128)(2,1)S(1)}, u32[]{:S(2)}, u32[]{:S(2)}) collective-permute-start(bf16[256,768]{1,0:T(8,128)(2,1)S(1)} %get-tuple-element.49), channel_id=1, source_target_pairs={{0,2},{1,3},{2,0},{3,1},{4,6},{5,7},{6,4},{7,5},{8,10},{9,11},{10,... | collective-permute-start | bytes 1179656 | tf_op jit(solution)/shard_map/ppermute | solution.py:197
  109.6 0.2 collective-permute-start.12
  109.8 0.6 dynamic-slice_add_fusion
  110.4 2.5 %collective-permute-done.9 = bf16[128,768]{1,0:T(8,128)(2,1)S(1)} collective-permute-done((bf16[128,768]{1,0:T(8,128)(2,1)S(1)}, bf16[128,768]{1,0:T(8,128)(2,1)S(1)}, u32[]{:S(2)}, u32[]{:S(2)}) %collective-permute-start.9) | collective-permute-done | bytes 196640 | tf_op jit(solution)/shard_map/ppermute | solution.py:61
  112.9 0.9 fusion.14
  113.7 2.7 %collective-permute-done.14 = bf16[256,768]{1,0:T(8,128)(2,1)S(1)} collective-permute-done((bf16[256,768]{1,0:T(8,128)(2,1)S(1)}, bf16[256,768]{1,0:T(8,128)(2,1)S(1)}, u32[]{:S(2)}, u32[]{:S(2)}) %collective-permute-start.14) | collective-permute-done | bytes 393248 | tf_op jit(solution)/shard_map/ppermute | solution.py:197
  116.5 11.4 %collective-permute-done.13 = bf16[256,768]{1,0:T(8,128)(2,1)S(1)} collective-permute-done((bf16[256,768]{1,0:T(8,128)(2,1)S(1)}, bf16[256,768]{1,0:T(8,128)(2,1)S(1)}, u32[]{:S(2)}, u32[]{:S(2)}) %collective-permute-start.13) | collective-permute-done | bytes 393248 | tf_op jit(solution)/shard_map/ppermute | solution.py:197
  127.9 1.1 fusion.5
  (44 shorter events, 1.3 us)
Async XLA Ops:
  0.6 53.7 %copy-start = (bf16[1024,768]{1,0:T(8,128)(2,1)S(1)}, bf16[1024,768]{1,0:T(8,128)(2,1)}, u32[]{:S(2)}) copy-start(bf16[1024,768]{1,0:T(8,128)(2,1)} %param.8) | copy-start | bytes 4718596
  0.6 18.0 %copy-start.1 = (s32[256]{0:T(256)S(1)}, s32[256]{0:T(256)}, u32[]{:S(2)}) copy-start(s32[256]{0:T(256)} %param.10) | copy-start | bytes 3076
  0.7 36.4 %collective-permute-start.4 = (bf16[128,768]{1,0:T(8,128)(2,1)}, bf16[128,768]{1,0:T(8,128)(2,1)}, u32[]{:S(2)}, u32[]{:S(2)}) collective-permute-start(bf16[128,768]{1,0:T(8,128)(2,1)} %param.6), channel_id=1, source_target_pairs={{0,4},{4,0},{8,12},{12,8},{16,20},{20,16},{24,28},{28,24},{1,5},{5... | collective-permute-start | bytes 589832 | tf_op jit(solution)/shard_map/ppermute | solution.py:61
  3.7 19.1 %collective-permute-start = (bf16[128,768]{1,0:T(8,128)(2,1)}, bf16[128,768]{1,0:T(8,128)(2,1)S(1)}, u32[]{:S(2)}, u32[]{:S(2)}) collective-permute-start(bf16[128,768]{1,0:T(8,128)(2,1)} %param.6), channel_id=1, source_target_pairs={{0,8},{4,12},{8,0},{12,4},{16,24},{20,28},{24,16},{28,20},{1,9},{5... | collective-permute-start | bytes 589832 | tf_op jit(solution)/shard_map/ppermute | solution.py:61
  5.2 17.5 %collective-permute-start.1 = (bf16[128,768]{1,0:T(8,128)(2,1)}, bf16[128,768]{1,0:T(8,128)(2,1)S(1)}, u32[]{:S(2)}, u32[]{:S(2)}) collective-permute-start(bf16[128,768]{1,0:T(8,128)(2,1)} %param.6), channel_id=1, source_target_pairs={{0,16},{4,20},{8,24},{12,28},{16,0},{20,4},{24,8},{28,12},{1,17},{... | collective-permute-start | bytes 589832 | tf_op jit(solution)/shard_map/ppermute | solution.py:61
  7.8 14.9 %collective-permute-start.2 = (bf16[128,768]{1,0:T(8,128)(2,1)}, bf16[128,768]{1,0:T(8,128)(2,1)S(1)}, u32[]{:S(2)}, u32[]{:S(2)}) collective-permute-start(bf16[128,768]{1,0:T(8,128)(2,1)} %param.6), channel_id=1, source_target_pairs={{0,24},{4,28},{8,16},{12,20},{16,8},{20,12},{24,0},{28,4},{1,25},{... | collective-permute-start | bytes 589832 | tf_op jit(solution)/shard_map/ppermute | solution.py:61
  22.7 14.2 %all-to-all-start = ((f32[8,128,80]{1,2,0:T(8,128)}), f32[8,128,80]{1,2,0:T(8,128)S(1)}, u32[]{:S(2)}, u32[]{:S(2)}) async-start(f32[8,128,80]{1,2,0:T(8,128)} %pad_maximum_fusion.1), calls=%async_computation | async-start | bytes 655360 | tf_op jit(solution)/shard_map/all_to_all | solution.py:100
  29.2 16.8 %collective-permute-start.3 = (bf16[3,128,768]{2,1,0:T(8,128)(2,1)}, bf16[3,128,768]{2,1,0:T(8,128)(2,1)S(1)}, u32[]{:S(2)}, u32[]{:S(2)}) collective-permute-start(bf16[3,128,768]{2,1,0:T(8,128)(2,1)} %pad_maximum_fusion), channel_id=1, source_target_pairs={{0,4},{4,0},{8,12},{12,8},{16,20},{20,16},{24,28},{28,24},{1,5},{5... | collective-permute-start | bytes 1769480 | tf_op jit(solution)/shard_map/ppermute | solution.py:61
  65.5 12.1 %all-to-all-start.1 = ((f32[8,3,1024]{2,1,0:T(4,128)}), f32[8,3,1024]{2,1,0:T(4,128)S(1)}, u32[]{:S(2)}, u32[]{:S(2)}) async-start(f32[8,3,1024]{2,1,0:T(4,128)} %broadcast_in_dim.208), calls=%async_computation.1 | async-start | bytes 262144 | tf_op jit(solution)/shard_map/all_to_all | solution.py:136
  85.4 7.9 %collective-permute-start.6 = (bf16[128,768]{1,0:T(8,128)(2,1)S(1)}, bf16[128,768]{1,0:T(8,128)(2,1)S(1)}, u32[]{:S(2)}, u32[]{:S(2)}) collective-permute-start(bf16[128,768]{1,0:T(8,128)(2,1)S(1)} %get-tuple-element.56), channel_id=1, source_target_pairs={{0,4},{4,0},{8,12},{12,8},{16,20},{20,16},{24,28},{28,24},{1,5},{5... | collective-permute-start | bytes 589832 | tf_op jit(solution)/shard_map/ppermute | solution.py:61
  85.7 11.8 %collective-permute-start.10 = (bf16[128,768]{1,0:T(8,128)(2,1)S(1)}, bf16[128,768]{1,0:T(8,128)(2,1)S(1)}, u32[]{:S(2)}, u32[]{:S(2)}) collective-permute-start(bf16[128,768]{1,0:T(8,128)(2,1)S(1)} %get-tuple-element.54), channel_id=1, source_target_pairs={{0,4},{4,0},{8,12},{12,8},{16,20},{20,16},{24,28},{28,24},{1,5},{5... | collective-permute-start | bytes 589832 | tf_op jit(solution)/shard_map/ppermute | solution.py:61
  87.5 12.6 %collective-permute-start.8 = (bf16[128,768]{1,0:T(8,128)(2,1)S(1)}, bf16[128,768]{1,0:T(8,128)(2,1)S(1)}, u32[]{:S(2)}, u32[]{:S(2)}) collective-permute-start(bf16[128,768]{1,0:T(8,128)(2,1)S(1)} %get-tuple-element.55), channel_id=1, source_target_pairs={{0,4},{4,0},{8,12},{12,8},{16,20},{20,16},{24,28},{28,24},{1,5},{5... | collective-permute-start | bytes 589832 | tf_op jit(solution)/shard_map/ppermute | solution.py:61
  87.7 20.3 %collective-permute-start.5 = (bf16[128,768]{1,0:T(8,128)(2,1)S(1)}, bf16[128,768]{1,0:T(8,128)(2,1)S(1)}, u32[]{:S(2)}, u32[]{:S(2)}) collective-permute-start(bf16[128,768]{1,0:T(8,128)(2,1)S(1)} %get-tuple-element.53), channel_id=1, source_target_pairs={{0,4},{4,0},{8,12},{12,8},{16,20},{20,16},{24,28},{28,24},{1,5},{5... | collective-permute-start | bytes 589832 | tf_op jit(solution)/shard_map/ppermute | solution.py:61
  100.2 9.4 %collective-permute-start.11 = (bf16[128,768]{1,0:T(8,128)(2,1)S(1)}, bf16[128,768]{1,0:T(8,128)(2,1)S(1)}, u32[]{:S(2)}, u32[]{:S(2)}) collective-permute-start(bf16[128,768]{1,0:T(8,128)(2,1)S(1)} %get-tuple-element.51), channel_id=1, source_target_pairs={{0,8},{4,12},{8,0},{12,4},{16,24},{20,28},{24,16},{28,20},{1,9},{5... | collective-permute-start | bytes 589832 | tf_op jit(solution)/shard_map/ppermute | solution.py:61
  100.3 12.6 %collective-permute-start.9 = (bf16[128,768]{1,0:T(8,128)(2,1)S(1)}, bf16[128,768]{1,0:T(8,128)(2,1)S(1)}, u32[]{:S(2)}, u32[]{:S(2)}) collective-permute-start(bf16[128,768]{1,0:T(8,128)(2,1)S(1)} %get-tuple-element.52), channel_id=1, source_target_pairs={{0,16},{4,20},{8,24},{12,28},{16,0},{20,4},{24,8},{28,12},{1,17},{... | collective-permute-start | bytes 589832 | tf_op jit(solution)/shard_map/ppermute | solution.py:61
  101.4 11.5 %collective-permute-start.7 = (bf16[128,768]{1,0:T(8,128)(2,1)S(1)}, bf16[128,768]{1,0:T(8,128)(2,1)S(1)}, u32[]{:S(2)}, u32[]{:S(2)}) collective-permute-start(bf16[128,768]{1,0:T(8,128)(2,1)S(1)} %get-tuple-element.50), channel_id=1, source_target_pairs={{0,24},{4,28},{8,16},{12,20},{16,8},{20,12},{24,0},{28,4},{1,25},{... | collective-permute-start | bytes 589832 | tf_op jit(solution)/shard_map/ppermute | solution.py:61
  108.0 8.5 %collective-permute-start.14 = (bf16[256,768]{1,0:T(8,128)(2,1)S(1)}, bf16[256,768]{1,0:T(8,128)(2,1)S(1)}, u32[]{:S(2)}, u32[]{:S(2)}) collective-permute-start(bf16[256,768]{1,0:T(8,128)(2,1)S(1)} %get-tuple-element.48), channel_id=1, source_target_pairs={{0,3},{1,0},{2,1},{3,2},{4,7},{5,4},{6,5},{7,6},{8,11},{9,8},{10,9... | collective-permute-start | bytes 1179656 | tf_op jit(solution)/shard_map/ppermute | solution.py:197
  108.1 19.8 %collective-permute-start.13 = (bf16[256,768]{1,0:T(8,128)(2,1)S(1)}, bf16[256,768]{1,0:T(8,128)(2,1)S(1)}, u32[]{:S(2)}, u32[]{:S(2)}) collective-permute-start(bf16[256,768]{1,0:T(8,128)(2,1)S(1)} %get-tuple-element.49), channel_id=1, source_target_pairs={{0,2},{1,3},{2,0},{3,1},{4,6},{5,7},{6,4},{7,5},{8,10},{9,11},{10,... | collective-permute-start | bytes 1179656 | tf_op jit(solution)/shard_map/ppermute | solution.py:197
  109.6 18.3 %collective-permute-start.12 = (bf16[256,768]{1,0:T(8,128)(2,1)S(1)}, bf16[256,768]{1,0:T(8,128)(2,1)S(1)}, u32[]{:S(2)}, u32[]{:S(2)}) collective-permute-start(bf16[256,768]{1,0:T(8,128)(2,1)S(1)} %get-tuple-element.47), channel_id=1, source_target_pairs={{0,1},{1,2},{2,3},{3,0},{4,5},{5,6},{6,7},{7,4},{8,9},{9,10},{10,1... | collective-permute-start | bytes 1179656 | tf_op jit(solution)/shard_map/ppermute | solution.py:197

commit v6 on v4

--- a/solution.py
+++ b/solution.py
@@ -164,10 +164,13 @@
         give = give.astype(jnp.bfloat16)
         query_grad = None
         halfway = []
-        for d in range(groups // 2 - 1, -1, -1):
-            target = (me // 2) ^ d
-            block = lax.dynamic_index_in_dim(give, target, 0, keepdims=False)
-            halfway.append((d, target, swap_with(block, 1, groups)))
+        for d in range(groups // 2 - 1, -1, -2):
+            targets = [(me // 2) ^ d, (me // 2) ^ (d - 1)]
+            pair = jnp.stack(
+                [lax.dynamic_index_in_dim(give, t, 0, keepdims=False) for t in targets]
+            )
+            arrived = swap_with(pair, 1, groups)
+            halfway += [(d - n, targets[n], arrived[n]) for n in range(2)]
         far_parts = []
         for d, target, arrived in halfway:
             both = lax.dynamic_index_in_dim(keep, target, 0, keepdims=False) + arrived.astype(f32)

time: 119 us -> 122 us (1.025)
  waiting for transfers between devices: 47.6 us -> 49.3 us
    ppermute x12 -> x10, waiting for transfers between devices: 34.4 us -> 36.1 us  [swap_with(): lax.ppermute(block, 'corpus', [(i, i ^ distance) for i in range(groups)])]
    ppermute x12 -> x10, starting transfers between devices: 15.5 us -> 16 us  [swap_with(): lax.ppermute(block, 'corpus', [(i, i ^ distance) for i in range(groups)])]
  transfers between devices with their start and end apart: 17 -> 15, of which waited for: 9 -> 7; matrix products, arithmetic and copies ran while one was open for 15% -> 15% of each run, Pallas kernels for 0% -> 0%
where the time goes in v6:
time: 122 us; the launch traced here: 121 us
  waiting for transfers between devices  49.3 us (40%)
  starting transfers between devices  28.6 us (23%)
  other arithmetic  19.7 us (16%)
  matrix products  19.4 us (16%)
  local copies, waits for them, and re-layouts  2.53 us (2%)
    ppermute x10, waiting for transfers between devices, swap_with(): lax.ppermute(block, 'corpus', [(i, i ^ distance) for i in range(groups)])  36.1 us
    ppermute x10, starting transfers between devices, swap_with(): lax.ppermute(block, 'corpus', [(i, i ^ distance) for i in range(groups)])  16 us
    all_to_all x1, waiting for transfers between devices, shards(): lax.all_to_all(jnp.broadcast_to(stats[None], (groups, *stats.shape)), 'co...  7.34 us
    dot_general x1, matrix products, shards(): lax.dot_general(all_queries, slab, across, preferred_element_type=f32)  7.1 us
    all_to_all x1, waiting for transfers between devices, shards(): lax.all_to_all(message, 'corpus', split_axis=0, concat_axis=0, tiled=True)  5.86 us
    dot_general x1, matrix products, shards(): weight = jnp.dot(hot_weight, place, preferred_element_type=f32)  5.5 us
    all_to_all x1, starting transfers between devices, shards(): lax.all_to_all(message, 'corpus', split_axis=0, concat_axis=0, tiled=True)  4.94 us
    all_to_all x1, starting transfers between devices, shards(): lax.all_to_all(jnp.broadcast_to(stats[None], (groups, *stats.shape)), 'co...  4.64 us
  transfers between devices with their start and end apart: 15, of which 7 were waited for; matrix products, arithmetic and copies ran while one was open for 15% of the time, Pallas kernels for 0%

profile of v6, /device:TPU:0, one launch (start us, length us, event | category | flops | bytes accessed | tf_op | source)
XLA Modules:
  0.0 120.7 jit_solution(14400971064776073711)
XLA Ops:
  0.7 3.1 %collective-permute-start = (bf16[128,768]{1,0:T(8,128)(2,1)}, bf16[128,768]{1,0:T(8,128)(2,1)S(1)}, u32[]{:S(2)}, u32[]{:S(2)}) collective-permute-start(bf16[128,768]{1,0:T(8,128)(2,1)} %param.6), channel_id=1, source_target_pairs={{0,8},{4,12},{8,0},{12,4},{16,24},{20,28},{24,16},{28,20},{1,9},{5... | collective-permute-start | bytes 589832 | tf_op jit(solution)/shard_map/ppermute | solution.py:61
  3.7 2.6 %collective-permute-start.1 = (bf16[128,768]{1,0:T(8,128)(2,1)}, bf16[128,768]{1,0:T(8,128)(2,1)S(1)}, u32[]{:S(2)}, u32[]{:S(2)}) collective-permute-start(bf16[128,768]{1,0:T(8,128)(2,1)} %param.6), channel_id=1, source_target_pairs={{0,16},{4,20},{8,24},{12,28},{16,0},{20,4},{24,8},{28,12},{1,17},{... | collective-permute-start | bytes 589832 | tf_op jit(solution)/shard_map/ppermute | solution.py:61
  6.3 1.7 %collective-permute-start.4 = (bf16[128,768]{1,0:T(8,128)(2,1)}, bf16[128,768]{1,0:T(8,128)(2,1)}, u32[]{:S(2)}, u32[]{:S(2)}) collective-permute-start(bf16[128,768]{1,0:T(8,128)(2,1)} %param.6), channel_id=1, source_target_pairs={{0,4},{4,0},{8,12},{12,8},{16,20},{20,16},{24,28},{28,24},{1,5},{5... | collective-permute-start | bytes 589832 | tf_op jit(solution)/shard_map/ppermute | solution.py:61
  8.0 0.8 copy.34
  8.9 4.4 %compare_reduce_fusion = pred[128,64]{1,0:T(8,128)(4,1)S(1)} fusion(s32[256]{0:T(256)} %param.10, s32[128,64]{1,0:T(8,128)S(1)} %copy.34), kind=kLoop, calls=%fused_computation | loop fusion | flops 4186112 | bytes 41984 | tf_op jit(solution)/shard_map/reduce_or | solution.py:35
  13.3 0.1 copy.38
  13.4 0.2 fusion.3
  13.6 0.8 select_reduce_fusion.9
  14.4 0.8 reduce_max.36
  15.1 0.8 exponential_reduce_fusion
  15.9 0.8 subtract_exponential_fusion
  16.8 0.1 copy.36
  16.9 0.1 copy.39
  17.0 0.1 broadcast_in_dim_reshape.4
  17.1 0.8 fusion.22
  17.9 0.5 fusion.8
  18.4 0.1 fusion.7
  18.6 3.0 %fusion = (f32[128,256]{1,0:T(8,128)S(1)}, f32[128,256]{1,0:T(8,128)S(1)}) fusion(s32[256]{0:T(256)S(1)} %copy-done.3, s32[128,64]{1,0:T(8,128)S(1)} %copy.34, f32[128,64]{1,0:T(8,128)S(1)} %copy.36), kind=kLoop, calls=%fused_computation.3 | loop fusion | flops 10420224 | bytes 328704 | tf_op jit(solution)/shard_map/reduce_sum | solution.py:33
  21.6 0.1 copy.35
  21.7 0.1 copy.37
  21.8 0.1 and_select_fusion.1
  21.9 0.7 pad_maximum_fusion.3
  22.7 4.9 %all-to-all-start = ((f32[8,128,80]{1,2,0:T(8,128)}), f32[8,128,80]{1,2,0:T(8,128)S(1)}, u32[]{:S(2)}, u32[]{:S(2)}) async-start(f32[8,128,80]{1,2,0:T(8,128)} %pad_maximum_fusion.3), calls=%async_computation | async-start | bytes 655360 | tf_op jit(solution)/shard_map/all_to_all | solution.py:100
  27.7 0.2 fusion.31
  27.9 0.2 fusion.35
  28.1 0.9 pad_maximum_fusion
  28.9 2.0 %collective-permute-start.3 = (bf16[3,128,768]{2,1,0:T(8,128)(2,1)}, bf16[3,128,768]{2,1,0:T(8,128)(2,1)S(1)}, u32[]{:S(2)}, u32[]{:S(2)}) collective-permute-start(bf16[3,128,768]{2,1,0:T(8,128)(2,1)} %pad_maximum_fusion), channel_id=1, source_target_pairs={{0,4},{4,0},{8,12},{12,8},{16,20},{20,16},{24,28},{28,24},{1,5},{5... | collective-permute-start | bytes 1769480 | tf_op jit(solution)/shard_map/ppermute | solution.py:61
  31.0 5.9 %all-to-all-done = f32[8,128,80]{1,2,0:T(8,128)S(1)} async-done(((f32[8,128,80]{1,2,0:T(8,128)}), f32[8,128,80]{1,2,0:T(8,128)S(1)}, u32[]{:S(2)}, u32[]{:S(2)}) %all-to-all-start) | async-done | bytes 327712 | tf_op jit(solution)/shard_map/all_to_all | solution.py:100
  36.9 9.0 %collective-permute-done.3 = bf16[3,128,768]{2,1,0:T(8,128)(2,1)S(1)} collective-permute-done((bf16[3,128,768]{2,1,0:T(8,128)(2,1)}, bf16[3,128,768]{2,1,0:T(8,128)(2,1)S(1)}, u32[]{:S(2)}, u32[]{:S(2)}) %collective-permute-start.3) | collective-permute-done | bytes 589856 | tf_op jit(solution)/shard_map/ppermute | solution.py:61
  45.9 1.2 select_dynamic-update-slice_fusion.7
  47.0 1.2 select_dynamic-update-slice_fusion.6
  48.2 0.1 select_dynamic-update-slice_fusion.5
  48.3 0.1 select_dynamic-update-slice_fusion.4
  48.4 0.1 select_dynamic-update-slice_fusion.3
  48.5 0.1 select_dynamic-update-slice_fusion.2
  48.6 0.1 select_dynamic-update-slice_fusion.1
  48.8 0.1 select_dynamic-update-slice_fusion
  48.9 7.1 %select_reduce_fusion = (f32[1024]{0:T(1024)S(1)}, f32[1024]{0:T(1024)S(1)}, f32[1024]{0:T(1024)S(1)}, f32[1024]{0:T(1024)S(1)}, f32[1024]{0:T(1024)S(1)}, /*ind...) fusion(s32[1024]{0:T(1024)S(1)} %bitcast.184, s32[1024]{0:T(1024)S(1)} %bitcast.182, s32[1024]{0:T(1024)S(1)} %bitcast.180, ...), kind=kOutput, calls=%fused_computation.6 | convolution fusion | flops 1636818944 | bytes 3211264 | tf_op jit(solution)/shard_map/dot_general | solution.py:116
  56.1 2.3 %fusion.45 = (f32[1024]{0:T(1024)S(1)}, f32[1024,32]{0,1:T(8,128)S(1)}) fusion(bf16[1024,768]{1,0:T(8,128)(2,1)} %copy-done.1, bf16[1024,768]{1,0:T(8,128)(2,1)S(1)} %copy-done, s32[32]{0:T(128)S(1)} %convert_subtract_fusion), kind=kOutput, calls=%fused_computation.172 | convolution fusion | flops 100785152 | bytes 3281024 | tf_op jit(solution)/shard_map/dot_general | solution.py:115
  58.5 0.7 broadcast_in_dim.208
  59.2 4.6 %all-to-all-start.1 = ((f32[8,3,1024]{2,1,0:T(4,128)}), f32[8,3,1024]{2,1,0:T(4,128)S(1)}, u32[]{:S(2)}, u32[]{:S(2)}) async-start(f32[8,3,1024]{2,1,0:T(4,128)} %broadcast_in_dim.208), calls=%async_computation.1 | async-start | bytes 262144 | tf_op jit(solution)/shard_map/all_to_all | solution.py:136
  63.8 7.3 %all-to-all-done.1 = f32[8,3,1024]{2,1,0:T(4,128)S(1)} async-done(((f32[8,3,1024]{2,1,0:T(4,128)}), f32[8,3,1024]{2,1,0:T(4,128)S(1)}, u32[]{:S(2)}, u32[]{:S(2)}) %all-to-all-start.1) | async-done | bytes 98336 | tf_op jit(solution)/shard_map/all_to_all | solution.py:136
  71.2 0.1 slice_reduce_fusion
  71.4 5.5 %add_convert_fusion = bf16[1024,1024]{0,1:T(8,128)(2,1)S(1)} fusion(f32[1024]{0:T(1024)S(1)} %bitcast.187, f32[1024]{0:T(1024)S(1)} %bitcast.188, f32[1024]{0:T(1024)S(1)} %bitcast.189, f32[1024]{0:T(1024)S(1)} %bitcast.190, f32[1024]{0:T(1024)S(1)} %bitcast.191, f32[1024]{0:T(1024)S(1)} %bitcast.192, f32[1024]{0:T(1024)S(1)} %bitcast.193, ...), kind=kOutput, calls=%fused_computation.5 | convolution fusion | flops 93519872 | bytes 2560512 | tf_op jit(solution)/shard_map/dot_general | solution.py:151
  76.9 1.8 %multiply_convert_fusion = bf16[1024,768]{1,0:T(8,128)(2,1)S(1)} fusion(bf16[1024,1024]{0,1:T(8,128)(2,1)S(1)} %add_convert_fusion, bf16[1024,768]{1,0:T(8,128)(2,1)S(1)} %copy-done.2), kind=kOutput, calls=%fused_computation.22 | convolution fusion | flops 1612185600 | bytes 5242880 | tf_op jit(solution)/shard_map/dot_general | solution.py:189
  78.7 1.9 %convolution_multiply_fusion = f32[1024,768]{1,0:T(8,128)S(1)} fusion(bf16[1024,1024]{0,1:T(8,128)(2,1)S(1)} %add_convert_fusion, bf16[1024,768]{1,0:T(8,128)(2,1)S(1)} %copy-done), kind=kOutput, calls=%fused_computation.23 | convolution fusion | flops 1611399168 | bytes 6815744 | tf_op jit(solution)/shard_map/dot_general | solution.py:158
  80.7 0.1 dynamic-slice_bitcast_fusion.2
  80.8 1.6 %collective-permute-start.11 = (bf16[256,768]{1,0:T(8,128)(2,1)S(1)}, bf16[256,768]{1,0:T(8,128)(2,1)S(1)}, u32[]{:S(2)}, u32[]{:S(2)}) collective-permute-start(bf16[256,768]{1,0:T(8,128)(2,1)S(1)} %get-tuple-element.47), channel_id=1, source_target_pairs={{0,2},{1,3},{2,0},{3,1},{4,6},{5,7},{6,4},{7,5},{8,10},{9,11},{10,... | collective-permute-start | bytes 1179656 | tf_op jit(solution)/shard_map/ppermute | solution.py:197
  82.4 1.4 %collective-permute-start.12 = (bf16[256,768]{1,0:T(8,128)(2,1)S(1)}, bf16[256,768]{1,0:T(8,128)(2,1)S(1)}, u32[]{:S(2)}, u32[]{:S(2)}) collective-permute-start(bf16[256,768]{1,0:T(8,128)(2,1)S(1)} %get-tuple-element.46), channel_id=1, source_target_pairs={{0,3},{1,0},{2,1},{3,2},{4,7},{5,4},{6,5},{7,6},{8,11},{9,8},{10,9... | collective-permute-start | bytes 1179656 | tf_op jit(solution)/shard_map/ppermute | solution.py:197
  83.8 0.1 select_convert_fusion
  84.1 0.3 collective-permute-start.5
  84.4 1.9 %collective-permute-start.6 = (bf16[2,128,768]{2,1,0:T(8,128)(2,1)S(1)}, bf16[2,128,768]{2,1,0:T(8,128)(2,1)S(1)}, u32[]{:S(2)}, u32[]{:S(2)}) collective-permute-start(bf16[2,128,768]{2,1,0:T(8,128)(2,1)S(1)} %pad_maximum_fusion.2), channel_id=1, source_target_pairs={{0,4},{4,0},{8,12},{12,8},{16,20},{20,16},{24,28},{28,24},{1,5},{5... | collective-permute-start | bytes 1179656 | tf_op jit(solution)/shard_map/ppermute | solution.py:61
  86.2 0.2 slice_select_fusion
  86.5 0.6 dynamic-slice_add_fusion
  87.0 9.1 %collective-permute-done.5 = bf16[2,128,768]{2,1,0:T(8,128)(2,1)S(1)} collective-permute-done((bf16[2,128,768]{2,1,0:T(8,128)(2,1)S(1)}, bf16[2,128,768]{2,1,0:T(8,128)(2,1)S(1)}, u32[]{:S(2)}, u32[]{:S(2)}) %collective-permute-start.5) | collective-permute-done | bytes 393248 | tf_op jit(solution)/shard_map/ppermute | solution.py:61
  96.2 6.5 %collective-permute-done.6 = bf16[2,128,768]{2,1,0:T(8,128)(2,1)S(1)} collective-permute-done((bf16[2,128,768]{2,1,0:T(8,128)(2,1)S(1)}, bf16[2,128,768]{2,1,0:T(8,128)(2,1)S(1)}, u32[]{:S(2)}, u32[]{:S(2)}) %collective-permute-start.6) | collective-permute-done | bytes 393248 | tf_op jit(solution)/shard_map/ppermute | solution.py:61
  102.7 0.1 fusion.11
  102.8 0.6 collective-permute-start.7
  103.4 0.8 collective-permute-start.8
  104.2 3.1 %collective-permute-start.9 = (bf16[128,768]{1,0:T(8,128)(2,1)S(1)}, bf16[128,768]{1,0:T(8,128)(2,1)S(1)}, u32[]{:S(2)}, u32[]{:S(2)}) collective-permute-start(bf16[128,768]{1,0:T(8,128)(2,1)S(1)} %get-tuple-element.48), channel_id=1, source_target_pairs={{0,8},{4,12},{8,0},{12,4},{16,24},{20,28},{24,16},{28,20},{1,9},{5... | collective-permute-start | bytes 589832 | tf_op jit(solution)/shard_map/ppermute | solution.py:61
  107.3 1.1 fusion.5
  108.4 4.2 %collective-permute-done.7 = bf16[128,768]{1,0:T(8,128)(2,1)S(1)} collective-permute-done((bf16[128,768]{1,0:T(8,128)(2,1)S(1)}, bf16[128,768]{1,0:T(8,128)(2,1)S(1)}, u32[]{:S(2)}, u32[]{:S(2)}) %collective-permute-start.7) | collective-permute-done | bytes 196640 | tf_op jit(solution)/shard_map/ppermute | solution.py:61
  112.6 7.3 %collective-permute-done.8 = bf16[128,768]{1,0:T(8,128)(2,1)S(1)} collective-permute-done((bf16[128,768]{1,0:T(8,128)(2,1)S(1)}, bf16[128,768]{1,0:T(8,128)(2,1)S(1)}, u32[]{:S(2)}, u32[]{:S(2)}) %collective-permute-start.8) | collective-permute-done | bytes 196640 | tf_op jit(solution)/shard_map/ppermute | solution.py:61
  119.9 0.9 fusion.14
  (46 shorter events, 0.9 us)
Async XLA Ops:
  0.6 48.2 %copy-start = (bf16[1024,768]{1,0:T(8,128)(2,1)S(1)}, bf16[1024,768]{1,0:T(8,128)(2,1)}, u32[]{:S(2)}) copy-start(bf16[1024,768]{1,0:T(8,128)(2,1)} %param.8) | copy-start | bytes 4718596
  0.6 18.0 %copy-start.3 = (s32[256]{0:T(256)S(1)}, s32[256]{0:T(256)}, u32[]{:S(2)}) copy-start(s32[256]{0:T(256)} %param.10) | copy-start | bytes 3076
  0.7 22.1 %collective-permute-start = (bf16[128,768]{1,0:T(8,128)(2,1)}, bf16[128,768]{1,0:T(8,128)(2,1)S(1)}, u32[]{:S(2)}, u32[]{:S(2)}) collective-permute-start(bf16[128,768]{1,0:T(8,128)(2,1)} %param.6), channel_id=1, source_target_pairs={{0,8},{4,12},{8,0},{12,4},{16,24},{20,28},{24,16},{28,20},{1,9},{5... | collective-permute-start | bytes 589832 | tf_op jit(solution)/shard_map/ppermute | solution.py:61
  3.7 19.0 %collective-permute-start.1 = (bf16[128,768]{1,0:T(8,128)(2,1)}, bf16[128,768]{1,0:T(8,128)(2,1)S(1)}, u32[]{:S(2)}, u32[]{:S(2)}) collective-permute-start(bf16[128,768]{1,0:T(8,128)(2,1)} %param.6), channel_id=1, source_target_pairs={{0,16},{4,20},{8,24},{12,28},{16,0},{20,4},{24,8},{28,12},{1,17},{... | collective-permute-start | bytes 589832 | tf_op jit(solution)/shard_map/ppermute | solution.py:61
  6.3 16.4 %collective-permute-start.2 = (bf16[128,768]{1,0:T(8,128)(2,1)}, bf16[128,768]{1,0:T(8,128)(2,1)S(1)}, u32[]{:S(2)}, u32[]{:S(2)}) collective-permute-start(bf16[128,768]{1,0:T(8,128)(2,1)} %param.6), channel_id=1, source_target_pairs={{0,24},{4,28},{8,16},{12,20},{16,8},{20,12},{24,0},{28,4},{1,25},{... | collective-permute-start | bytes 589832 | tf_op jit(solution)/shard_map/ppermute | solution.py:61
  6.3 30.6 %collective-permute-start.4 = (bf16[128,768]{1,0:T(8,128)(2,1)}, bf16[128,768]{1,0:T(8,128)(2,1)}, u32[]{:S(2)}, u32[]{:S(2)}) collective-permute-start(bf16[128,768]{1,0:T(8,128)(2,1)} %param.6), channel_id=1, source_target_pairs={{0,4},{4,0},{8,12},{12,8},{16,20},{20,16},{24,28},{28,24},{1,5},{5... | collective-permute-start | bytes 589832 | tf_op jit(solution)/shard_map/ppermute | solution.py:61
  22.7 14.1 %all-to-all-start = ((f32[8,128,80]{1,2,0:T(8,128)}), f32[8,128,80]{1,2,0:T(8,128)S(1)}, u32[]{:S(2)}, u32[]{:S(2)}) async-start(f32[8,128,80]{1,2,0:T(8,128)} %pad_maximum_fusion.3), calls=%async_computation | async-start | bytes 655360 | tf_op jit(solution)/shard_map/all_to_all | solution.py:100
  28.9 16.9 %collective-permute-start.3 = (bf16[3,128,768]{2,1,0:T(8,128)(2,1)}, bf16[3,128,768]{2,1,0:T(8,128)(2,1)S(1)}, u32[]{:S(2)}, u32[]{:S(2)}) collective-permute-start(bf16[3,128,768]{2,1,0:T(8,128)(2,1)} %pad_maximum_fusion), channel_id=1, source_target_pairs={{0,4},{4,0},{8,12},{12,8},{16,20},{20,16},{24,28},{28,24},{1,5},{5... | collective-permute-start | bytes 1769480 | tf_op jit(solution)/shard_map/ppermute | solution.py:61
  48.9 7.1 %copy-start.1 = (bf16[1024,768]{1,0:T(8,128)(2,1)}, bf16[1024,768]{1,0:T(8,128)(2,1)S(1)}, u32[]{:S(2)}) copy-start(bf16[1024,768]{1,0:T(8,128)(2,1)S(1)} %select_dynamic-update-slice_fusion) | copy-start | bytes 4718596
  59.2 12.0 %all-to-all-start.1 = ((f32[8,3,1024]{2,1,0:T(4,128)}), f32[8,3,1024]{2,1,0:T(4,128)S(1)}, u32[]{:S(2)}, u32[]{:S(2)}) async-start(f32[8,3,1024]{2,1,0:T(4,128)} %broadcast_in_dim.208), calls=%async_computation.1 | async-start | bytes 262144 | tf_op jit(solution)/shard_map/all_to_all | solution.py:136
  71.4 5.5 %copy-start.2 = (bf16[1024,768]{1,0:T(8,128)(2,1)S(1)}, bf16[1024,768]{1,0:T(8,128)(2,1)}, u32[]{:S(2)}) copy-start(bf16[1024,768]{1,0:T(8,128)(2,1)} %copy-done.1) | copy-start | bytes 4718596
  80.8 23.5 %collective-permute-start.10 = (bf16[256,768]{1,0:T(8,128)(2,1)S(1)}, bf16[256,768]{1,0:T(8,128)(2,1)S(1)}, u32[]{:S(2)}, u32[]{:S(2)}) collective-permute-start(bf16[256,768]{1,0:T(8,128)(2,1)S(1)} %get-tuple-element.45), channel_id=1, source_target_pairs={{0,1},{1,2},{2,3},{3,0},{4,5},{5,6},{6,7},{7,4},{8,9},{9,10},{10,1... | collective-permute-start | bytes 1179656 | tf_op jit(solution)/shard_map/ppermute | solution.py:197
  80.8 26.5 %collective-permute-start.11 = (bf16[256,768]{1,0:T(8,128)(2,1)S(1)}, bf16[256,768]{1,0:T(8,128)(2,1)S(1)}, u32[]{:S(2)}, u32[]{:S(2)}) collective-permute-start(bf16[256,768]{1,0:T(8,128)(2,1)S(1)} %get-tuple-element.47), channel_id=1, source_target_pairs={{0,2},{1,3},{2,0},{3,1},{4,6},{5,7},{6,4},{7,5},{8,10},{9,11},{10,... | collective-permute-start | bytes 1179656 | tf_op jit(solution)/shard_map/ppermute | solution.py:197
  82.4 24.9 %collective-permute-start.12 = (bf16[256,768]{1,0:T(8,128)(2,1)S(1)}, bf16[256,768]{1,0:T(8,128)(2,1)S(1)}, u32[]{:S(2)}, u32[]{:S(2)}) collective-permute-start(bf16[256,768]{1,0:T(8,128)(2,1)S(1)} %get-tuple-element.46), channel_id=1, source_target_pairs={{0,3},{1,0},{2,1},{3,2},{4,7},{5,4},{6,5},{7,6},{8,11},{9,8},{10,9... | collective-permute-start | bytes 1179656 | tf_op jit(solution)/shard_map/ppermute | solution.py:197
  84.1 12.1 %collective-permute-start.5 = (bf16[2,128,768]{2,1,0:T(8,128)(2,1)S(1)}, bf16[2,128,768]{2,1,0:T(8,128)(2,1)S(1)}, u32[]{:S(2)}, u32[]{:S(2)}) collective-permute-start(bf16[2,128,768]{2,1,0:T(8,128)(2,1)S(1)} %pad_maximum_fusion.1), channel_id=1, source_target_pairs={{0,4},{4,0},{8,12},{12,8},{16,20},{20,16},{24,28},{28,24},{1,5},{5... | collective-permute-start | bytes 1179656 | tf_op jit(solution)/shard_map/ppermute | solution.py:61
  84.4 18.3 %collective-permute-start.6 = (bf16[2,128,768]{2,1,0:T(8,128)(2,1)S(1)}, bf16[2,128,768]{2,1,0:T(8,128)(2,1)S(1)}, u32[]{:S(2)}, u32[]{:S(2)}) collective-permute-start(bf16[2,128,768]{2,1,0:T(8,128)(2,1)S(1)} %pad_maximum_fusion.2), channel_id=1, source_target_pairs={{0,4},{4,0},{8,12},{12,8},{16,20},{20,16},{24,28},{28,24},{1,5},{5... | collective-permute-start | bytes 1179656 | tf_op jit(solution)/shard_map/ppermute | solution.py:61
  102.8 9.7 %collective-permute-start.7 = (bf16[128,768]{1,0:T(8,128)(2,1)S(1)}, bf16[128,768]{1,0:T(8,128)(2,1)S(1)}, u32[]{:S(2)}, u32[]{:S(2)}) collective-permute-start(bf16[128,768]{1,0:T(8,128)(2,1)S(1)} %get-tuple-element.43), channel_id=1, source_target_pairs={{0,24},{4,28},{8,16},{12,20},{16,8},{20,12},{24,0},{28,4},{1,25},{... | collective-permute-start | bytes 589832 | tf_op jit(solution)/shard_map/ppermute | solution.py:61
  103.4 16.4 %collective-permute-start.8 = (bf16[128,768]{1,0:T(8,128)(2,1)S(1)}, bf16[128,768]{1,0:T(8,128)(2,1)S(1)}, u32[]{:S(2)}, u32[]{:S(2)}) collective-permute-start(bf16[128,768]{1,0:T(8,128)(2,1)S(1)} %get-tuple-element.44), channel_id=1, source_target_pairs={{0,16},{4,20},{8,24},{12,28},{16,0},{20,4},{24,8},{28,12},{1,17},{... | collective-permute-start | bytes 589832 | tf_op jit(solution)/shard_map/ppermute | solution.py:61
  104.2 15.6 %collective-permute-start.9 = (bf16[128,768]{1,0:T(8,128)(2,1)S(1)}, bf16[128,768]{1,0:T(8,128)(2,1)S(1)}, u32[]{:S(2)}, u32[]{:S(2)}) collective-permute-start(bf16[128,768]{1,0:T(8,128)(2,1)S(1)} %get-tuple-element.48), channel_id=1, source_target_pairs={{0,8},{4,12},{8,0},{12,4},{16,24},{20,28},{24,16},{28,20},{1,9},{5... | collective-permute-start | bytes 589832 | tf_op jit(solution)/shard_map/ppermute | solution.py:61
